TPU v7x, 256 devices: a whole 4x4x8 slice. The times are simulated.
256 devices in a mesh: pix: 32 (over x, z), head: 8 (over y, core).
Axes of the slice: x: 4, y: 4, z: 8, core: 2. Of those that a mesh axis runs over, the one named last changes fastest.
Arguments:
- query_rows: bfloat16 [65536, 1024], P(('pix', 'head')), may hold values from -28 to 28
- key_rows: bfloat16 [65536, 1024], P(('pix', 'head')), may hold values from -28 to 28
- value_rows: bfloat16 [65536, 1024], P(('pix', 'head')), may hold values from -6 to 6
- out_grad: bfloat16 [65536, 1024], P('pix', 'head'), may hold values from -6 to 6
- boundary_send_blocks: int32 [32, 5, 4], replicated, may hold values from 0 to 31, as said below
- neighbours: int32 [1024, 9], replicated, may hold values from 0 to 51, as said below
- live_count: int32 [1024], replicated, may hold values from 8 to 9
Outputs:
- attended: bfloat16 [65536, 1024], P(('pix', 'head'))
- query_grad: bfloat16 [65536, 1024], P('pix', 'head')
- key_grad: bfloat16 [65536, 1024], P('pix', 'head')
- value_grad: bfloat16 [65536, 1024], P('pix', 'head')
Inputs may be any that keep to these rules, and one draw needn't show every extreme that they name: For each range the 20 blocks in boundary_send_blocks[r] are distinct. `neighbours`: slot 0 of a block names the block itself (its place in its range); the entries of a row are distinct. A block that is boundary_send_blocks[r, b, s] names 32 + b * 4 + s in slot 1 and no other entry of 32 or more; every other block names only entries below 32.
All inputs are finite; a program needn't handle non-finite values.
Results may differ from a plain program's by a relative error of at most 0.03.
Values may be sent and summed in bfloat16 or wider, within the bound.
No kernel may reach another device: no remote copies, remote signals or barrier semaphores. Data moves between devices by JAX's collectives and lax.ppermute only.
A program may use at most 128 MiB of HBM per device.

v0:
```python
import functools
import jax
import jax.numpy as jnp
from jax import lax
from jax.experimental import pallas as pl
from jax.experimental.pallas import tpu as pltpu
from jax.sharding import PartitionSpec as P

HD = 64
BLK = 64
NNB = 9
NBLK = 32
LEVELS = 5
SEND = 4
WIDE = 2 * HD
OWN = NBLK * BLK
PART = SEND * BLK
FILL = -1e30
F32 = jnp.float32
BF16 = jnp.bfloat16

VM = pl.BlockSpec(memory_space=pltpu.VMEM)
SM = pl.BlockSpec(memory_space=pltpu.SMEM)


def swapped(block, bit):
    count = lax.axis_size("pix")
    route = [(low, low ^ (1 << bit)) for low in range(count)]
    return lax.ppermute(block, "pix", route)


def rows_of(start):
    return pl.ds(pl.multiple_of(start * BLK, BLK), BLK)


def pick_kernel(sends_ref, own_ref, *out_refs):
    for b in range(LEVELS):
        for s in range(SEND):
            out_refs[b][s * BLK : (s + 1) * BLK, :] = own_ref[rows_of(sends_ref[b, s]), :]


def pick(sends, own):
    return pl.pallas_call(
        pick_kernel,
        out_shape=[jax.ShapeDtypeStruct((PART, 2 * WIDE), BF16)] * LEVELS,
        in_specs=[SM, VM],
        out_specs=[VM] * LEVELS,
        compiler_params=pltpu.CompilerParams(vmem_limit_bytes=16 * 2**20),
        cost_estimate=pl.CostEstimate(flops=0, bytes_accessed=2 * 2**20, transcendentals=0),
        name="pick_boundary",
    )(sends, own)


def attend_block(i, rows_ref, counts_ref, q_ref, g_ref, kv_ref, att_ref, qg_ref, acc_ref):
    at = rows_of(i)
    q = q_ref[at, :] * jnp.array(HD**-0.5, BF16)
    g = g_ref[at, :]
    low = lax.broadcasted_iota(jnp.int32, (BLK, WIDE), 1) < HD
    z = jnp.zeros((BLK, WIDE), BF16)
    both = jnp.concatenate(
        [
            jnp.concatenate([jnp.where(low, q, z), z], 1),
            jnp.concatenate([jnp.where(low, z, q), z], 1),
            jnp.concatenate([z, jnp.where(low, g, z)], 1),
            jnp.concatenate([z, jnp.where(low, z, g)], 1),
        ],
        0,
    )
    starts = [rows_of(rows_ref[i, j]) for j in range(NNB)]
    kv = jnp.concatenate([kv_ref[start, :] for start in starts], 0)
    sd = lax.dot_general(kv, both, (((1,), (1,)), ((), ())), preferred_element_type=F32)
    s = [sd[j * BLK : (j + 1) * BLK, :WIDE] for j in range(NNB)]
    d = [sd[j * BLK : (j + 1) * BLK, WIDE:] for j in range(NNB)]
    s[-1] = jnp.where(counts_ref[i] > NNB - 1, s[-1], FILL)
    peak = functools.reduce(jnp.maximum, s)
    peak = jnp.max(peak, 0, keepdims=True)
    p = [jnp.exp(x - peak) for x in s]
    total = jnp.sum(sum(p[1:], p[0]), 0, keepdims=True)
    dot = [x * y for x, y in zip(p, d)]
    inv = 1.0 / total
    dot = jnp.sum(sum(dot[1:], dot[0]), 0, keepdims=True) * inv
    weights = [x * inv for x in p]
    rounded = jnp.concatenate([x.astype(BF16) for x in weights], 0)
    grads = jnp.concatenate([(x * (y - dot)).astype(BF16) for x, y in zip(weights, d)], 0)
    terms = lax.dot_general(
        jnp.concatenate([grads, rounded], 1), both, (((1,), (0,)), ((), ())), preferred_element_type=F32
    )
    down = (((0,), (0,)), ((), ()))
    qg = lax.dot_general(grads, kv[:, :WIDE], down, preferred_element_type=F32)
    att = lax.dot_general(rounded, kv[:, WIDE:], down, preferred_element_type=F32)
    att_ref[at, :] = jnp.where(low, att[:BLK], att[BLK:]).astype(BF16)
    qg_ref[at, :] = (jnp.where(low, qg[:BLK], qg[BLK:]) * HD**-0.5).astype(BF16)
    for j in range(NNB):
        acc_ref[starts[j], :] += terms[j * BLK : (j + 1) * BLK]


def attend_kernel(unroll, rows_ref, counts_ref, q_ref, g_ref, own_ref, *refs):
    recv_refs = refs[:LEVELS]
    att_ref, qg_ref, acc_out = refs[LEVELS : LEVELS + 3]
    back_refs = refs[LEVELS + 3 : 2 * LEVELS + 3]
    kv_ref, acc_ref = refs[2 * LEVELS + 3 :]
    kv_ref[:OWN, :] = own_ref[...]
    for b in range(LEVELS):
        kv_ref[OWN + b * PART : OWN + (b + 1) * PART, :] = recv_refs[b][...]
    acc_ref[...] = jnp.zeros_like(acc_ref)

    def step(t, carry):
        for u in range(unroll):
            attend_block(t * unroll + u, rows_ref, counts_ref, q_ref, g_ref, kv_ref, att_ref, qg_ref, acc_ref)
        return carry

    lax.fori_loop(0, NBLK // unroll, step, 0)
    acc_out[...] = acc_ref[:OWN, :]
    for b in range(LEVELS):
        back_refs[b][...] = acc_ref[OWN + b * PART : OWN + (b + 1) * PART, :].astype(BF16)


def attend(rows, counts, q, g, own, recv):
    ext = OWN + LEVELS * PART
    return pl.pallas_call(
        functools.partial(attend_kernel, 2),
        out_shape=[
            jax.ShapeDtypeStruct((OWN, WIDE), BF16),
            jax.ShapeDtypeStruct((OWN, WIDE), BF16),
            jax.ShapeDtypeStruct((OWN, 2 * WIDE), F32),
        ]
        + [jax.ShapeDtypeStruct((PART, 2 * WIDE), BF16)] * LEVELS,
        in_specs=[SM, SM] + [VM] * (3 + LEVELS),
        out_specs=[VM] * (3 + LEVELS),
        scratch_shapes=[pltpu.VMEM((ext, 2 * WIDE), BF16), pltpu.VMEM((ext, 2 * WIDE), F32)],
        compiler_params=pltpu.CompilerParams(vmem_limit_bytes=40 * 2**20),
        cost_estimate=pl.CostEstimate(flops=4 * 10**9, bytes_accessed=8 * 2**20, transcendentals=3 * 10**6),
        name="attend_blocks",
    )(rows, counts, q, g, own, *recv)


def join_kernel(sends_ref, acc_ref, *refs):
    arrived_refs = refs[:LEVELS]
    key_ref, value_ref = refs[LEVELS : LEVELS + 2]
    key_ref[...] = acc_ref[:, :WIDE].astype(BF16)
    value_ref[...] = acc_ref[:, WIDE:].astype(BF16)
    for b in range(LEVELS):
        for s in range(SEND):
            at = rows_of(sends_ref[b, s])
            both = acc_ref[at, :] + arrived_refs[b][s * BLK : (s + 1) * BLK, :].astype(F32)
            key_ref[at, :] = both[:, :WIDE].astype(BF16)
            value_ref[at, :] = both[:, WIDE:].astype(BF16)


def join(sends, acc, arrived):
    return pl.pallas_call(
        join_kernel,
        out_shape=[jax.ShapeDtypeStruct((OWN, WIDE), BF16)] * 2,
        in_specs=[SM] + [VM] * (1 + LEVELS),
        out_specs=[VM] * 2,
        compiler_params=pltpu.CompilerParams(vmem_limit_bytes=24 * 2**20),
        cost_estimate=pl.CostEstimate(flops=10**6, bytes_accessed=4 * 2**20, transcendentals=0),
        name="join_gradients",
    )(sends, acc, *arrived)


def body(query_rows, key_rows, value_rows, out_grad, boundary_send_blocks, neighbours, live_count):
    heads = lax.axis_size("head")
    mine = query_rows.shape[0]
    my_range = lax.axis_index("pix")
    sends = lax.dynamic_index_in_dim(boundary_send_blocks, my_range, 0, keepdims=False)
    rows = lax.dynamic_slice_in_dim(neighbours, my_range * NBLK, NBLK, 0)
    counts = lax.dynamic_slice_in_dim(live_count, my_range * NBLK, NBLK, 0)

    def by_head(x):
        return x.reshape(mine, heads, WIDE)

    kv = jnp.concatenate([by_head(key_rows), by_head(value_rows)], axis=2).transpose(1, 0, 2)
    own = lax.all_to_all(kv, "head", 0, 0, tiled=True).reshape(OWN, 2 * WIDE)
    q = lax.all_to_all(by_head(query_rows).transpose(1, 0, 2), "head", 0, 0, tiled=True).reshape(OWN, WIDE)
    outgoing = pick(sends, own)
    recv = [swapped(outgoing[b], b) for b in range(LEVELS)]
    results = attend(rows, counts, q, out_grad, own, recv)
    attended, query_grad, acc = results[:3]
    arrived = [swapped(results[3 + b], b) for b in range(LEVELS)]
    attended = lax.all_to_all(attended.reshape(heads, mine, WIDE), "head", 0, 0, tiled=True)
    attended = attended.transpose(1, 0, 2).reshape(mine, heads * WIDE)
    key_grad, value_grad = join(sends, acc, arrived)
    return attended, query_grad, key_grad, value_grad


def solution(mesh):
    rows = P(("pix", "head"), None)
    split = P("pix", "head")
    return jax.shard_map(
        body,
        mesh=mesh,
        in_specs=(rows, rows, rows, split, P(), P(), P()),
        out_specs=(rows, split, split, split),
        check_vma=False,
    )
```

profile of v0, /device:TPU:8, one launch (start us, length us, event | category | flops | bytes accessed | tf_op | source)
XLA Modules:
  0.0 102.4 jit_solution(5817618400973061377)
XLA Ops:
  0.6 0.0 copy-start
  0.6 1.0 %copy-done = bf16[256,1024]{1,0:T(8,128)(2,1)S(1)} copy-done((bf16[256,1024]{1,0:T(8,128)(2,1)S(1)}, bf16[256,1024]{1,0:T(8,128)(2,1)}, u32[]{:S(2)}) %copy-start) | copy-done | bytes 524312
  1.7 1.3 %copy_bitcast_fusion.1 = (bf16[256,8,128]{2,0,1:T(8,128)(2,1)S(1)}, bf16[256,8,128]{2,0,1:T(8,128)(2,1)S(1)}) fusion(bf16[256,1024]{1,0:T(8,128)(2,1)S(1)} %copy-done, bf16[256,1024]{1,0:T(8,128)(2,1)} %param.9), kind=kLoop, calls=%fused_computation.2 | loop fusion | bytes 2097152 | tf_op jit(solution)/shard_map/reshape | solution.py:171
  3.0 0.0 copy-start.8
  3.0 1.1 %maximum_bitcast_fusion = bf16[8,256,256]{2,1,0:T(8,128)(2,1)} fusion(bf16[256,8,128]{2,0,1:T(8,128)(2,1)S(1)} %get-tuple-element.34, bf16[256,8,128]{2,0,1:T(8,128)(2,1)S(1)} %get-tuple-element.35), kind=kLoop, calls=%fused_computation | loop fusion | flops 2097152 | bytes 2097152 | tf_op jit(solution)/shard_map/transpose | solution.py:173
  4.1 0.0 copy-start.9
  4.1 5.8 %all-to-all-start.1 = ((bf16[8,256,256]{2,1,0:T(8,128)(2,1)}), bf16[8,256,256]{2,1,0:T(8,128)(2,1)S(1)}, u32[]{:S(2)}, u32[]{:S(2)}) async-start(bf16[8,256,256]{2,1,0:T(8,128)(2,1)} %maximum_bitcast_fusion), calls=%async_computation.1 | async-start | bytes 2097152 | tf_op jit(solution)/shard_map/all_to_all | solution.py:174
  9.9 0.0 copy-done.8
  9.9 0.0 copy-start.3
  9.9 0.9 bitcast_bitcast_fusion
  10.8 13.6 %all-to-all-done.1 = bf16[8,256,256]{2,1,0:T(8,128)(2,1)S(1)} async-done(((bf16[8,256,256]{2,1,0:T(8,128)(2,1)}), bf16[8,256,256]{2,1,0:T(8,128)(2,1)S(1)}, u32[]{:S(2)}, u32[]{:S(2)}) %all-to-all-start.1) | async-done | bytes 1048608 | tf_op jit(solution)/shard_map/all_to_all | solution.py:174
  24.4 4.9 %all-to-all-start = ((bf16[8,256,128]{2,1,0:T(8,128)(2,1)}), bf16[8,256,128]{2,1,0:T(8,128)(2,1)S(1)}, u32[]{:S(2)}, u32[]{:S(2)}) async-start(bf16[8,256,128]{2,1,0:T(8,128)(2,1)} %bitcast_bitcast_fusion), calls=%async_computation | async-start | bytes 1048576 | tf_op jit(solution)/shard_map/all_to_all | solution.py:175
  29.3 0.0 copy-done.9
  29.3 0.1 constant_dynamic-slice_fusion
  29.4 0.1 copy.15
  29.5 0.1 copy.16.sends_ref
  29.6 1.4 %pick_boundary.1 = (bf16[256,256]{1,0:T(8,128)(2,1)}, bf16[256,256]{1,0:T(8,128)(2,1)}, bf16[256,256]{1,0:T(8,128)(2,1)}, bf16[256,256]{1,0:T(8,128)(2,1)}, bf16[256,256]{1,0:T(8,128)(2,1)S(1)}) custom-call(s32[5,4]{1,0:T(8,128)S(1)} %copy.16.sends_ref, bf16[2048,256]{1,0:T(8,128)(2,1)S(1)} %bitcast.29), custom_call_target="tpu_custom_call" | custom-call | bytes 2097152 | tf_op jit(solution)/shard_map/pick_boundary/pallas_call | solution.py:43
  31.0 1.2 %collective-permute-start = (bf16[256,256]{1,0:T(8,128)(2,1)}, bf16[256,256]{1,0:T(8,128)(2,1)S(1)}, u32[]{:S(2)}, u32[]{:S(2)}) collective-permute-start(bf16[256,256]{1,0:T(8,128)(2,1)} %get-tuple-element.19), channel_id=1, source_target_pairs={{0,8},{8,0},{16,24},{24,16},{32,40},{40,32},{48,56},{56,48},{64,72... | collective-permute-start | bytes 393224 | tf_op jit(solution)/shard_map/ppermute | solution.py:29
  32.2 3.3 %collective-permute-start.1 = (bf16[256,256]{1,0:T(8,128)(2,1)}, bf16[256,256]{1,0:T(8,128)(2,1)S(1)}, u32[]{:S(2)}, u32[]{:S(2)}) collective-permute-start(bf16[256,256]{1,0:T(8,128)(2,1)} %get-tuple-element.20), channel_id=1, source_target_pairs={{0,16},{8,24},{16,0},{24,8},{32,48},{40,56},{48,32},{56,40},{64,80... | collective-permute-start | bytes 393224 | tf_op jit(solution)/shard_map/ppermute | solution.py:29
  35.4 4.5 %collective-permute-start.2 = (bf16[256,256]{1,0:T(8,128)(2,1)}, bf16[256,256]{1,0:T(8,128)(2,1)S(1)}, u32[]{:S(2)}, u32[]{:S(2)}) collective-permute-start(bf16[256,256]{1,0:T(8,128)(2,1)} %get-tuple-element.21), channel_id=1, source_target_pairs={{0,32},{8,40},{16,48},{24,56},{32,0},{40,8},{48,16},{56,24},{64,96... | collective-permute-start | bytes 393224 | tf_op jit(solution)/shard_map/ppermute | solution.py:29
  39.9 1.5 %collective-permute-start.3 = (bf16[256,256]{1,0:T(8,128)(2,1)}, bf16[256,256]{1,0:T(8,128)(2,1)S(1)}, u32[]{:S(2)}, u32[]{:S(2)}) collective-permute-start(bf16[256,256]{1,0:T(8,128)(2,1)} %get-tuple-element.22), channel_id=1, source_target_pairs={{0,64},{8,72},{16,80},{24,88},{32,96},{40,104},{48,112},{56,120},{... | collective-permute-start | bytes 393224 | tf_op jit(solution)/shard_map/ppermute | solution.py:29
  41.4 2.7 %collective-permute-start.4 = (bf16[256,256]{1,0:T(8,128)(2,1)S(1)}, bf16[256,256]{1,0:T(8,128)(2,1)S(1)}, u32[]{:S(2)}, u32[]{:S(2)}) collective-permute-start(bf16[256,256]{1,0:T(8,128)(2,1)S(1)} %get-tuple-element.23), channel_id=1, source_target_pairs={{0,128},{8,136},{16,144},{24,152},{32,160},{40,168},{48,176},{56,1... | collective-permute-start | bytes 393224 | tf_op jit(solution)/shard_map/ppermute | solution.py:29
  44.1 0.8 dynamic_slice.11.counts_ref
  44.9 0.8 constant_dynamic-slice_fusion.1
  45.7 0.1 copy.19.rows_ref
  45.8 0.0 all-to-all-done
  45.8 0.0 collective-permute-done.refs_0_
  45.8 0.0 collective-permute-done.1.refs_1_
  45.8 2.6 %collective-permute-done.2.refs_2_ = bf16[256,256]{1,0:T(8,128)(2,1)S(1)} collective-permute-done((bf16[256,256]{1,0:T(8,128)(2,1)}, bf16[256,256]{1,0:T(8,128)(2,1)S(1)}, u32[]{:S(2)}, u32[]{:S(2)}) %collective-permute-start.2) | collective-permute-done | bytes 131104 | tf_op jit(solution)/shard_map/ppermute | solution.py:29
  48.4 0.0 collective-permute-done.3.refs_3_
  48.4 1.5 %collective-permute-done.4.refs_4_ = bf16[256,256]{1,0:T(8,128)(2,1)S(1)} collective-permute-done((bf16[256,256]{1,0:T(8,128)(2,1)S(1)}, bf16[256,256]{1,0:T(8,128)(2,1)S(1)}, u32[]{:S(2)}, u32[]{:S(2)}) %collective-permute-start.4) | collective-permute-done | bytes 131104 | tf_op jit(solution)/shard_map/ppermute | solution.py:29
  49.8 0.0 copy-done.3
  49.8 23.5 %attend_blocks.1 = (bf16[2048,128]{1,0:T(8,128)(2,1)}, bf16[2048,128]{1,0:T(8,128)(2,1)}, f32[2048,256]{1,0:T(8,128)S(1)}, bf16[256,256]{1,0:T(8,128)(2,1)S(1)},...) custom-call(s32[32,9]{1,0:T(8,128)S(1)} %copy.19.rows_ref, ...), custom_call_target="tpu_custom_call" | custom-call | flops 4000000000 | bytes 8388608 | tf_op jit(solution)/shard_map/attend_blocks/pallas_call | solution.py:120
  73.3 0.0 copy-start.1
  73.3 1.3 %copy-done.1 = f32[2048,256]{1,0:T(8,128)} copy-done((f32[2048,256]{1,0:T(8,128)}, f32[2048,256]{1,0:T(8,128)S(1)}, u32[]{:S(2)}) %copy-start.1) | copy-done | bytes 2097176
  74.7 0.0 copy-start.4
  74.7 0.6 copy-done.4
  75.3 0.0 copy-start.5
  75.3 0.6 copy-done.5
  76.0 0.0 copy-start.6
  76.0 0.7 copy-done.6
  76.6 0.0 copy-start.7
  76.6 0.7 copy-done.7
  77.3 4.8 %all-to-all-start.2 = ((bf16[8,256,128]{2,1,0:T(8,128)(2,1)}), bf16[8,256,128]{2,1,0:T(8,128)(2,1)S(1)}, u32[]{:S(2)}, u32[]{:S(2)}) async-start(bf16[8,256,128]{2,1,0:T(8,128)(2,1)} %bitcast.5), calls=%async_computation.2 | async-start | bytes 1048576 | tf_op jit(solution)/shard_map/all_to_all | solution.py:181
  82.1 1.0 collective-permute-start.5
  83.1 2.4 %collective-permute-start.6 = (bf16[256,256]{1,0:T(8,128)(2,1)}, bf16[256,256]{1,0:T(8,128)(2,1)S(1)}, u32[]{:S(2)}, u32[]{:S(2)}) collective-permute-start(bf16[256,256]{1,0:T(8,128)(2,1)} %copy-done.6), channel_id=1, source_target_pairs={{0,16},{8,24},{16,0},{24,8},{32,48},{40,56},{48,32},{56,40},{64,80... | collective-permute-start | bytes 393224 | tf_op jit(solution)/shard_map/ppermute | solution.py:29
  85.5 1.3 %collective-permute-start.7 = (bf16[256,256]{1,0:T(8,128)(2,1)}, bf16[256,256]{1,0:T(8,128)(2,1)S(1)}, u32[]{:S(2)}, u32[]{:S(2)}) collective-permute-start(bf16[256,256]{1,0:T(8,128)(2,1)} %copy-done.5), channel_id=1, source_target_pairs={{0,32},{8,40},{16,48},{24,56},{32,0},{40,8},{48,16},{56,24},{64,96... | collective-permute-start | bytes 393224 | tf_op jit(solution)/shard_map/ppermute | solution.py:29
  86.7 1.5 %collective-permute-start.8 = (bf16[256,256]{1,0:T(8,128)(2,1)}, bf16[256,256]{1,0:T(8,128)(2,1)S(1)}, u32[]{:S(2)}, u32[]{:S(2)}) collective-permute-start(bf16[256,256]{1,0:T(8,128)(2,1)} %copy-done.4), channel_id=1, source_target_pairs={{0,64},{8,72},{16,80},{24,88},{32,96},{40,104},{48,112},{56,120},{... | collective-permute-start | bytes 393224 | tf_op jit(solution)/shard_map/ppermute | solution.py:29
  88.2 2.7 %collective-permute-start.9 = (bf16[256,256]{1,0:T(8,128)(2,1)S(1)}, bf16[256,256]{1,0:T(8,128)(2,1)S(1)}, u32[]{:S(2)}, u32[]{:S(2)}) collective-permute-start(bf16[256,256]{1,0:T(8,128)(2,1)S(1)} %get-tuple-element.31), channel_id=1, source_target_pairs={{0,128},{8,136},{16,144},{24,152},{32,160},{40,168},{48,176},{56,1... | collective-permute-start | bytes 393224 | tf_op jit(solution)/shard_map/ppermute | solution.py:29
  91.0 0.4 collective-permute-done.5.refs_0_
  91.4 6.4 %collective-permute-done.6.refs_1_ = bf16[256,256]{1,0:T(8,128)(2,1)S(1)} collective-permute-done((bf16[256,256]{1,0:T(8,128)(2,1)}, bf16[256,256]{1,0:T(8,128)(2,1)S(1)}, u32[]{:S(2)}, u32[]{:S(2)}) %collective-permute-start.6) | collective-permute-done | bytes 131104 | tf_op jit(solution)/shard_map/ppermute | solution.py:29
  97.8 0.4 collective-permute-done.7.refs_2_
  98.1 0.0 collective-permute-done.8.refs_3_
  98.1 0.0 collective-permute-done.9.refs_4_
  98.1 0.0 copy-start.2
  98.1 1.6 %copy-done.2 = f32[2048,256]{1,0:T(8,128)S(1)} copy-done((f32[2048,256]{1,0:T(8,128)S(1)}, f32[2048,256]{1,0:T(8,128)}, u32[]{:S(2)}) %copy-start.2) | copy-done | bytes 2097176
  99.7 1.8 %join_gradients.1 = (bf16[2048,128]{1,0:T(8,128)(2,1)}, bf16[2048,128]{1,0:T(8,128)(2,1)}) custom-call(s32[5,4]{1,0:T(8,128)S(1)} %copy.16.sends_ref, f32[2048,256]{1,0:T(8,128)S(1)} %copy-done.2, bf16[256,256]{1,0:T(8,128)(2,1)S(1)} %collective-permute-done.5.refs_0_, bf16[256,256]{1,0:T(8,128)(2,1)S(1)} %collective-permute-done.6.refs_1_, ...), custom_call_target="tpu_custom_call" | custom-call | flops 1000000 | bytes 4194304 | tf_op jit(solution)/shard_map/join_gradients/pallas_call | solution.py:151
  101.5 0.0 all-to-all-done.2
  101.5 0.9 copy_bitcast_fusion
Async XLA Ops:
  0.6 1.0 %copy-start = (bf16[256,1024]{1,0:T(8,128)(2,1)S(1)}, bf16[256,1024]{1,0:T(8,128)(2,1)}, u32[]{:S(2)}) copy-start(bf16[256,1024]{1,0:T(8,128)(2,1)} %param.8) | copy-start | bytes 1572868
  3.0 6.9 %copy-start.8 = (bf16[256,1024]{1,0:T(8,128)(2,1)S(1)}, bf16[256,1024]{1,0:T(8,128)(2,1)}, u32[]{:S(2)}) copy-start(bf16[256,1024]{1,0:T(8,128)(2,1)} %param.7) | copy-start | bytes 1572868
  4.1 25.2 %copy-start.9 = (s32[32,5,4]{0,2,1:T(4,128)S(1)}, s32[32,5,4]{0,2,1:T(4,128)}, u32[]{:S(2)}) copy-start(s32[32,5,4]{0,2,1:T(4,128)} %param.11) | copy-start | bytes 7684
  4.1 20.3 %all-to-all-start.1 = ((bf16[8,256,256]{2,1,0:T(8,128)(2,1)}), bf16[8,256,256]{2,1,0:T(8,128)(2,1)S(1)}, u32[]{:S(2)}, u32[]{:S(2)}) async-start(bf16[8,256,256]{2,1,0:T(8,128)(2,1)} %maximum_bitcast_fusion), calls=%async_computation.1 | async-start | bytes 2097152 | tf_op jit(solution)/shard_map/all_to_all | solution.py:174
  9.9 40.0 %copy-start.3 = (bf16[2048,128]{1,0:T(8,128)(2,1)S(1)}, bf16[2048,128]{1,0:T(8,128)(2,1)}, u32[]{:S(2)}) copy-start(bf16[2048,128]{1,0:T(8,128)(2,1)} %g_ref.1) | copy-start | bytes 1572868
  24.4 21.3 %all-to-all-start = ((bf16[8,256,128]{2,1,0:T(8,128)(2,1)}), bf16[8,256,128]{2,1,0:T(8,128)(2,1)S(1)}, u32[]{:S(2)}, u32[]{:S(2)}) async-start(bf16[8,256,128]{2,1,0:T(8,128)(2,1)} %bitcast_bitcast_fusion), calls=%async_computation | async-start | bytes 1048576 | tf_op jit(solution)/shard_map/all_to_all | solution.py:175
  31.0 14.8 %collective-permute-start = (bf16[256,256]{1,0:T(8,128)(2,1)}, bf16[256,256]{1,0:T(8,128)(2,1)S(1)}, u32[]{:S(2)}, u32[]{:S(2)}) collective-permute-start(bf16[256,256]{1,0:T(8,128)(2,1)} %get-tuple-element.19), channel_id=1, source_target_pairs={{0,8},{8,0},{16,24},{24,16},{32,40},{40,32},{48,56},{56,48},{64,72... | collective-permute-start | bytes 393224 | tf_op jit(solution)/shard_map/ppermute | solution.py:29
  32.2 13.6 %collective-permute-start.1 = (bf16[256,256]{1,0:T(8,128)(2,1)}, bf16[256,256]{1,0:T(8,128)(2,1)S(1)}, u32[]{:S(2)}, u32[]{:S(2)}) collective-permute-start(bf16[256,256]{1,0:T(8,128)(2,1)} %get-tuple-element.20), channel_id=1, source_target_pairs={{0,16},{8,24},{16,0},{24,8},{32,48},{40,56},{48,32},{56,40},{64,80... | collective-permute-start | bytes 393224 | tf_op jit(solution)/shard_map/ppermute | solution.py:29
  35.4 13.0 %collective-permute-start.2 = (bf16[256,256]{1,0:T(8,128)(2,1)}, bf16[256,256]{1,0:T(8,128)(2,1)S(1)}, u32[]{:S(2)}, u32[]{:S(2)}) collective-permute-start(bf16[256,256]{1,0:T(8,128)(2,1)} %get-tuple-element.21), channel_id=1, source_target_pairs={{0,32},{8,40},{16,48},{24,56},{32,0},{40,8},{48,16},{56,24},{64,96... | collective-permute-start | bytes 393224 | tf_op jit(solution)/shard_map/ppermute | solution.py:29
  39.9 8.5 %collective-permute-start.3 = (bf16[256,256]{1,0:T(8,128)(2,1)}, bf16[256,256]{1,0:T(8,128)(2,1)S(1)}, u32[]{:S(2)}, u32[]{:S(2)}) collective-permute-start(bf16[256,256]{1,0:T(8,128)(2,1)} %get-tuple-element.22), channel_id=1, source_target_pairs={{0,64},{8,72},{16,80},{24,88},{32,96},{40,104},{48,112},{56,120},{... | collective-permute-start | bytes 393224 | tf_op jit(solution)/shard_map/ppermute | solution.py:29
  41.4 8.4 %collective-permute-start.4 = (bf16[256,256]{1,0:T(8,128)(2,1)S(1)}, bf16[256,256]{1,0:T(8,128)(2,1)S(1)}, u32[]{:S(2)}, u32[]{:S(2)}) collective-permute-start(bf16[256,256]{1,0:T(8,128)(2,1)S(1)} %get-tuple-element.23), channel_id=1, source_target_pairs={{0,128},{8,136},{16,144},{24,152},{32,160},{40,168},{48,176},{56,1... | collective-permute-start | bytes 393224 | tf_op jit(solution)/shard_map/ppermute | solution.py:29
  73.3 1.3 %copy-start.1 = (f32[2048,256]{1,0:T(8,128)}, f32[2048,256]{1,0:T(8,128)S(1)}, u32[]{:S(2)}) copy-start(f32[2048,256]{1,0:T(8,128)S(1)} %get-tuple-element.26.acc_ref) | copy-start | bytes 6291460
  74.7 0.6 copy-start.4
  75.3 0.6 copy-start.5
  76.0 0.7 copy-start.6
  76.6 0.7 copy-start.7
  77.3 24.3 %all-to-all-start.2 = ((bf16[8,256,128]{2,1,0:T(8,128)(2,1)}), bf16[8,256,128]{2,1,0:T(8,128)(2,1)S(1)}, u32[]{:S(2)}, u32[]{:S(2)}) async-start(bf16[8,256,128]{2,1,0:T(8,128)(2,1)} %bitcast.5), calls=%async_computation.2 | async-start | bytes 1048576 | tf_op jit(solution)/shard_map/all_to_all | solution.py:181
  82.1 9.3 %collective-permute-start.5 = (bf16[256,256]{1,0:T(8,128)(2,1)}, bf16[256,256]{1,0:T(8,128)(2,1)S(1)}, u32[]{:S(2)}, u32[]{:S(2)}) collective-permute-start(bf16[256,256]{1,0:T(8,128)(2,1)} %copy-done.7), channel_id=1, source_target_pairs={{0,8},{8,0},{16,24},{24,16},{32,40},{40,32},{48,56},{56,48},{64,72... | collective-permute-start | bytes 393224 | tf_op jit(solution)/shard_map/ppermute | solution.py:29
  83.1 14.7 %collective-permute-start.6 = (bf16[256,256]{1,0:T(8,128)(2,1)}, bf16[256,256]{1,0:T(8,128)(2,1)S(1)}, u32[]{:S(2)}, u32[]{:S(2)}) collective-permute-start(bf16[256,256]{1,0:T(8,128)(2,1)} %copy-done.6), channel_id=1, source_target_pairs={{0,16},{8,24},{16,0},{24,8},{32,48},{40,56},{48,32},{56,40},{64,80... | collective-permute-start | bytes 393224 | tf_op jit(solution)/shard_map/ppermute | solution.py:29
  85.5 12.7 %collective-permute-start.7 = (bf16[256,256]{1,0:T(8,128)(2,1)}, bf16[256,256]{1,0:T(8,128)(2,1)S(1)}, u32[]{:S(2)}, u32[]{:S(2)}) collective-permute-start(bf16[256,256]{1,0:T(8,128)(2,1)} %copy-done.5), channel_id=1, source_target_pairs={{0,32},{8,40},{16,48},{24,56},{32,0},{40,8},{48,16},{56,24},{64,96... | collective-permute-start | bytes 393224 | tf_op jit(solution)/shard_map/ppermute | solution.py:29
  86.7 11.4 %collective-permute-start.8 = (bf16[256,256]{1,0:T(8,128)(2,1)}, bf16[256,256]{1,0:T(8,128)(2,1)S(1)}, u32[]{:S(2)}, u32[]{:S(2)}) collective-permute-start(bf16[256,256]{1,0:T(8,128)(2,1)} %copy-done.4), channel_id=1, source_target_pairs={{0,64},{8,72},{16,80},{24,88},{32,96},{40,104},{48,112},{56,120},{... | collective-permute-start | bytes 393224 | tf_op jit(solution)/shard_map/ppermute | solution.py:29
  88.2 9.9 %collective-permute-start.9 = (bf16[256,256]{1,0:T(8,128)(2,1)S(1)}, bf16[256,256]{1,0:T(8,128)(2,1)S(1)}, u32[]{:S(2)}, u32[]{:S(2)}) collective-permute-start(bf16[256,256]{1,0:T(8,128)(2,1)S(1)} %get-tuple-element.31), channel_id=1, source_target_pairs={{0,128},{8,136},{16,144},{24,152},{32,160},{40,168},{48,176},{56,1... | collective-permute-start | bytes 393224 | tf_op jit(solution)/shard_map/ppermute | solution.py:29
  98.1 1.6 %copy-start.2 = (f32[2048,256]{1,0:T(8,128)S(1)}, f32[2048,256]{1,0:T(8,128)}, u32[]{:S(2)}) copy-start(f32[2048,256]{1,0:T(8,128)} %copy-done.1) | copy-start | bytes 6291460
where the time goes:
time: 104 us; the launch traced here: 102 us
  starting transfers between devices  37.5 us (36%)
  Pallas kernels  26.7 us (26%)
  waiting for transfers between devices  24.9 us (24%)
  local copies, waits for them, and re-layouts  11.5 us (11%)
  other arithmetic  1.11 us (1%)
    pallas_call x1, Pallas kernels, attend(): pl.pallas_call(functools.partial(attend_kernel, 2), out_shape=[jax.ShapeD...  23.5 us
    ppermute x10, starting transfers between devices, swapped(): return lax.ppermute(block, 'pix', route)  22 us
    all_to_all x1, waiting for transfers between devices, body(): own = lax.all_to_all(kv, 'head', 0, 0, tiled=True).reshape(OWN, 2 * WIDE)  13.6 us
    ppermute x10, waiting for transfers between devices, swapped(): return lax.ppermute(block, 'pix', route)  11.2 us
    unnamed x21, local copies, waits for them, and re-layouts  6.67 us
    all_to_all x1, starting transfers between devices, body(): own = lax.all_to_all(kv, 'head', 0, 0, tiled=True).reshape(OWN, 2 * WIDE)  5.78 us
    all_to_all x1, starting transfers between devices, body(): lax.all_to_all(by_head(query_rows).transpose(1, 0, 2), 'head', 0, 0, tile...  4.85 us
    all_to_all x1, starting transfers between devices, body(): lax.all_to_all(attended.reshape(heads, mine, WIDE), 'head', 0, 0, tiled=T...  4.82 us
  transfers between devices with their start and end apart: 13, of which 6 were waited for; matrix products, arithmetic and copies ran while one was open for 3% of the time, Pallas kernels for 3%

commit v1 on v0

v1 whole, which is shorter than its diff:
```python
import functools
import jax
import jax.numpy as jnp
from jax import lax
from jax.experimental import pallas as pl
from jax.experimental.pallas import tpu as pltpu
from jax.sharding import PartitionSpec as P

HD = 64
BLK = 64
NNB = 9
NBLK = 32
LEVELS = 5
SEND = 4
WIDE = 2 * HD
OWN = NBLK * BLK
PART = SEND * BLK
FILL = -1e30
HEAD_DEVICES = 8
OFFSETS = ((1, 0), (3, 0), (1, 1), (3, 1), (2, 0), (2, 1), (0, 1), (0, 0))
F32 = jnp.float32
BF16 = jnp.bfloat16

VM = pl.BlockSpec(memory_space=pltpu.VMEM)
SM = pl.BlockSpec(memory_space=pltpu.SMEM)
HB = pl.BlockSpec(memory_space=pltpu.HBM)


def swapped(block, bit):
    count = lax.axis_size("pix")
    route = [(low, low ^ (1 << bit)) for low in range(count)]
    return lax.ppermute(block, "pix", route)


def rows_of(start):
    return pl.ds(pl.multiple_of(start * BLK, BLK), BLK)


def offset_index(index, steps, core):
    chips = HEAD_DEVICES // 2
    return (index // 2 + steps) % chips * 2 + (index % 2 + core) % 2


def shifted(block, steps, core):
    route = [(i, offset_index(i, steps, core)) for i in range(HEAD_DEVICES)]
    return lax.ppermute(block, "head", route)


def limits(megabytes):
    return pltpu.CompilerParams(vmem_limit_bytes=megabytes * 2**20)


def split_kernel(key_ref, value_ref, *refs):
    parts, sems = refs[:-1], refs[-1]
    me = lax.axis_index("head")
    copies = []
    for t, (steps, core) in enumerate(OFFSETS):
        column = pl.ds(pl.multiple_of(offset_index(me, steps, core) * WIDE, WIDE), WIDE)
        for n, ref in enumerate((key_ref, value_ref)):
            copies.append(
                pltpu.make_async_copy(
                    ref.at[:, column], parts[t].at[:, n * WIDE : (n + 1) * WIDE], sems.at[2 * t + n]
                )
            )
    for copy in copies:
        copy.start()
    for copy in copies:
        copy.wait()


def split(keys, values):
    mine = keys.shape[0]
    return pl.pallas_call(
        split_kernel,
        out_shape=[pltpu.VMEM((mine, 2 * WIDE), BF16)] * HEAD_DEVICES,
        in_specs=[HB] * 2,
        out_specs=[VM] * HEAD_DEVICES,
        scratch_shapes=[pltpu.SemaphoreType.DMA((2 * HEAD_DEVICES,))],
        compiler_params=limits(4),
        cost_estimate=pl.CostEstimate(flops=0, bytes_accessed=2 * 2**20, transcendentals=0),
        name="split_keys_values",
    )(pltpu.with_memory_space_constraint(keys, pltpu.HBM), pltpu.with_memory_space_constraint(values, pltpu.HBM))


def pick_kernel(sends_ref, grad_ref, *refs):
    parts, refs = refs[:HEAD_DEVICES], refs[HEAD_DEVICES:]
    own_ref, near_ref, out_refs, sem = refs[0], refs[1], refs[2:-1], refs[-1]
    copy = pltpu.make_async_copy(grad_ref, near_ref, sem)
    copy.start()
    me = lax.axis_index("head")
    mine = OWN // HEAD_DEVICES
    for t, (steps, core) in enumerate(OFFSETS):
        source = offset_index(me, HEAD_DEVICES // 2 - steps, core)
        own_ref[pl.ds(pl.multiple_of(source * mine, mine), mine), :] = parts[t][...]
    for b in range(LEVELS):
        for s in range(SEND):
            out_refs[b][s * BLK : (s + 1) * BLK, :] = own_ref[rows_of(sends_ref[b, s]), :]
    copy.wait()


def pick(sends, parts, grad):
    return pl.pallas_call(
        pick_kernel,
        out_shape=[pltpu.VMEM((OWN, 2 * WIDE), BF16), pltpu.VMEM((OWN, WIDE), BF16)]
        + [pltpu.VMEM((PART, 2 * WIDE), BF16)] * LEVELS,
        in_specs=[SM, HB] + [VM] * HEAD_DEVICES,
        out_specs=[VM] * (2 + LEVELS),
        scratch_shapes=[pltpu.SemaphoreType.DMA],
        compiler_params=limits(8),
        cost_estimate=pl.CostEstimate(flops=0, bytes_accessed=4 * 2**20, transcendentals=0),
        name="pick_boundary",
    )(sends, pltpu.with_memory_space_constraint(grad, pltpu.HBM), *parts)


def pixel_grads(i, live, kv, q_ref, g_ref, att_ref, qg_ref, outs):
    at = rows_of(i)
    q = q_ref[at, :] * jnp.array(HD**-0.5, BF16)
    g = g_ref[at, :]
    low = lax.broadcasted_iota(jnp.int32, (BLK, WIDE), 1) < HD
    z = jnp.zeros((BLK, WIDE), BF16)
    both = jnp.concatenate(
        [
            jnp.concatenate([jnp.where(low, q, z), z], 1),
            jnp.concatenate([jnp.where(low, z, q), z], 1),
            jnp.concatenate([z, jnp.where(low, g, z)], 1),
            jnp.concatenate([z, jnp.where(low, z, g)], 1),
        ],
        0,
    )
    sd = lax.dot_general(kv, both, (((1,), (1,)), ((), ())), preferred_element_type=F32)
    s = [sd[j * BLK : (j + 1) * BLK, :WIDE] for j in range(NNB)]
    d = [sd[j * BLK : (j + 1) * BLK, WIDE:] for j in range(NNB)]
    s[-1] = jnp.where(live, s[-1], FILL)
    peak = functools.reduce(jnp.maximum, s)
    peak = jnp.max(peak, 0, keepdims=True)
    p = [jnp.exp(x - peak) for x in s]
    total = jnp.sum(sum(p[1:], p[0]), 0, keepdims=True)
    dot = [x * y for x, y in zip(p, d)]
    inv = 1.0 / total
    dot = jnp.sum(sum(dot[1:], dot[0]), 0, keepdims=True) * inv
    weights = [x * inv for x in p]
    rounded = jnp.concatenate([x.astype(BF16) for x in weights], 0)
    grads = jnp.concatenate([(x * (y - dot)).astype(BF16) for x, y in zip(weights, d)], 0)
    terms = lax.dot_general(
        jnp.concatenate([grads, rounded], 1), both, (((1,), (0,)), ((), ())), preferred_element_type=F32
    )
    down = (((0,), (0,)), ((), ()))
    qg = lax.dot_general(grads, kv[:, :WIDE], down, preferred_element_type=F32)
    att = lax.dot_general(rounded, kv[:, WIDE:], down, preferred_element_type=F32)
    att_ref[at, :] = jnp.where(low, att[:BLK], att[BLK:]).astype(BF16)
    qg_ref[at, :] = (jnp.where(low, qg[:BLK], qg[BLK:]) * HD**-0.5).astype(BF16)
    for copy in outs(i):
        copy.start()
    return [terms[j * BLK : (j + 1) * BLK] for j in range(NNB)]


def row_copies(at, staged, outs, sems):
    return [
        pltpu.make_async_copy(x.at[rows_of(at), :], y.at[rows_of(at), :], sems.at[n, at])
        for n, (x, y) in enumerate(zip(staged, outs))
    ]


def inner_kernel(unroll, rows_ref, counts_ref, q_ref, g_ref, own_ref, att_ref, qg_ref, acc_ref, *refs):
    list_ref, staged, sems = refs[0], refs[1:3], refs[3]
    outs = lambda i: row_copies(i, staged, (att_ref, qg_ref), sems)
    steps = NBLK - LEVELS * SEND
    acc_ref[...] = jnp.zeros_like(acc_ref)

    def note(i, count):
        list_ref[count] = i
        return count + (rows_ref[i, 1] < NBLK).astype(jnp.int32)

    lax.fori_loop(0, NBLK, note, jnp.int32(0))

    def step(t, carry):
        for u in range(unroll):
            i = list_ref[t * unroll + u]
            at = [rows_of(rows_ref[i, j]) for j in range(NNB)]
            kv = jnp.concatenate([own_ref[a, :] for a in at], 0)
            terms = pixel_grads(i, counts_ref[i] > NNB - 1, kv, q_ref, g_ref, *staged, outs)
            for j in range(NNB):
                acc_ref[at[j], :] += terms[j]
        return carry

    lax.fori_loop(0, steps // unroll, step, 0)

    def settle(t, carry):
        for copy in outs(list_ref[t]):
            copy.wait()
        return carry

    lax.fori_loop(0, steps, settle, 0)


def inner(rows, counts, q, g, own):
    return pl.pallas_call(
        functools.partial(inner_kernel, 2),
        out_shape=[
            pltpu.HBM((OWN, WIDE), BF16),
            pltpu.HBM((OWN, WIDE), BF16),
            pltpu.VMEM((OWN, 2 * WIDE), F32),
        ],
        in_specs=[SM, SM] + [VM] * 3,
        out_specs=[HB, HB, VM],
        scratch_shapes=[pltpu.SMEM((NBLK + 1,), jnp.int32)]
        + [pltpu.VMEM((OWN, WIDE), BF16)] * 2
        + [pltpu.SemaphoreType.DMA((2, NBLK))],
        compiler_params=limits(16),
        cost_estimate=pl.CostEstimate(flops=4 * 10**9, bytes_accessed=8 * 2**20, transcendentals=10**6),
        name="attend_inner",
    )(rows, counts, q, g, own)


def outer_kernel(unroll, sends_ref, rows_ref, counts_ref, q_ref, g_ref, own_ref, *refs):
    recv_refs, refs = refs[:LEVELS], refs[LEVELS + 3 :]
    att_ref, qg_ref, acc_ref = refs[:3]
    back_refs, refs = refs[3 : 3 + LEVELS], refs[3 + LEVELS :]
    far_ref, back_ref, staged, sems, back_sems = refs[0], refs[1], refs[2:4], refs[4], refs[5]
    outs = lambda i: row_copies(i, staged, (att_ref, qg_ref), sems)
    backs = [
        pltpu.make_async_copy(back_ref.at[b * PART : (b + 1) * PART, :], back_refs[b], back_sems.at[b])
        for b in range(LEVELS)
    ]
    for b in range(LEVELS):
        far_ref[b * PART : (b + 1) * PART, :] = recv_refs[b][...]

    def step(t, carry):
        for u in range(unroll):
            e = t * unroll + u
            i = sends_ref[e // SEND, e % SEND]
            at = [rows_of(rows_ref[i, j]) if j != 1 else None for j in range(NNB)]
            far = rows_of(e)
            kv = jnp.concatenate([own_ref[a, :] if a is not None else far_ref[far, :] for a in at], 0)
            terms = pixel_grads(i, counts_ref[i] > NNB - 1, kv, q_ref, g_ref, *staged, outs)
            for j in range(NNB):
                if j == 1:
                    back_ref[far, :] = terms[j].astype(BF16)
                else:
                    acc_ref[at[j], :] += terms[j]
        for b in range(LEVELS):
            pl.when(t == (b + 1) * SEND // unroll - 1)(backs[b].start)
        return carry

    lax.fori_loop(0, LEVELS * SEND // unroll, step, 0)

    def settle(e, carry):
        for copy in outs(sends_ref[e // SEND, e % SEND]):
            copy.wait()
        return carry

    lax.fori_loop(0, LEVELS * SEND, settle, 0)
    for copy in backs:
        copy.wait()


def outer(sends, rows, counts, q, g, own, recv, done):
    far = (LEVELS * PART, 2 * WIDE)
    return pl.pallas_call(
        functools.partial(outer_kernel, 2),
        out_shape=[
            pltpu.HBM((OWN, WIDE), BF16),
            pltpu.HBM((OWN, WIDE), BF16),
            pltpu.VMEM((OWN, 2 * WIDE), F32),
        ]
        + [pltpu.HBM((PART, 2 * WIDE), BF16)] * LEVELS,
        in_specs=[SM] * 3 + [VM] * (3 + LEVELS) + [HB, HB, VM],
        out_specs=[HB, HB, VM] + [HB] * LEVELS,
        scratch_shapes=[pltpu.VMEM(far, BF16), pltpu.VMEM(far, BF16)]
        + [pltpu.VMEM((OWN, WIDE), BF16)] * 2
        + [pltpu.SemaphoreType.DMA((2, NBLK)), pltpu.SemaphoreType.DMA((LEVELS,))],
        input_output_aliases={6 + LEVELS + n: n for n in range(3)},
        compiler_params=limits(16),
        cost_estimate=pl.CostEstimate(flops=8 * 10**9, bytes_accessed=8 * 2**20, transcendentals=2 * 10**6),
        name="attend_outer",
    )(sends, rows, counts, q, g, own, *recv, *done)


def join_kernel(sends_ref, acc_ref, *refs):
    arrived_refs = refs[:LEVELS]
    key_ref, value_ref = refs[LEVELS : LEVELS + 2]
    key_ref[...] = acc_ref[:, :WIDE].astype(BF16)
    value_ref[...] = acc_ref[:, WIDE:].astype(BF16)
    for b in range(LEVELS):
        for s in range(SEND):
            at = rows_of(sends_ref[b, s])
            both = acc_ref[at, :] + arrived_refs[b][s * BLK : (s + 1) * BLK, :].astype(F32)
            key_ref[at, :] = both[:, :WIDE].astype(BF16)
            value_ref[at, :] = both[:, WIDE:].astype(BF16)


def join(sends, acc, arrived):
    return pl.pallas_call(
        join_kernel,
        out_shape=[jax.ShapeDtypeStruct((OWN, WIDE), BF16)] * 2,
        in_specs=[SM] + [VM] * (1 + LEVELS),
        out_specs=[VM] * 2,
        compiler_params=limits(10),
        cost_estimate=pl.CostEstimate(flops=10**6, bytes_accessed=4 * 2**20, transcendentals=0),
        name="join_gradients",
    )(sends, acc, *arrived)


def body(query_rows, key_rows, value_rows, out_grad, boundary_send_blocks, neighbours, live_count):
    heads = lax.axis_size("head")
    mine = query_rows.shape[0]
    my_range = lax.axis_index("pix")
    sends = lax.dynamic_index_in_dim(boundary_send_blocks, my_range, 0, keepdims=False)
    rows = lax.dynamic_slice_in_dim(neighbours, my_range * NBLK, NBLK, 0)
    counts = lax.dynamic_slice_in_dim(live_count, my_range * NBLK, NBLK, 0)

    parts = split(key_rows, value_rows)
    parts = [shifted(x, *o) if o != (0, 0) else x for x, o in zip(parts, OFFSETS)]
    q = query_rows.reshape(mine, heads, WIDE).transpose(1, 0, 2)
    q, parts[0] = lax.optimization_barrier((q, parts[0]))
    q = lax.all_to_all(q, "head", 0, 0, tiled=True).reshape(OWN, WIDE)
    own, grad, *outgoing = pick(sends, parts, out_grad)
    recv = [swapped(outgoing[b], b) for b in range(LEVELS)]
    done = inner(rows, counts, q, grad, own)
    attended, query_grad, acc, *back = outer(sends, rows, counts, q, grad, own, recv, done)
    arrived = [swapped(back[b], b) for b in range(LEVELS)]
    attended = lax.all_to_all(attended.reshape(heads, mine, WIDE), "head", 0, 0, tiled=True)
    attended = attended.transpose(1, 0, 2).reshape(mine, heads * WIDE)
    key_grad, value_grad = join(sends, acc, arrived)
    return attended, query_grad, key_grad, value_grad


def solution(mesh):
    rows = P(("pix", "head"), None)
    split = P("pix", "head")
    return jax.shard_map(
        body,
        mesh=mesh,
        in_specs=(rows, rows, rows, split, P(), P(), P()),
        out_specs=(rows, split, split, split),
        check_vma=False,
    )
```

time: 104 us -> 101 us (0.971)
  Pallas kernels: 26.7 us -> 32 us
  local copies, waits for them, and re-layouts: 11.5 us -> 7.71 us
  starting transfers between devices: 37.5 us -> 35.4 us
  other arithmetic: 1.11 us -> 0 us
    ppermute x0 -> x7, waiting for transfers between devices: none -> 14.3 us  [shifted(): return lax.ppermute(block, 'head', route)]
    all_to_all x2 -> x1, waiting for transfers between devices: 13.6 us -> 0.01 us  [body(): q = lax.all_to_all(q, 'head', 0, 0, tiled=True).reshape(OWN, WIDE)]
    ppermute x0 -> x7, starting transfers between devices: none -> 7.89 us  [shifted(): return lax.ppermute(block, 'head', route)]
    pallas_call x2 -> x4, Pallas kernels: 24.9 us -> 30.2 us  [the longest x1 15.8 us: outer(): pl.pallas_call(functools.partial(outer_kernel, 2), out_shape=[pltpu.HBM((...]
    ppermute x10, starting transfers between devices: 22 us -> 17.1 us  [swapped(): return lax.ppermute(block, 'pix', route)]
    all_to_all x2 -> x1, starting transfers between devices: 10.6 us -> 6.53 us  [body(): q = lax.all_to_all(q, 'head', 0, 0, tiled=True).reshape(OWN, WIDE)]
    unnamed x21 -> x13, local copies, waits for them, and re-layouts: 6.67 us -> 4.13 us
    reshape x1 -> x0, local copies, waits for them, and re-layouts: 1.29 us -> none  [by_head(): return x.reshape(mine, heads, WIDE)]
  transfers between devices with their start and end apart: 13 -> 19, of which waited for: 6 -> 6; matrix products, arithmetic and copies ran while one was open for 3% -> 3% of each run, Pallas kernels for 3% -> 15%
where the time goes in v1:
time: 101 us; the launch traced here: 100 us
  starting transfers between devices  35.4 us (35%)
  Pallas kernels  32 us (32%)
  waiting for transfers between devices  24.3 us (24%)
  local copies, waits for them, and re-layouts  7.71 us (8%)
    ppermute x10, starting transfers between devices, swapped(): return lax.ppermute(block, 'pix', route)  17.1 us
    pallas_call x1, Pallas kernels, outer(): pl.pallas_call(functools.partial(outer_kernel, 2), out_shape=[pltpu.HBM((...  15.8 us
    ppermute x7, waiting for transfers between devices, shifted(): return lax.ppermute(block, 'head', route)  14.3 us
    pallas_call x1, Pallas kernels, inner(): pl.pallas_call(functools.partial(inner_kernel, 2), out_shape=[pltpu.HBM((...  10.4 us
    ppermute x10, waiting for transfers between devices, swapped(): return lax.ppermute(block, 'pix', route)  9.98 us
    ppermute x7, starting transfers between devices, shifted(): return lax.ppermute(block, 'head', route)  7.89 us
    all_to_all x1, starting transfers between devices, body(): q = lax.all_to_all(q, 'head', 0, 0, tiled=True).reshape(OWN, WIDE)  6.53 us
    unnamed x13, local copies, waits for them, and re-layouts  4.13 us
  transfers between devices with their start and end apart: 19, of which 6 were waited for; matrix products, arithmetic and copies ran while one was open for 3% of the time, Pallas kernels for 15%

profile of v1, /device:TPU:8, one launch (start us, length us, event | category | flops | bytes accessed | tf_op | source)
XLA Modules:
  0.0 100.1 jit_solution(14981545386037319085)
XLA Ops:
  0.6 0.0 copy-start
  0.6 0.0 copy-start.5
  0.7 1.5 %split_keys_values.1 = (bf16[256,256]{1,0:T(8,128)(2,1)S(1)}, bf16[256,256]{1,0:T(8,128)(2,1)S(1)}, bf16[256,256]{1,0:T(8,128)(2,1)S(1)}, bf16[256,256]{1,0:T(8,...) custom-call(bf16[256,1024]{1,0:T(8,128)(2,1)} %key_ref.1, ...), custom_call_target="tpu_custom_call" | custom-call | bytes 2097152 | tf_op jit(solution)/shard_map/split_keys_values/pallas_call | solution.py:73
  2.1 1.7 %collective-permute-start = (bf16[256,256]{1,0:T(8,128)(2,1)S(1)}, bf16[256,256]{1,0:T(8,128)(2,1)S(1)}, u32[]{:S(2)}, u32[]{:S(2)}) collective-permute-start(bf16[256,256]{1,0:T(8,128)(2,1)S(1)} %get-tuple-element.34), channel_id=1, source_target_pairs={{0,2},{1,3},{2,4},{3,5},{4,6},{5,7},{6,0},{7,1},{8,10},{9,11},{10,... | collective-permute-start | bytes 393224 | tf_op jit(solution)/shard_map/ppermute | solution.py:46
  3.8 0.0 copy-done
  3.8 0.9 bitcast_bitcast_fusion
  4.7 2.8 %collective-permute-done.refs_0_ = bf16[256,256]{1,0:T(8,128)(2,1)S(1)} collective-permute-done((bf16[256,256]{1,0:T(8,128)(2,1)S(1)}, bf16[256,256]{1,0:T(8,128)(2,1)S(1)}, u32[]{:S(2)}, u32[]{:S(2)}) %collective-permute-start) | collective-permute-done | bytes 131104 | tf_op jit(solution)/shard_map/ppermute | solution.py:46
  7.5 6.5 %all-to-all-start = ((bf16[8,256,128]{2,1,0:T(8,128)(2,1)}), bf16[8,256,128]{2,1,0:T(8,128)(2,1)S(1)}, u32[]{:S(2)}, u32[]{:S(2)}) async-start(bf16[8,256,128]{2,1,0:T(8,128)(2,1)} %bitcast_bitcast_fusion), calls=%async_computation | async-start | bytes 1048576 | tf_op jit(solution)/shard_map/all_to_all | solution.py:316
  14.0 0.2 collective-permute-start.1
  14.2 1.3 %collective-permute-start.2 = (bf16[256,256]{1,0:T(8,128)(2,1)S(1)}, bf16[256,256]{1,0:T(8,128)(2,1)S(1)}, u32[]{:S(2)}, u32[]{:S(2)}) collective-permute-start(bf16[256,256]{1,0:T(8,128)(2,1)S(1)} %get-tuple-element.38), channel_id=1, source_target_pairs={{0,3},{1,2},{2,5},{3,4},{4,7},{5,6},{6,1},{7,0},{8,11},{9,10},{10,... | collective-permute-start | bytes 393224 | tf_op jit(solution)/shard_map/ppermute | solution.py:46
  15.5 1.2 %collective-permute-start.3 = (bf16[256,256]{1,0:T(8,128)(2,1)S(1)}, bf16[256,256]{1,0:T(8,128)(2,1)S(1)}, u32[]{:S(2)}, u32[]{:S(2)}) collective-permute-start(bf16[256,256]{1,0:T(8,128)(2,1)S(1)} %get-tuple-element.39), channel_id=1, source_target_pairs={{0,7},{1,6},{2,1},{3,0},{4,3},{5,2},{6,5},{7,4},{8,15},{9,14},{10,... | collective-permute-start | bytes 393224 | tf_op jit(solution)/shard_map/ppermute | solution.py:46
  16.7 2.1 %collective-permute-start.4 = (bf16[256,256]{1,0:T(8,128)(2,1)S(1)}, bf16[256,256]{1,0:T(8,128)(2,1)S(1)}, u32[]{:S(2)}, u32[]{:S(2)}) collective-permute-start(bf16[256,256]{1,0:T(8,128)(2,1)S(1)} %get-tuple-element.40), channel_id=1, source_target_pairs={{0,4},{1,5},{2,6},{3,7},{4,0},{5,1},{6,2},{7,3},{8,12},{9,13},{10,... | collective-permute-start | bytes 393224 | tf_op jit(solution)/shard_map/ppermute | solution.py:46
  18.8 1.4 %collective-permute-start.5 = (bf16[256,256]{1,0:T(8,128)(2,1)S(1)}, bf16[256,256]{1,0:T(8,128)(2,1)S(1)}, u32[]{:S(2)}, u32[]{:S(2)}) collective-permute-start(bf16[256,256]{1,0:T(8,128)(2,1)S(1)} %get-tuple-element.41), channel_id=1, source_target_pairs={{0,5},{1,4},{2,7},{3,6},{4,1},{5,0},{6,3},{7,2},{8,13},{9,12},{10,... | collective-permute-start | bytes 393224 | tf_op jit(solution)/shard_map/ppermute | solution.py:46
  20.2 5.3 %collective-permute-done.1.refs_1_ = bf16[256,256]{1,0:T(8,128)(2,1)S(1)} collective-permute-done((bf16[256,256]{1,0:T(8,128)(2,1)S(1)}, bf16[256,256]{1,0:T(8,128)(2,1)S(1)}, u32[]{:S(2)}, u32[]{:S(2)}) %collective-permute-start.1) | collective-permute-done | bytes 131104 | tf_op jit(solution)/shard_map/ppermute | solution.py:46
  25.6 0.0 collective-permute-start.6
  25.6 0.8 constant_dynamic-slice_fusion
  26.3 0.8 dynamic_slice.12.counts_ref
  27.1 0.1 copy.21.rows_ref
  27.2 0.0 copy-done.5
  27.2 0.1 constant_dynamic-slice_fusion.1
  27.3 0.1 copy.14
  27.4 0.1 copy.18.sends_ref
  27.5 0.0 collective-permute-done.2.refs_2_
  27.5 0.0 collective-permute-done.3.refs_3_
  27.5 4.4 %collective-permute-done.4.refs_4_ = bf16[256,256]{1,0:T(8,128)(2,1)S(1)} collective-permute-done((bf16[256,256]{1,0:T(8,128)(2,1)S(1)}, bf16[256,256]{1,0:T(8,128)(2,1)S(1)}, u32[]{:S(2)}, u32[]{:S(2)}) %collective-permute-start.4) | collective-permute-done | bytes 131104 | tf_op jit(solution)/shard_map/ppermute | solution.py:46
  31.8 1.9 %collective-permute-done.5.refs_5_ = bf16[256,256]{1,0:T(8,128)(2,1)S(1)} collective-permute-done((bf16[256,256]{1,0:T(8,128)(2,1)S(1)}, bf16[256,256]{1,0:T(8,128)(2,1)S(1)}, u32[]{:S(2)}, u32[]{:S(2)}) %collective-permute-start.5) | collective-permute-done | bytes 131104 | tf_op jit(solution)/shard_map/ppermute | solution.py:46
  33.7 0.0 collective-permute-done.6.refs_6_
  33.7 2.5 %pick_boundary.1 = (bf16[2048,256]{1,0:T(8,128)(2,1)S(1)}, bf16[2048,128]{1,0:T(8,128)(2,1)S(1)}, bf16[256,256]{1,0:T(8,128)(2,1)}, bf16[256,256]{1,0:T(8,128)(2...) custom-call(s32[5,4]{1,0:T(8,128)S(1)} %copy.18.sends_ref, ...), custom_call_target="tpu_custom_call" | custom-call | bytes 4194304 | tf_op jit(solution)/shard_map/pick_boundary/pallas_call | solution.py:102
  36.2 0.0 copy-start.1
  36.2 1.0 copy-done.1
  37.2 0.0 copy-start.3
  37.2 0.8 copy-done.3
  38.0 0.5 collective-permute-start.7
  38.5 3.3 %collective-permute-start.8 = (bf16[256,256]{1,0:T(8,128)(2,1)}, bf16[256,256]{1,0:T(8,128)(2,1)S(1)}, u32[]{:S(2)}, u32[]{:S(2)}) collective-permute-start(bf16[256,256]{1,0:T(8,128)(2,1)} %get-tuple-element.47), channel_id=1, source_target_pairs={{0,16},{8,24},{16,0},{24,8},{32,48},{40,56},{48,32},{56,40},{64,80... | collective-permute-start | bytes 393224 | tf_op jit(solution)/shard_map/ppermute | solution.py:32
  41.8 4.5 %collective-permute-start.9 = (bf16[256,256]{1,0:T(8,128)(2,1)}, bf16[256,256]{1,0:T(8,128)(2,1)}, u32[]{:S(2)}, u32[]{:S(2)}) collective-permute-start(bf16[256,256]{1,0:T(8,128)(2,1)} %get-tuple-element.48), channel_id=1, source_target_pairs={{0,32},{8,40},{16,48},{24,56},{32,0},{40,8},{48,16},{56,24},{64,96... | collective-permute-start | bytes 393224 | tf_op jit(solution)/shard_map/ppermute | solution.py:32
  46.3 1.5 %collective-permute-start.10 = (bf16[256,256]{1,0:T(8,128)(2,1)}, bf16[256,256]{1,0:T(8,128)(2,1)}, u32[]{:S(2)}, u32[]{:S(2)}) collective-permute-start(bf16[256,256]{1,0:T(8,128)(2,1)} %get-tuple-element.49), channel_id=1, source_target_pairs={{0,64},{8,72},{16,80},{24,88},{32,96},{40,104},{48,112},{56,120},{... | collective-permute-start | bytes 393224 | tf_op jit(solution)/shard_map/ppermute | solution.py:32
  47.8 2.7 %collective-permute-start.11 = (bf16[256,256]{1,0:T(8,128)(2,1)}, bf16[256,256]{1,0:T(8,128)(2,1)}, u32[]{:S(2)}, u32[]{:S(2)}) collective-permute-start(bf16[256,256]{1,0:T(8,128)(2,1)} %get-tuple-element.50), channel_id=1, source_target_pairs={{0,128},{8,136},{16,144},{24,152},{32,160},{40,168},{48,176},{56,1... | collective-permute-start | bytes 393224 | tf_op jit(solution)/shard_map/ppermute | solution.py:32
  50.5 0.0 all-to-all-done
  50.5 0.0 copy-start.2
  50.5 1.2 %copy-done.2 = bf16[2048,256]{1,0:T(8,128)(2,1)S(1)} copy-done((bf16[2048,256]{1,0:T(8,128)(2,1)S(1)}, bf16[2048,256]{1,0:T(8,128)(2,1)}, u32[]{:S(2)}) %copy-start.2) | copy-done | bytes 1048600
  51.7 0.0 copy-start.4
  51.7 1.0 %copy-done.4 = bf16[2048,128]{1,0:T(8,128)(2,1)S(1)} copy-done((bf16[2048,128]{1,0:T(8,128)(2,1)S(1)}, bf16[2048,128]{1,0:T(8,128)(2,1)}, u32[]{:S(2)}) %copy-start.4) | copy-done | bytes 524312
  52.8 10.4 %attend_inner.1 = (bf16[2048,128]{1,0:T(8,128)(2,1)}, bf16[2048,128]{1,0:T(8,128)(2,1)}, f32[2048,256]{1,0:T(8,128)S(1)}) custom-call(s32[32,9]{1,0:T(8,128)S(1)} %copy.21.rows_ref, s32[32]{0:T(128)S(1)} %dynamic_slice.12.counts_ref, bf16[2048,128]{1,0:T(8,128)(2,1)S(1)} %bitcast.16, bf16[2048,128]{1,0:T(8,128)(2,1)S(1)} %copy-done.4, ...), custom_call_target="tpu_custom_call" | custom-call | flops 4000000000 | bytes 8388608 | tf_op jit(solution)/shard_map/attend_inner/pallas_call | solution.py:197
  63.2 0.0 collective-permute-done.7.refs_0_
  63.2 0.0 collective-permute-done.8.refs_1_
  63.2 0.0 collective-permute-done.9.refs_2_
  63.2 0.0 collective-permute-done.10.refs_3_
  63.2 0.0 collective-permute-done.11.refs_4_
  63.2 15.8 %attend_outer.1 = (bf16[2048,128]{1,0:T(8,128)(2,1)}, bf16[2048,128]{1,0:T(8,128)(2,1)}, f32[2048,256]{1,0:T(8,128)S(1)}, bf16[256,256]{1,0:T(8,128)(2,1)}, bf16...) custom-call(s32[5,4]{1,0:T(8,128)S(1)} %copy.18.sends_ref, ...), custom_call_target="tpu_custom_call", output_to_operand_aliasing={{0}: (11, {}), {1}: (12, {}), {2}: (13, {})} | custom-call | flops 8000000000 | bytes 8388608 | tf_op jit(solution)/shard_map/attend_outer/pallas_call | solution.py:259
  79.0 3.9 %all-to-all-start.1 = ((bf16[8,256,128]{2,1,0:T(8,128)(2,1)}), bf16[8,256,128]{2,1,0:T(8,128)(2,1)S(1)}, u32[]{:S(2)}, u32[]{:S(2)}) async-start(bf16[8,256,128]{2,1,0:T(8,128)(2,1)} %bitcast.18), calls=%async_computation.1 | async-start | bytes 1048576 | tf_op jit(solution)/shard_map/all_to_all | solution.py:322
  82.9 1.0 %collective-permute-start.12 = (bf16[256,256]{1,0:T(8,128)(2,1)}, bf16[256,256]{1,0:T(8,128)(2,1)S(1)}, u32[]{:S(2)}, u32[]{:S(2)}) collective-permute-start(bf16[256,256]{1,0:T(8,128)(2,1)} %get-tuple-element.57), channel_id=1, source_target_pairs={{0,8},{8,0},{16,24},{24,16},{32,40},{40,32},{48,56},{56,48},{64,72... | collective-permute-start | bytes 393224 | tf_op jit(solution)/shard_map/ppermute | solution.py:32
  83.9 1.5 %collective-permute-start.13 = (bf16[256,256]{1,0:T(8,128)(2,1)}, bf16[256,256]{1,0:T(8,128)(2,1)S(1)}, u32[]{:S(2)}, u32[]{:S(2)}) collective-permute-start(bf16[256,256]{1,0:T(8,128)(2,1)} %get-tuple-element.58), channel_id=1, source_target_pairs={{0,16},{8,24},{16,0},{24,8},{32,48},{40,56},{48,32},{56,40},{64,80... | collective-permute-start | bytes 393224 | tf_op jit(solution)/shard_map/ppermute | solution.py:32
  85.4 0.0 collective-permute-start.14
  85.4 0.2 collective-permute-start.15
  85.6 1.9 %collective-permute-start.16 = (bf16[256,256]{1,0:T(8,128)(2,1)}, bf16[256,256]{1,0:T(8,128)(2,1)S(1)}, u32[]{:S(2)}, u32[]{:S(2)}) collective-permute-start(bf16[256,256]{1,0:T(8,128)(2,1)} %get-tuple-element.61), channel_id=1, source_target_pairs={{0,128},{8,136},{16,144},{24,152},{32,160},{40,168},{48,176},{56,1... | collective-permute-start | bytes 393224 | tf_op jit(solution)/shard_map/ppermute | solution.py:32
  87.5 4.1 %collective-permute-done.12.refs_0_ = bf16[256,256]{1,0:T(8,128)(2,1)S(1)} collective-permute-done((bf16[256,256]{1,0:T(8,128)(2,1)}, bf16[256,256]{1,0:T(8,128)(2,1)S(1)}, u32[]{:S(2)}, u32[]{:S(2)}) %collective-permute-start.12) | collective-permute-done | bytes 131104 | tf_op jit(solution)/shard_map/ppermute | solution.py:32
  91.6 5.8 %collective-permute-done.13.refs_1_ = bf16[256,256]{1,0:T(8,128)(2,1)S(1)} collective-permute-done((bf16[256,256]{1,0:T(8,128)(2,1)}, bf16[256,256]{1,0:T(8,128)(2,1)S(1)}, u32[]{:S(2)}, u32[]{:S(2)}) %collective-permute-start.13) | collective-permute-done | bytes 131104 | tf_op jit(solution)/shard_map/ppermute | solution.py:32
  97.4 0.0 collective-permute-done.14.refs_2_
  97.4 0.0 collective-permute-done.15.refs_3_
  97.4 0.0 collective-permute-done.16.refs_4_
  97.5 1.8 %join_gradients.1 = (bf16[2048,128]{1,0:T(8,128)(2,1)}, bf16[2048,128]{1,0:T(8,128)(2,1)}) custom-call(s32[5,4]{1,0:T(8,128)S(1)} %copy.18.sends_ref, f32[2048,256]{1,0:T(8,128)S(1)} %get-tuple-element.56.acc_ref, bf16[256,256]{1,0:T(8,128)(2,1)S(1)} %collective-permute-done.12.refs_0_, bf16[256,256]{1,0:T(8,128)(2,1)S(1)} %collective-permute-done.13.refs_1_, ...), custom_call_target="tpu_custom_call" | custom-call | flops 1000000 | bytes 4194304 | tf_op jit(solution)/shard_map/join_gradients/pallas_call | solution.py:293
  99.3 0.0 all-to-all-done.1
  99.3 0.9 copy_bitcast_fusion
Async XLA Ops:
  0.6 3.2 %copy-start = (bf16[256,1024]{1,0:T(8,128)(2,1)S(1)}, bf16[256,1024]{1,0:T(8,128)(2,1)}, u32[]{:S(2)}) copy-start(bf16[256,1024]{1,0:T(8,128)(2,1)} %param.7) | copy-start | bytes 1572868
  0.6 26.5 %copy-start.5 = (s32[32,5,4]{0,2,1:T(4,128)S(1)}, s32[32,5,4]{0,2,1:T(4,128)}, u32[]{:S(2)}) copy-start(s32[32,5,4]{0,2,1:T(4,128)} %param.11) | copy-start | bytes 7684
  2.1 5.3 %collective-permute-start = (bf16[256,256]{1,0:T(8,128)(2,1)S(1)}, bf16[256,256]{1,0:T(8,128)(2,1)S(1)}, u32[]{:S(2)}, u32[]{:S(2)}) collective-permute-start(bf16[256,256]{1,0:T(8,128)(2,1)S(1)} %get-tuple-element.34), channel_id=1, source_target_pairs={{0,2},{1,3},{2,4},{3,5},{4,6},{5,7},{6,0},{7,1},{8,10},{9,11},{10,... | collective-permute-start | bytes 393224 | tf_op jit(solution)/shard_map/ppermute | solution.py:46
  7.5 43.1 %all-to-all-start = ((bf16[8,256,128]{2,1,0:T(8,128)(2,1)}), bf16[8,256,128]{2,1,0:T(8,128)(2,1)S(1)}, u32[]{:S(2)}, u32[]{:S(2)}) async-start(bf16[8,256,128]{2,1,0:T(8,128)(2,1)} %bitcast_bitcast_fusion), calls=%async_computation | async-start | bytes 1048576 | tf_op jit(solution)/shard_map/all_to_all | solution.py:316
  14.0 11.6 %collective-permute-start.1 = (bf16[256,256]{1,0:T(8,128)(2,1)S(1)}, bf16[256,256]{1,0:T(8,128)(2,1)S(1)}, u32[]{:S(2)}, u32[]{:S(2)}) collective-permute-start(bf16[256,256]{1,0:T(8,128)(2,1)S(1)} %get-tuple-element.37), channel_id=1, source_target_pairs={{0,6},{1,7},{2,0},{3,1},{4,2},{5,3},{6,4},{7,5},{8,14},{9,15},{10,... | collective-permute-start | bytes 393224 | tf_op jit(solution)/shard_map/ppermute | solution.py:46
  14.2 13.3 %collective-permute-start.2 = (bf16[256,256]{1,0:T(8,128)(2,1)S(1)}, bf16[256,256]{1,0:T(8,128)(2,1)S(1)}, u32[]{:S(2)}, u32[]{:S(2)}) collective-permute-start(bf16[256,256]{1,0:T(8,128)(2,1)S(1)} %get-tuple-element.38), channel_id=1, source_target_pairs={{0,3},{1,2},{2,5},{3,4},{4,7},{5,6},{6,1},{7,0},{8,11},{9,10},{10,... | collective-permute-start | bytes 393224 | tf_op jit(solution)/shard_map/ppermute | solution.py:46
  15.5 12.0 %collective-permute-start.3 = (bf16[256,256]{1,0:T(8,128)(2,1)S(1)}, bf16[256,256]{1,0:T(8,128)(2,1)S(1)}, u32[]{:S(2)}, u32[]{:S(2)}) collective-permute-start(bf16[256,256]{1,0:T(8,128)(2,1)S(1)} %get-tuple-element.39), channel_id=1, source_target_pairs={{0,7},{1,6},{2,1},{3,0},{4,3},{5,2},{6,5},{7,4},{8,15},{9,14},{10,... | collective-permute-start | bytes 393224 | tf_op jit(solution)/shard_map/ppermute | solution.py:46
  16.7 15.1 %collective-permute-start.4 = (bf16[256,256]{1,0:T(8,128)(2,1)S(1)}, bf16[256,256]{1,0:T(8,128)(2,1)S(1)}, u32[]{:S(2)}, u32[]{:S(2)}) collective-permute-start(bf16[256,256]{1,0:T(8,128)(2,1)S(1)} %get-tuple-element.40), channel_id=1, source_target_pairs={{0,4},{1,5},{2,6},{3,7},{4,0},{5,1},{6,2},{7,3},{8,12},{9,13},{10,... | collective-permute-start | bytes 393224 | tf_op jit(solution)/shard_map/ppermute | solution.py:46
  18.8 14.9 %collective-permute-start.5 = (bf16[256,256]{1,0:T(8,128)(2,1)S(1)}, bf16[256,256]{1,0:T(8,128)(2,1)S(1)}, u32[]{:S(2)}, u32[]{:S(2)}) collective-permute-start(bf16[256,256]{1,0:T(8,128)(2,1)S(1)} %get-tuple-element.41), channel_id=1, source_target_pairs={{0,5},{1,4},{2,7},{3,6},{4,1},{5,0},{6,3},{7,2},{8,13},{9,12},{10,... | collective-permute-start | bytes 393224 | tf_op jit(solution)/shard_map/ppermute | solution.py:46
  25.6 8.1 %collective-permute-start.6 = (bf16[256,256]{1,0:T(8,128)(2,1)S(1)}, bf16[256,256]{1,0:T(8,128)(2,1)S(1)}, u32[]{:S(2)}, u32[]{:S(2)}) collective-permute-start(bf16[256,256]{1,0:T(8,128)(2,1)S(1)} %get-tuple-element.42), channel_id=1, source_target_pairs={{0,1},{1,0},{2,3},{3,2},{4,5},{5,4},{6,7},{7,6},{8,9},{9,8},{10,11... | collective-permute-start | bytes 393224 | tf_op jit(solution)/shard_map/ppermute | solution.py:46
  36.2 1.0 copy-start.1
  37.2 0.8 copy-start.3
  38.0 25.2 %collective-permute-start.7 = (bf16[256,256]{1,0:T(8,128)(2,1)}, bf16[256,256]{1,0:T(8,128)(2,1)S(1)}, u32[]{:S(2)}, u32[]{:S(2)}) collective-permute-start(bf16[256,256]{1,0:T(8,128)(2,1)} %get-tuple-element.46), channel_id=1, source_target_pairs={{0,8},{8,0},{16,24},{24,16},{32,40},{40,32},{48,56},{56,48},{64,72... | collective-permute-start | bytes 393224 | tf_op jit(solution)/shard_map/ppermute | solution.py:32
  38.5 24.7 %collective-permute-start.8 = (bf16[256,256]{1,0:T(8,128)(2,1)}, bf16[256,256]{1,0:T(8,128)(2,1)S(1)}, u32[]{:S(2)}, u32[]{:S(2)}) collective-permute-start(bf16[256,256]{1,0:T(8,128)(2,1)} %get-tuple-element.47), channel_id=1, source_target_pairs={{0,16},{8,24},{16,0},{24,8},{32,48},{40,56},{48,32},{56,40},{64,80... | collective-permute-start | bytes 393224 | tf_op jit(solution)/shard_map/ppermute | solution.py:32
  41.8 21.4 %collective-permute-start.9 = (bf16[256,256]{1,0:T(8,128)(2,1)}, bf16[256,256]{1,0:T(8,128)(2,1)}, u32[]{:S(2)}, u32[]{:S(2)}) collective-permute-start(bf16[256,256]{1,0:T(8,128)(2,1)} %get-tuple-element.48), channel_id=1, source_target_pairs={{0,32},{8,40},{16,48},{24,56},{32,0},{40,8},{48,16},{56,24},{64,96... | collective-permute-start | bytes 393224 | tf_op jit(solution)/shard_map/ppermute | solution.py:32
  46.3 16.9 %collective-permute-start.10 = (bf16[256,256]{1,0:T(8,128)(2,1)}, bf16[256,256]{1,0:T(8,128)(2,1)}, u32[]{:S(2)}, u32[]{:S(2)}) collective-permute-start(bf16[256,256]{1,0:T(8,128)(2,1)} %get-tuple-element.49), channel_id=1, source_target_pairs={{0,64},{8,72},{16,80},{24,88},{32,96},{40,104},{48,112},{56,120},{... | collective-permute-start | bytes 393224 | tf_op jit(solution)/shard_map/ppermute | solution.py:32
  47.8 15.4 %collective-permute-start.11 = (bf16[256,256]{1,0:T(8,128)(2,1)}, bf16[256,256]{1,0:T(8,128)(2,1)}, u32[]{:S(2)}, u32[]{:S(2)}) collective-permute-start(bf16[256,256]{1,0:T(8,128)(2,1)} %get-tuple-element.50), channel_id=1, source_target_pairs={{0,128},{8,136},{16,144},{24,152},{32,160},{40,168},{48,176},{56,1... | collective-permute-start | bytes 393224 | tf_op jit(solution)/shard_map/ppermute | solution.py:32
  50.5 1.2 %copy-start.2 = (bf16[2048,256]{1,0:T(8,128)(2,1)S(1)}, bf16[2048,256]{1,0:T(8,128)(2,1)}, u32[]{:S(2)}) copy-start(bf16[2048,256]{1,0:T(8,128)(2,1)} %copy-done.1) | copy-start | bytes 3145732
  51.7 1.0 %copy-start.4 = (bf16[2048,128]{1,0:T(8,128)(2,1)S(1)}, bf16[2048,128]{1,0:T(8,128)(2,1)}, u32[]{:S(2)}) copy-start(bf16[2048,128]{1,0:T(8,128)(2,1)} %copy-done.3) | copy-start | bytes 1572868
  79.0 20.2 %all-to-all-start.1 = ((bf16[8,256,128]{2,1,0:T(8,128)(2,1)}), bf16[8,256,128]{2,1,0:T(8,128)(2,1)S(1)}, u32[]{:S(2)}, u32[]{:S(2)}) async-start(bf16[8,256,128]{2,1,0:T(8,128)(2,1)} %bitcast.18), calls=%async_computation.1 | async-start | bytes 1048576 | tf_op jit(solution)/shard_map/all_to_all | solution.py:322
  82.9 8.7 %collective-permute-start.12 = (bf16[256,256]{1,0:T(8,128)(2,1)}, bf16[256,256]{1,0:T(8,128)(2,1)S(1)}, u32[]{:S(2)}, u32[]{:S(2)}) collective-permute-start(bf16[256,256]{1,0:T(8,128)(2,1)} %get-tuple-element.57), channel_id=1, source_target_pairs={{0,8},{8,0},{16,24},{24,16},{32,40},{40,32},{48,56},{56,48},{64,72... | collective-permute-start | bytes 393224 | tf_op jit(solution)/shard_map/ppermute | solution.py:32
  83.9 13.5 %collective-permute-start.13 = (bf16[256,256]{1,0:T(8,128)(2,1)}, bf16[256,256]{1,0:T(8,128)(2,1)S(1)}, u32[]{:S(2)}, u32[]{:S(2)}) collective-permute-start(bf16[256,256]{1,0:T(8,128)(2,1)} %get-tuple-element.58), channel_id=1, source_target_pairs={{0,16},{8,24},{16,0},{24,8},{32,48},{40,56},{48,32},{56,40},{64,80... | collective-permute-start | bytes 393224 | tf_op jit(solution)/shard_map/ppermute | solution.py:32
  85.4 12.0 %collective-permute-start.14 = (bf16[256,256]{1,0:T(8,128)(2,1)}, bf16[256,256]{1,0:T(8,128)(2,1)S(1)}, u32[]{:S(2)}, u32[]{:S(2)}) collective-permute-start(bf16[256,256]{1,0:T(8,128)(2,1)} %get-tuple-element.59), channel_id=1, source_target_pairs={{0,32},{8,40},{16,48},{24,56},{32,0},{40,8},{48,16},{56,24},{64,96... | collective-permute-start | bytes 393224 | tf_op jit(solution)/shard_map/ppermute | solution.py:32
  85.4 12.0 %collective-permute-start.15 = (bf16[256,256]{1,0:T(8,128)(2,1)}, bf16[256,256]{1,0:T(8,128)(2,1)S(1)}, u32[]{:S(2)}, u32[]{:S(2)}) collective-permute-start(bf16[256,256]{1,0:T(8,128)(2,1)} %get-tuple-element.60), channel_id=1, source_target_pairs={{0,64},{8,72},{16,80},{24,88},{32,96},{40,104},{48,112},{56,120},{... | collective-permute-start | bytes 393224 | tf_op jit(solution)/shard_map/ppermute | solution.py:32
  85.6 11.8 %collective-permute-start.16 = (bf16[256,256]{1,0:T(8,128)(2,1)}, bf16[256,256]{1,0:T(8,128)(2,1)S(1)}, u32[]{:S(2)}, u32[]{:S(2)}) collective-permute-start(bf16[256,256]{1,0:T(8,128)(2,1)} %get-tuple-element.61), channel_id=1, source_target_pairs={{0,128},{8,136},{16,144},{24,152},{32,160},{40,168},{48,176},{56,1... | collective-permute-start | bytes 393224 | tf_op jit(solution)/shard_map/ppermute | solution.py:32

commit v2 on v1

--- a/solution.py
+++ b/solution.py
@@ -16,6 +16,7 @@
 OWN = NBLK * BLK
 PART = SEND * BLK
 FILL = -1e30
+CHUNKS = 8
 HEAD_DEVICES = 8
 OFFSETS = ((1, 0), (3, 0), (1, 1), (3, 1), (2, 0), (2, 1), (0, 1), (0, 0))
 F32 = jnp.float32
@@ -82,34 +83,36 @@
     )(pltpu.with_memory_space_constraint(keys, pltpu.HBM), pltpu.with_memory_space_constraint(values, pltpu.HBM))
 
 
-def pick_kernel(sends_ref, grad_ref, *refs):
+def pick_kernel(sends_ref, *refs):
     parts, refs = refs[:HEAD_DEVICES], refs[HEAD_DEVICES:]
-    own_ref, near_ref, out_refs, sem = refs[0], refs[1], refs[2:-1], refs[-1]
-    copy = pltpu.make_async_copy(grad_ref, near_ref, sem)
-    copy.start()
+    own_ref, out_refs, held_ref, sems = refs[0], refs[1 : 1 + LEVELS], refs[-2], refs[-1]
     me = lax.axis_index("head")
     mine = OWN // HEAD_DEVICES
+    copies = []
     for t, (steps, core) in enumerate(OFFSETS):
         source = offset_index(me, HEAD_DEVICES // 2 - steps, core)
-        own_ref[pl.ds(pl.multiple_of(source * mine, mine), mine), :] = parts[t][...]
+        at = pl.ds(pl.multiple_of(source * mine, mine), mine)
+        copies.append(pltpu.make_async_copy(parts[t], own_ref.at[at, :], sems.at[t]))
+        copies[-1].start()
+        held_ref[at, :] = parts[t][...]
     for b in range(LEVELS):
         for s in range(SEND):
-            out_refs[b][s * BLK : (s + 1) * BLK, :] = own_ref[rows_of(sends_ref[b, s]), :]
-    copy.wait()
-
-
-def pick(sends, parts, grad):
+            out_refs[b][s * BLK : (s + 1) * BLK, :] = held_ref[rows_of(sends_ref[b, s]), :]
+    for copy in copies:
+        copy.wait()
+
+
+def pick(sends, parts):
     return pl.pallas_call(
         pick_kernel,
-        out_shape=[pltpu.VMEM((OWN, 2 * WIDE), BF16), pltpu.VMEM((OWN, WIDE), BF16)]
-        + [pltpu.VMEM((PART, 2 * WIDE), BF16)] * LEVELS,
-        in_specs=[SM, HB] + [VM] * HEAD_DEVICES,
-        out_specs=[VM] * (2 + LEVELS),
-        scratch_shapes=[pltpu.SemaphoreType.DMA],
+        out_shape=[pltpu.HBM((OWN, 2 * WIDE), BF16)] + [pltpu.VMEM((PART, 2 * WIDE), BF16)] * LEVELS,
+        in_specs=[SM] + [VM] * HEAD_DEVICES,
+        out_specs=[HB] + [VM] * LEVELS,
+        scratch_shapes=[pltpu.VMEM((OWN, 2 * WIDE), BF16), pltpu.SemaphoreType.DMA((HEAD_DEVICES,))],
         compiler_params=limits(8),
         cost_estimate=pl.CostEstimate(flops=0, bytes_accessed=4 * 2**20, transcendentals=0),
         name="pick_boundary",
-    )(sends, pltpu.with_memory_space_constraint(grad, pltpu.HBM), *parts)
+    )(sends, *parts)
 
 
 def pixel_grads(i, live, kv, q_ref, g_ref, att_ref, qg_ref, outs):
@@ -161,8 +164,15 @@
     ]
 
 
-def inner_kernel(unroll, rows_ref, counts_ref, q_ref, g_ref, own_ref, att_ref, qg_ref, acc_ref, *refs):
-    list_ref, staged, sems = refs[0], refs[1:3], refs[3]
+def inner_kernel(unroll, rows_ref, counts_ref, q_ref, far_g_ref, far_own_ref, *refs):
+    att_ref, qg_ref, acc_ref, own_ref, g_ref, list_ref = refs[:6]
+    staged, sems, in_sems = refs[6:8], refs[8], refs[9]
+    loads = []
+    for n, (x, y) in enumerate(((far_own_ref, own_ref), (far_g_ref, g_ref))):
+        for c in range(CHUNKS):
+            part = pl.ds(c * (OWN // CHUNKS), OWN // CHUNKS)
+            loads.append(pltpu.make_async_copy(x.at[part, :], y.at[part, :], in_sems.at[n, c]))
+            loads[-1].start()
     outs = lambda i: row_copies(i, staged, (att_ref, qg_ref), sems)
     steps = NBLK - LEVELS * SEND
     acc_ref[...] = jnp.zeros_like(acc_ref)
@@ -172,6 +182,8 @@
         return count + (rows_ref[i, 1] < NBLK).astype(jnp.int32)
 
     lax.fori_loop(0, NBLK, note, jnp.int32(0))
+    for load in loads:
+        load.wait()
 
     def step(t, carry):
         for u in range(unroll):
@@ -200,16 +212,18 @@
             pltpu.HBM((OWN, WIDE), BF16),
             pltpu.HBM((OWN, WIDE), BF16),
             pltpu.VMEM((OWN, 2 * WIDE), F32),
+            pltpu.VMEM((OWN, 2 * WIDE), BF16),
+            pltpu.VMEM((OWN, WIDE), BF16),
         ],
-        in_specs=[SM, SM] + [VM] * 3,
-        out_specs=[HB, HB, VM],
+        in_specs=[SM, SM, VM, HB, HB],
+        out_specs=[HB, HB, VM, VM, VM],
         scratch_shapes=[pltpu.SMEM((NBLK + 1,), jnp.int32)]
         + [pltpu.VMEM((OWN, WIDE), BF16)] * 2
-        + [pltpu.SemaphoreType.DMA((2, NBLK))],
+        + [pltpu.SemaphoreType.DMA((2, NBLK)), pltpu.SemaphoreType.DMA((2, CHUNKS))],
         compiler_params=limits(16),
         cost_estimate=pl.CostEstimate(flops=4 * 10**9, bytes_accessed=8 * 2**20, transcendentals=10**6),
         name="attend_inner",
-    )(rows, counts, q, g, own)
+    )(rows, counts, q, *(pltpu.with_memory_space_constraint(x, pltpu.HBM) for x in (g, own)))
 
 
 def outer_kernel(unroll, sends_ref, rows_ref, counts_ref, q_ref, g_ref, own_ref, *refs):
@@ -312,11 +326,11 @@
     parts = split(key_rows, value_rows)
     parts = [shifted(x, *o) if o != (0, 0) else x for x, o in zip(parts, OFFSETS)]
     q = query_rows.reshape(mine, heads, WIDE).transpose(1, 0, 2)
-    q, parts[0] = lax.optimization_barrier((q, parts[0]))
+    own, *outgoing = pick(sends, parts)
+    q, own = lax.optimization_barrier((q, own))
     q = lax.all_to_all(q, "head", 0, 0, tiled=True).reshape(OWN, WIDE)
-    own, grad, *outgoing = pick(sends, parts, out_grad)
     recv = [swapped(outgoing[b], b) for b in range(LEVELS)]
-    done = inner(rows, counts, q, grad, own)
+    *done, own, grad = inner(rows, counts, q, out_grad, own)
     attended, query_grad, acc, *back = outer(sends, rows, counts, q, grad, own, recv, done)
     arrived = [swapped(back[b], b) for b in range(LEVELS)]
     attended = lax.all_to_all(attended.reshape(heads, mine, WIDE), "head", 0, 0, tiled=True)

time: 101 us -> 91 us (0.901)
  waiting for transfers between devices: 24.3 us -> 14.3 us
  local copies, waits for them, and re-layouts: 7.71 us -> 4.37 us
  starting transfers between devices: 35.4 us -> 37.8 us
  Pallas kernels: 32 us -> 33.3 us
    ppermute x7, waiting for transfers between devices: 14.3 us -> 5.75 us  [shifted(): return lax.ppermute(block, 'head', route)]
    unnamed x13 -> x3, local copies, waits for them, and re-layouts: 4.13 us -> 0.1 us
    ppermute x10, starting transfers between devices: 17.1 us -> 19.8 us  [swapped(): return lax.ppermute(block, 'pix', route)]
    all_to_all x1, starting transfers between devices: 6.53 us -> 4.68 us  [body(): q = lax.all_to_all(q, 'head', 0, 0, tiled=True).reshape(OWN, WIDE)]
    ppermute x10, waiting for transfers between devices: 9.98 us -> 8.58 us  [swapped(): return lax.ppermute(block, 'pix', route)]
    pallas_call x1, Pallas kernels: 10.4 us -> 11.6 us  [inner(): pl.pallas_call(functools.partial(inner_kernel, 2), out_shape=[pltpu.HBM((...]
  transfers between devices with their start and end apart: 19 -> 19, of which waited for: 6 -> 4; matrix products, arithmetic and copies ran while one was open for 3% -> 4% of each run, Pallas kernels for 15% -> 15%
where the time goes in v2:
time: 91 us; the launch traced here: 90.5 us
  starting transfers between devices  37.8 us (42%)
  Pallas kernels  33.3 us (37%)
  waiting for transfers between devices  14.3 us (16%)
  local copies, waits for them, and re-layouts  4.37 us (5%)
    ppermute x10, starting transfers between devices, swapped(): return lax.ppermute(block, 'pix', route)  19.8 us
    pallas_call x1, Pallas kernels, outer(): pl.pallas_call(functools.partial(outer_kernel, 2), out_shape=[pltpu.HBM((...  16 us
    pallas_call x1, Pallas kernels, inner(): pl.pallas_call(functools.partial(inner_kernel, 2), out_shape=[pltpu.HBM((...  11.6 us
    ppermute x10, waiting for transfers between devices, swapped(): return lax.ppermute(block, 'pix', route)  8.58 us
    ppermute x7, starting transfers between devices, shifted(): return lax.ppermute(block, 'head', route)  8.48 us
    ppermute x7, waiting for transfers between devices, shifted(): return lax.ppermute(block, 'head', route)  5.75 us
    all_to_all x1, starting transfers between devices, body(): lax.all_to_all(attended.reshape(heads, mine, WIDE), 'head', 0, 0, tiled=T...  4.81 us
    all_to_all x1, starting transfers between devices, body(): q = lax.all_to_all(q, 'head', 0, 0, tiled=True).reshape(OWN, WIDE)  4.68 us
  transfers between devices with their start and end apart: 19, of which 4 were waited for; matrix products, arithmetic and copies ran while one was open for 4% of the time, Pallas kernels for 15%

profile of v2, /device:TPU:8, one launch (start us, length us, event | category | flops | bytes accessed | tf_op | source)
XLA Modules:
  0.0 90.5 jit_solution(16083627534494763762)
XLA Ops:
  0.6 0.0 copy-start
  0.6 1.5 %split_keys_values.1 = (bf16[256,256]{1,0:T(8,128)(2,1)S(1)}, bf16[256,256]{1,0:T(8,128)(2,1)S(1)}, bf16[256,256]{1,0:T(8,128)(2,1)S(1)}, bf16[256,256]{1,0:T(8,...) custom-call(bf16[256,1024]{1,0:T(8,128)(2,1)} %key_ref.1, ...), custom_call_target="tpu_custom_call" | custom-call | bytes 2097152 | tf_op jit(solution)/shard_map/split_keys_values/pallas_call | solution.py:74
  2.1 1.7 %collective-permute-start = (bf16[256,256]{1,0:T(8,128)(2,1)S(1)}, bf16[256,256]{1,0:T(8,128)(2,1)S(1)}, u32[]{:S(2)}, u32[]{:S(2)}) collective-permute-start(bf16[256,256]{1,0:T(8,128)(2,1)S(1)} %get-tuple-element.35), channel_id=1, source_target_pairs={{0,2},{1,3},{2,4},{3,5},{4,6},{5,7},{6,0},{7,1},{8,10},{9,11},{10,... | collective-permute-start | bytes 393224 | tf_op jit(solution)/shard_map/ppermute | solution.py:47
  3.8 0.7 collective-permute-start.1
  4.5 0.2 collective-permute-start.2
  4.7 1.5 %collective-permute-start.3 = (bf16[256,256]{1,0:T(8,128)(2,1)S(1)}, bf16[256,256]{1,0:T(8,128)(2,1)S(1)}, u32[]{:S(2)}, u32[]{:S(2)}) collective-permute-start(bf16[256,256]{1,0:T(8,128)(2,1)S(1)} %get-tuple-element.38), channel_id=1, source_target_pairs={{0,7},{1,6},{2,1},{3,0},{4,3},{5,2},{6,5},{7,4},{8,15},{9,14},{10,... | collective-permute-start | bytes 393224 | tf_op jit(solution)/shard_map/ppermute | solution.py:47
  6.2 2.0 %collective-permute-start.4 = (bf16[256,256]{1,0:T(8,128)(2,1)S(1)}, bf16[256,256]{1,0:T(8,128)(2,1)S(1)}, u32[]{:S(2)}, u32[]{:S(2)}) collective-permute-start(bf16[256,256]{1,0:T(8,128)(2,1)S(1)} %get-tuple-element.39), channel_id=1, source_target_pairs={{0,4},{1,5},{2,6},{3,7},{4,0},{5,1},{6,2},{7,3},{8,12},{9,13},{10,... | collective-permute-start | bytes 393224 | tf_op jit(solution)/shard_map/ppermute | solution.py:47
  8.3 0.8 constant_dynamic-slice_fusion.1
  9.1 0.1 copy.14
  9.2 0.1 copy.18.sends_ref
  9.3 0.0 collective-permute-done.refs_0_
  9.3 2.3 %collective-permute-start.5 = (bf16[256,256]{1,0:T(8,128)(2,1)S(1)}, bf16[256,256]{1,0:T(8,128)(2,1)S(1)}, u32[]{:S(2)}, u32[]{:S(2)}) collective-permute-start(bf16[256,256]{1,0:T(8,128)(2,1)S(1)} %get-tuple-element.40), channel_id=1, source_target_pairs={{0,5},{1,4},{2,7},{3,6},{4,1},{5,0},{6,3},{7,2},{8,13},{9,12},{10,... | collective-permute-start | bytes 393224 | tf_op jit(solution)/shard_map/ppermute | solution.py:47
  11.6 0.0 collective-permute-done.1.refs_1_
  11.6 0.0 collective-permute-start.6
  11.6 0.0 copy-done
  11.6 0.9 bitcast_bitcast_fusion
  12.5 0.0 collective-permute-done.2.refs_2_
  12.5 0.0 collective-permute-done.3.refs_3_
  12.5 2.1 %collective-permute-done.4.refs_4_ = bf16[256,256]{1,0:T(8,128)(2,1)S(1)} collective-permute-done((bf16[256,256]{1,0:T(8,128)(2,1)S(1)}, bf16[256,256]{1,0:T(8,128)(2,1)S(1)}, u32[]{:S(2)}, u32[]{:S(2)}) %collective-permute-start.4) | collective-permute-done | bytes 131104 | tf_op jit(solution)/shard_map/ppermute | solution.py:47
  14.6 3.6 %collective-permute-done.5.refs_5_ = bf16[256,256]{1,0:T(8,128)(2,1)S(1)} collective-permute-done((bf16[256,256]{1,0:T(8,128)(2,1)S(1)}, bf16[256,256]{1,0:T(8,128)(2,1)S(1)}, u32[]{:S(2)}, u32[]{:S(2)}) %collective-permute-start.5) | collective-permute-done | bytes 131104 | tf_op jit(solution)/shard_map/ppermute | solution.py:47
  18.2 0.0 collective-permute-done.6.refs_6_
  18.2 2.4 %pick_boundary.1 = (bf16[2048,256]{1,0:T(8,128)(2,1)}, bf16[256,256]{1,0:T(8,128)(2,1)}, bf16[256,256]{1,0:T(8,128)(2,1)}, bf16[256,256]{1,0:T(8,128)(2,1)}, bf1...) custom-call(s32[5,4]{1,0:T(8,128)S(1)} %copy.18.sends_ref, bf16[256,256]{1,0:T(8,128)(2,1)S(1)} %collective-permute-done.refs_0_, ...), custom_call_target="tpu_custom_call" | custom-call | bytes 4194304 | tf_op jit(solution)/shard_map/pick_boundary/pallas_call | solution.py:106
  20.7 4.7 %all-to-all-start = ((bf16[8,256,128]{2,1,0:T(8,128)(2,1)}), bf16[8,256,128]{2,1,0:T(8,128)(2,1)S(1)}, u32[]{:S(2)}, u32[]{:S(2)}) async-start(bf16[8,256,128]{2,1,0:T(8,128)(2,1)} %bitcast_bitcast_fusion), calls=%async_computation | async-start | bytes 1048576 | tf_op jit(solution)/shard_map/all_to_all | solution.py:331
  25.4 0.8 dynamic_slice.12.counts_ref
  26.1 0.8 constant_dynamic-slice_fusion
  26.9 0.1 copy.21.rows_ref
  27.0 0.5 collective-permute-start.7
  27.5 3.3 %collective-permute-start.8 = (bf16[256,256]{1,0:T(8,128)(2,1)}, bf16[256,256]{1,0:T(8,128)(2,1)}, u32[]{:S(2)}, u32[]{:S(2)}) collective-permute-start(bf16[256,256]{1,0:T(8,128)(2,1)} %get-tuple-element.49), channel_id=1, source_target_pairs={{0,16},{8,24},{16,0},{24,8},{32,48},{40,56},{48,32},{56,40},{64,80... | collective-permute-start | bytes 393224 | tf_op jit(solution)/shard_map/ppermute | solution.py:33
  30.8 4.5 %collective-permute-start.9 = (bf16[256,256]{1,0:T(8,128)(2,1)}, bf16[256,256]{1,0:T(8,128)(2,1)}, u32[]{:S(2)}, u32[]{:S(2)}) collective-permute-start(bf16[256,256]{1,0:T(8,128)(2,1)} %get-tuple-element.50), channel_id=1, source_target_pairs={{0,32},{8,40},{16,48},{24,56},{32,0},{40,8},{48,16},{56,24},{64,96... | collective-permute-start | bytes 393224 | tf_op jit(solution)/shard_map/ppermute | solution.py:33
  35.3 1.5 %collective-permute-start.10 = (bf16[256,256]{1,0:T(8,128)(2,1)S(1)}, bf16[256,256]{1,0:T(8,128)(2,1)}, u32[]{:S(2)}, u32[]{:S(2)}) collective-permute-start(bf16[256,256]{1,0:T(8,128)(2,1)S(1)} %get-tuple-element.51), channel_id=1, source_target_pairs={{0,64},{8,72},{16,80},{24,88},{32,96},{40,104},{48,112},{56,120},{... | collective-permute-start | bytes 393224 | tf_op jit(solution)/shard_map/ppermute | solution.py:33
  36.8 2.8 %collective-permute-start.11 = (bf16[256,256]{1,0:T(8,128)(2,1)S(1)}, bf16[256,256]{1,0:T(8,128)(2,1)}, u32[]{:S(2)}, u32[]{:S(2)}) collective-permute-start(bf16[256,256]{1,0:T(8,128)(2,1)S(1)} %get-tuple-element.52), channel_id=1, source_target_pairs={{0,128},{8,136},{16,144},{24,152},{32,160},{40,168},{48,176},{56,1... | collective-permute-start | bytes 393224 | tf_op jit(solution)/shard_map/ppermute | solution.py:33
  39.5 0.0 all-to-all-done
  39.5 11.6 %attend_inner.1 = (bf16[2048,128]{1,0:T(8,128)(2,1)}, bf16[2048,128]{1,0:T(8,128)(2,1)}, f32[2048,256]{1,0:T(8,128)S(1)}, bf16[2048,256]{1,0:T(8,128)(2,1)S(1)}, bf16[2048,128]{1,0:T(8,128)(2,1)S(1)}) custom-call(s32[32,9]{1,0:T(8,128)S(1)} %copy.21.rows_ref, s32[32]{0:T(128)S(1)} %dynamic_slice.12.counts_ref, bf16[2048,128]{1,0:T(8,128)(2,1)S(1)} %bitcast.16, ...), custom_call_target="tpu_custom_call" | custom-call | flops 4000000000 | bytes 8388608 | tf_op jit(solution)/shard_map/attend_inner/pallas_call | solution.py:209
  51.1 0.0 collective-permute-done.7.refs_0_
  51.1 0.0 collective-permute-done.8.refs_1_
  51.2 0.0 collective-permute-done.9.refs_2_
  51.2 0.0 collective-permute-done.10.refs_3_
  51.2 0.0 collective-permute-done.11.refs_4_
  51.2 16.0 %attend_outer.1 = (bf16[2048,128]{1,0:T(8,128)(2,1)}, bf16[2048,128]{1,0:T(8,128)(2,1)}, f32[2048,256]{1,0:T(8,128)S(1)}, bf16[256,256]{1,0:T(8,128)(2,1)}, bf16...) custom-call(s32[5,4]{1,0:T(8,128)S(1)} %copy.18.sends_ref, ...), custom_call_target="tpu_custom_call", output_to_operand_aliasing={{0}: (11, {}), {1}: (12, {}), {2}: (13, {})} | custom-call | flops 8000000000 | bytes 8388608 | tf_op jit(solution)/shard_map/attend_outer/pallas_call | solution.py:273
  67.1 4.8 %all-to-all-start.1 = ((bf16[8,256,128]{2,1,0:T(8,128)(2,1)}), bf16[8,256,128]{2,1,0:T(8,128)(2,1)S(1)}, u32[]{:S(2)}, u32[]{:S(2)}) async-start(bf16[8,256,128]{2,1,0:T(8,128)(2,1)} %bitcast.18), calls=%async_computation.1 | async-start | bytes 1048576 | tf_op jit(solution)/shard_map/all_to_all | solution.py:336
  72.0 1.0 %collective-permute-start.12 = (bf16[256,256]{1,0:T(8,128)(2,1)}, bf16[256,256]{1,0:T(8,128)(2,1)S(1)}, u32[]{:S(2)}, u32[]{:S(2)}) collective-permute-start(bf16[256,256]{1,0:T(8,128)(2,1)} %get-tuple-element.59), channel_id=1, source_target_pairs={{0,8},{8,0},{16,24},{24,16},{32,40},{40,32},{48,56},{56,48},{64,72... | collective-permute-start | bytes 393224 | tf_op jit(solution)/shard_map/ppermute | solution.py:33
  73.0 1.5 %collective-permute-start.13 = (bf16[256,256]{1,0:T(8,128)(2,1)}, bf16[256,256]{1,0:T(8,128)(2,1)S(1)}, u32[]{:S(2)}, u32[]{:S(2)}) collective-permute-start(bf16[256,256]{1,0:T(8,128)(2,1)} %get-tuple-element.60), channel_id=1, source_target_pairs={{0,16},{8,24},{16,0},{24,8},{32,48},{40,56},{48,32},{56,40},{64,80... | collective-permute-start | bytes 393224 | tf_op jit(solution)/shard_map/ppermute | solution.py:33
  74.4 0.6 collective-permute-start.14
  75.0 1.5 %collective-permute-start.15 = (bf16[256,256]{1,0:T(8,128)(2,1)}, bf16[256,256]{1,0:T(8,128)(2,1)S(1)}, u32[]{:S(2)}, u32[]{:S(2)}) collective-permute-start(bf16[256,256]{1,0:T(8,128)(2,1)} %get-tuple-element.62), channel_id=1, source_target_pairs={{0,64},{8,72},{16,80},{24,88},{32,96},{40,104},{48,112},{56,120},{... | collective-permute-start | bytes 393224 | tf_op jit(solution)/shard_map/ppermute | solution.py:33
  76.5 2.7 %collective-permute-start.16 = (bf16[256,256]{1,0:T(8,128)(2,1)}, bf16[256,256]{1,0:T(8,128)(2,1)S(1)}, u32[]{:S(2)}, u32[]{:S(2)}) collective-permute-start(bf16[256,256]{1,0:T(8,128)(2,1)} %get-tuple-element.63), channel_id=1, source_target_pairs={{0,128},{8,136},{16,144},{24,152},{32,160},{40,168},{48,176},{56,1... | collective-permute-start | bytes 393224 | tf_op jit(solution)/shard_map/ppermute | solution.py:33
  79.3 1.4 %collective-permute-done.12.refs_0_ = bf16[256,256]{1,0:T(8,128)(2,1)S(1)} collective-permute-done((bf16[256,256]{1,0:T(8,128)(2,1)}, bf16[256,256]{1,0:T(8,128)(2,1)S(1)}, u32[]{:S(2)}, u32[]{:S(2)}) %collective-permute-start.12) | collective-permute-done | bytes 131104 | tf_op jit(solution)/shard_map/ppermute | solution.py:33
  80.6 7.2 %collective-permute-done.13.refs_1_ = bf16[256,256]{1,0:T(8,128)(2,1)S(1)} collective-permute-done((bf16[256,256]{1,0:T(8,128)(2,1)}, bf16[256,256]{1,0:T(8,128)(2,1)S(1)}, u32[]{:S(2)}, u32[]{:S(2)}) %collective-permute-start.13) | collective-permute-done | bytes 131104 | tf_op jit(solution)/shard_map/ppermute | solution.py:33
  87.8 0.0 collective-permute-done.14.refs_2_
  87.8 0.0 collective-permute-done.15.refs_3_
  87.8 0.0 collective-permute-done.16.refs_4_
  87.8 1.8 %join_gradients.1 = (bf16[2048,128]{1,0:T(8,128)(2,1)}, bf16[2048,128]{1,0:T(8,128)(2,1)}) custom-call(s32[5,4]{1,0:T(8,128)S(1)} %copy.18.sends_ref, f32[2048,256]{1,0:T(8,128)S(1)} %get-tuple-element.58.acc_ref, bf16[256,256]{1,0:T(8,128)(2,1)S(1)} %collective-permute-done.12.refs_0_, bf16[256,256]{1,0:T(8,128)(2,1)S(1)} %collective-permute-done.13.refs_1_, ...), custom_call_target="tpu_custom_call" | custom-call | flops 1000000 | bytes 4194304 | tf_op jit(solution)/shard_map/join_gradients/pallas_call | solution.py:307
  89.6 0.0 all-to-all-done.1
  89.6 0.9 copy_bitcast_fusion
Async XLA Ops:
  0.6 11.0 %copy-start = (bf16[256,1024]{1,0:T(8,128)(2,1)S(1)}, bf16[256,1024]{1,0:T(8,128)(2,1)}, u32[]{:S(2)}) copy-start(bf16[256,1024]{1,0:T(8,128)(2,1)} %param.7) | copy-start | bytes 1572868
  2.1 7.1 %collective-permute-start = (bf16[256,256]{1,0:T(8,128)(2,1)S(1)}, bf16[256,256]{1,0:T(8,128)(2,1)S(1)}, u32[]{:S(2)}, u32[]{:S(2)}) collective-permute-start(bf16[256,256]{1,0:T(8,128)(2,1)S(1)} %get-tuple-element.35), channel_id=1, source_target_pairs={{0,2},{1,3},{2,4},{3,5},{4,6},{5,7},{6,0},{7,1},{8,10},{9,11},{10,... | collective-permute-start | bytes 393224 | tf_op jit(solution)/shard_map/ppermute | solution.py:47
  3.8 7.8 %collective-permute-start.1 = (bf16[256,256]{1,0:T(8,128)(2,1)S(1)}, bf16[256,256]{1,0:T(8,128)(2,1)S(1)}, u32[]{:S(2)}, u32[]{:S(2)}) collective-permute-start(bf16[256,256]{1,0:T(8,128)(2,1)S(1)} %get-tuple-element.36), channel_id=1, source_target_pairs={{0,6},{1,7},{2,0},{3,1},{4,2},{5,3},{6,4},{7,5},{8,14},{9,15},{10,... | collective-permute-start | bytes 393224 | tf_op jit(solution)/shard_map/ppermute | solution.py:47
  4.5 8.0 %collective-permute-start.2 = (bf16[256,256]{1,0:T(8,128)(2,1)S(1)}, bf16[256,256]{1,0:T(8,128)(2,1)S(1)}, u32[]{:S(2)}, u32[]{:S(2)}) collective-permute-start(bf16[256,256]{1,0:T(8,128)(2,1)S(1)} %get-tuple-element.37), channel_id=1, source_target_pairs={{0,3},{1,2},{2,5},{3,4},{4,7},{5,6},{6,1},{7,0},{8,11},{9,10},{10,... | collective-permute-start | bytes 393224 | tf_op jit(solution)/shard_map/ppermute | solution.py:47
  4.7 7.8 %collective-permute-start.3 = (bf16[256,256]{1,0:T(8,128)(2,1)S(1)}, bf16[256,256]{1,0:T(8,128)(2,1)S(1)}, u32[]{:S(2)}, u32[]{:S(2)}) collective-permute-start(bf16[256,256]{1,0:T(8,128)(2,1)S(1)} %get-tuple-element.38), channel_id=1, source_target_pairs={{0,7},{1,6},{2,1},{3,0},{4,3},{5,2},{6,5},{7,4},{8,15},{9,14},{10,... | collective-permute-start | bytes 393224 | tf_op jit(solution)/shard_map/ppermute | solution.py:47
  6.2 8.4 %collective-permute-start.4 = (bf16[256,256]{1,0:T(8,128)(2,1)S(1)}, bf16[256,256]{1,0:T(8,128)(2,1)S(1)}, u32[]{:S(2)}, u32[]{:S(2)}) collective-permute-start(bf16[256,256]{1,0:T(8,128)(2,1)S(1)} %get-tuple-element.39), channel_id=1, source_target_pairs={{0,4},{1,5},{2,6},{3,7},{4,0},{5,1},{6,2},{7,3},{8,12},{9,13},{10,... | collective-permute-start | bytes 393224 | tf_op jit(solution)/shard_map/ppermute | solution.py:47
  9.3 9.0 %collective-permute-start.5 = (bf16[256,256]{1,0:T(8,128)(2,1)S(1)}, bf16[256,256]{1,0:T(8,128)(2,1)S(1)}, u32[]{:S(2)}, u32[]{:S(2)}) collective-permute-start(bf16[256,256]{1,0:T(8,128)(2,1)S(1)} %get-tuple-element.40), channel_id=1, source_target_pairs={{0,5},{1,4},{2,7},{3,6},{4,1},{5,0},{6,3},{7,2},{8,13},{9,12},{10,... | collective-permute-start | bytes 393224 | tf_op jit(solution)/shard_map/ppermute | solution.py:47
  11.6 6.6 %collective-permute-start.6 = (bf16[256,256]{1,0:T(8,128)(2,1)S(1)}, bf16[256,256]{1,0:T(8,128)(2,1)S(1)}, u32[]{:S(2)}, u32[]{:S(2)}) collective-permute-start(bf16[256,256]{1,0:T(8,128)(2,1)S(1)} %get-tuple-element.41), channel_id=1, source_target_pairs={{0,1},{1,0},{2,3},{3,2},{4,5},{5,4},{6,7},{7,6},{8,9},{9,8},{10,11... | collective-permute-start | bytes 393224 | tf_op jit(solution)/shard_map/ppermute | solution.py:47
  20.7 18.8 %all-to-all-start = ((bf16[8,256,128]{2,1,0:T(8,128)(2,1)}), bf16[8,256,128]{2,1,0:T(8,128)(2,1)S(1)}, u32[]{:S(2)}, u32[]{:S(2)}) async-start(bf16[8,256,128]{2,1,0:T(8,128)(2,1)} %bitcast_bitcast_fusion), calls=%async_computation | async-start | bytes 1048576 | tf_op jit(solution)/shard_map/all_to_all | solution.py:331
  27.0 24.1 %collective-permute-start.7 = (bf16[256,256]{1,0:T(8,128)(2,1)}, bf16[256,256]{1,0:T(8,128)(2,1)}, u32[]{:S(2)}, u32[]{:S(2)}) collective-permute-start(bf16[256,256]{1,0:T(8,128)(2,1)} %get-tuple-element.48), channel_id=1, source_target_pairs={{0,8},{8,0},{16,24},{24,16},{32,40},{40,32},{48,56},{56,48},{64,72... | collective-permute-start | bytes 393224 | tf_op jit(solution)/shard_map/ppermute | solution.py:33
  27.5 23.6 %collective-permute-start.8 = (bf16[256,256]{1,0:T(8,128)(2,1)}, bf16[256,256]{1,0:T(8,128)(2,1)}, u32[]{:S(2)}, u32[]{:S(2)}) collective-permute-start(bf16[256,256]{1,0:T(8,128)(2,1)} %get-tuple-element.49), channel_id=1, source_target_pairs={{0,16},{8,24},{16,0},{24,8},{32,48},{40,56},{48,32},{56,40},{64,80... | collective-permute-start | bytes 393224 | tf_op jit(solution)/shard_map/ppermute | solution.py:33
  30.8 20.4 %collective-permute-start.9 = (bf16[256,256]{1,0:T(8,128)(2,1)}, bf16[256,256]{1,0:T(8,128)(2,1)}, u32[]{:S(2)}, u32[]{:S(2)}) collective-permute-start(bf16[256,256]{1,0:T(8,128)(2,1)} %get-tuple-element.50), channel_id=1, source_target_pairs={{0,32},{8,40},{16,48},{24,56},{32,0},{40,8},{48,16},{56,24},{64,96... | collective-permute-start | bytes 393224 | tf_op jit(solution)/shard_map/ppermute | solution.py:33
  35.3 15.9 %collective-permute-start.10 = (bf16[256,256]{1,0:T(8,128)(2,1)S(1)}, bf16[256,256]{1,0:T(8,128)(2,1)}, u32[]{:S(2)}, u32[]{:S(2)}) collective-permute-start(bf16[256,256]{1,0:T(8,128)(2,1)S(1)} %get-tuple-element.51), channel_id=1, source_target_pairs={{0,64},{8,72},{16,80},{24,88},{32,96},{40,104},{48,112},{56,120},{... | collective-permute-start | bytes 393224 | tf_op jit(solution)/shard_map/ppermute | solution.py:33
  36.8 14.4 %collective-permute-start.11 = (bf16[256,256]{1,0:T(8,128)(2,1)S(1)}, bf16[256,256]{1,0:T(8,128)(2,1)}, u32[]{:S(2)}, u32[]{:S(2)}) collective-permute-start(bf16[256,256]{1,0:T(8,128)(2,1)S(1)} %get-tuple-element.52), channel_id=1, source_target_pairs={{0,128},{8,136},{16,144},{24,152},{32,160},{40,168},{48,176},{56,1... | collective-permute-start | bytes 393224 | tf_op jit(solution)/shard_map/ppermute | solution.py:33
  67.1 22.5 %all-to-all-start.1 = ((bf16[8,256,128]{2,1,0:T(8,128)(2,1)}), bf16[8,256,128]{2,1,0:T(8,128)(2,1)S(1)}, u32[]{:S(2)}, u32[]{:S(2)}) async-start(bf16[8,256,128]{2,1,0:T(8,128)(2,1)} %bitcast.18), calls=%async_computation.1 | async-start | bytes 1048576 | tf_op jit(solution)/shard_map/all_to_all | solution.py:336
  72.0 8.7 %collective-permute-start.12 = (bf16[256,256]{1,0:T(8,128)(2,1)}, bf16[256,256]{1,0:T(8,128)(2,1)S(1)}, u32[]{:S(2)}, u32[]{:S(2)}) collective-permute-start(bf16[256,256]{1,0:T(8,128)(2,1)} %get-tuple-element.59), channel_id=1, source_target_pairs={{0,8},{8,0},{16,24},{24,16},{32,40},{40,32},{48,56},{56,48},{64,72... | collective-permute-start | bytes 393224 | tf_op jit(solution)/shard_map/ppermute | solution.py:33
  73.0 14.9 %collective-permute-start.13 = (bf16[256,256]{1,0:T(8,128)(2,1)}, bf16[256,256]{1,0:T(8,128)(2,1)S(1)}, u32[]{:S(2)}, u32[]{:S(2)}) collective-permute-start(bf16[256,256]{1,0:T(8,128)(2,1)} %get-tuple-element.60), channel_id=1, source_target_pairs={{0,16},{8,24},{16,0},{24,8},{32,48},{40,56},{48,32},{56,40},{64,80... | collective-permute-start | bytes 393224 | tf_op jit(solution)/shard_map/ppermute | solution.py:33
  74.4 13.4 %collective-permute-start.14 = (bf16[256,256]{1,0:T(8,128)(2,1)}, bf16[256,256]{1,0:T(8,128)(2,1)S(1)}, u32[]{:S(2)}, u32[]{:S(2)}) collective-permute-start(bf16[256,256]{1,0:T(8,128)(2,1)} %get-tuple-element.61), channel_id=1, source_target_pairs={{0,32},{8,40},{16,48},{24,56},{32,0},{40,8},{48,16},{56,24},{64,96... | collective-permute-start | bytes 393224 | tf_op jit(solution)/shard_map/ppermute | solution.py:33
  75.0 12.8 %collective-permute-start.15 = (bf16[256,256]{1,0:T(8,128)(2,1)}, bf16[256,256]{1,0:T(8,128)(2,1)S(1)}, u32[]{:S(2)}, u32[]{:S(2)}) collective-permute-start(bf16[256,256]{1,0:T(8,128)(2,1)} %get-tuple-element.62), channel_id=1, source_target_pairs={{0,64},{8,72},{16,80},{24,88},{32,96},{40,104},{48,112},{56,120},{... | collective-permute-start | bytes 393224 | tf_op jit(solution)/shard_map/ppermute | solution.py:33
  76.5 11.3 %collective-permute-start.16 = (bf16[256,256]{1,0:T(8,128)(2,1)}, bf16[256,256]{1,0:T(8,128)(2,1)S(1)}, u32[]{:S(2)}, u32[]{:S(2)}) collective-permute-start(bf16[256,256]{1,0:T(8,128)(2,1)} %get-tuple-element.63), channel_id=1, source_target_pairs={{0,128},{8,136},{16,144},{24,152},{32,160},{40,168},{48,176},{56,1... | collective-permute-start | bytes 393224 | tf_op jit(solution)/shard_map/ppermute | solution.py:33

commit v3 on v2

--- a/solution.py
+++ b/solution.py
@@ -115,27 +115,25 @@
     )(sends, *parts)
 
 
-def pixel_grads(i, live, kv, q_ref, g_ref, att_ref, qg_ref, outs):
-    at = rows_of(i)
-    q = q_ref[at, :] * jnp.array(HD**-0.5, BF16)
-    g = g_ref[at, :]
+def staged_block(i, live, at, far, q_ref, g_ref, own_ref, acc_ref, staged, outs):
+    rows = rows_of(i)
+    q = q_ref[rows, :] * jnp.array(HD**-0.5, BF16)
+    g = g_ref[rows, :]
     low = lax.broadcasted_iota(jnp.int32, (BLK, WIDE), 1) < HD
     z = jnp.zeros((BLK, WIDE), BF16)
-    both = jnp.concatenate(
-        [
-            jnp.concatenate([jnp.where(low, q, z), z], 1),
-            jnp.concatenate([jnp.where(low, z, q), z], 1),
-            jnp.concatenate([z, jnp.where(low, g, z)], 1),
-            jnp.concatenate([z, jnp.where(low, z, g)], 1),
-        ],
-        0,
-    )
-    sd = lax.dot_general(kv, both, (((1,), (1,)), ((), ())), preferred_element_type=F32)
-    s = [sd[j * BLK : (j + 1) * BLK, :WIDE] for j in range(NNB)]
-    d = [sd[j * BLK : (j + 1) * BLK, WIDE:] for j in range(NNB)]
+    q = jnp.concatenate([jnp.where(low, q, z), jnp.where(low, z, q)], 0)
+    g = jnp.concatenate([jnp.where(low, g, z), jnp.where(low, z, g)], 0)
+    blocks = [own_ref[a, :] if a is not None else far[0][...] for a in at]
+    kv = jnp.concatenate(blocks, 0)
+    product = functools.partial(lax.dot_general, preferred_element_type=F32)
+    across, plain, down = (((1,), (1,)), ((), ())), (((1,), (0,)), ((), ())), (((0,), (0,)), ((), ()))
+    s = product(kv[:, :WIDE], q, across)
+    d = product(kv[:, WIDE:], g, across)
+    yield
+    s = [s[j * BLK : (j + 1) * BLK] for j in range(NNB)]
+    d = [d[j * BLK : (j + 1) * BLK] for j in range(NNB)]
     s[-1] = jnp.where(live, s[-1], FILL)
-    peak = functools.reduce(jnp.maximum, s)
-    peak = jnp.max(peak, 0, keepdims=True)
+    peak = jnp.max(functools.reduce(jnp.maximum, s), 0, keepdims=True)
     p = [jnp.exp(x - peak) for x in s]
     total = jnp.sum(sum(p[1:], p[0]), 0, keepdims=True)
     dot = [x * y for x, y in zip(p, d)]
@@ -144,17 +142,30 @@
     weights = [x * inv for x in p]
     rounded = jnp.concatenate([x.astype(BF16) for x in weights], 0)
     grads = jnp.concatenate([(x * (y - dot)).astype(BF16) for x, y in zip(weights, d)], 0)
-    terms = lax.dot_general(
-        jnp.concatenate([grads, rounded], 1), both, (((1,), (0,)), ((), ())), preferred_element_type=F32
-    )
-    down = (((0,), (0,)), ((), ()))
-    qg = lax.dot_general(grads, kv[:, :WIDE], down, preferred_element_type=F32)
-    att = lax.dot_general(rounded, kv[:, WIDE:], down, preferred_element_type=F32)
-    att_ref[at, :] = jnp.where(low, att[:BLK], att[BLK:]).astype(BF16)
-    qg_ref[at, :] = (jnp.where(low, qg[:BLK], qg[BLK:]) * HD**-0.5).astype(BF16)
+    yield
+    terms = jnp.concatenate([product(grads, q, plain), product(rounded, g, plain)], 1)
+    for j in range(NNB):
+        term = terms[j * BLK : (j + 1) * BLK]
+        if at[j] is None:
+            far[1][...] = term.astype(BF16)
+        else:
+            acc_ref[at[j], :] += term
+    yield
+    results = product(jnp.concatenate([grads, rounded], 1), kv, down)
+    qg, att = results[:WIDE, :WIDE], results[WIDE:, WIDE:]
+    staged[0][rows, :] = jnp.where(low, att[:BLK], att[BLK:]).astype(BF16)
+    staged[1][rows, :] = (jnp.where(low, qg[:BLK], qg[BLK:]) * HD**-0.5).astype(BF16)
     for copy in outs(i):
         copy.start()
-    return [terms[j * BLK : (j + 1) * BLK] for j in range(NNB)]
+    yield
+
+
+def run_staged(blocks):
+    stages = 4
+    for t in range(len(blocks) + stages - 1):
+        for k in reversed(range(stages)):
+            if 0 <= t - k < len(blocks):
+                next(blocks[t - k])
 
 
 def row_copies(at, staged, outs, sems):
@@ -186,13 +197,13 @@
         load.wait()
 
     def step(t, carry):
+        blocks = []
         for u in range(unroll):
             i = list_ref[t * unroll + u]
             at = [rows_of(rows_ref[i, j]) for j in range(NNB)]
-            kv = jnp.concatenate([own_ref[a, :] for a in at], 0)
-            terms = pixel_grads(i, counts_ref[i] > NNB - 1, kv, q_ref, g_ref, *staged, outs)
-            for j in range(NNB):
-                acc_ref[at[j], :] += terms[j]
+            live = counts_ref[i] > NNB - 1
+            blocks.append(staged_block(i, live, at, None, q_ref, g_ref, own_ref, acc_ref, staged, outs))
+        run_staged(blocks)
         return carry
 
     lax.fori_loop(0, steps // unroll, step, 0)
@@ -207,7 +218,7 @@
 
 def inner(rows, counts, q, g, own):
     return pl.pallas_call(
-        functools.partial(inner_kernel, 2),
+        functools.partial(inner_kernel, 12),
         out_shape=[
             pltpu.HBM((OWN, WIDE), BF16),
             pltpu.HBM((OWN, WIDE), BF16),
@@ -240,20 +251,17 @@
         far_ref[b * PART : (b + 1) * PART, :] = recv_refs[b][...]
 
     def step(t, carry):
+        blocks = []
         for u in range(unroll):
             e = t * unroll + u
             i = sends_ref[e // SEND, e % SEND]
             at = [rows_of(rows_ref[i, j]) if j != 1 else None for j in range(NNB)]
-            far = rows_of(e)
-            kv = jnp.concatenate([own_ref[a, :] if a is not None else far_ref[far, :] for a in at], 0)
-            terms = pixel_grads(i, counts_ref[i] > NNB - 1, kv, q_ref, g_ref, *staged, outs)
-            for j in range(NNB):
-                if j == 1:
-                    back_ref[far, :] = terms[j].astype(BF16)
-                else:
-                    acc_ref[at[j], :] += terms[j]
+            far = (far_ref.at[rows_of(e), :], back_ref.at[rows_of(e), :])
+            live = counts_ref[i] > NNB - 1
+            blocks.append(staged_block(i, live, at, far, q_ref, g_ref, own_ref, acc_ref, staged, outs))
+        run_staged(blocks)
         for b in range(LEVELS):
-            pl.when(t == (b + 1) * SEND // unroll - 1)(backs[b].start)
+            pl.when(t == ((b + 1) * SEND - 1) // unroll)(backs[b].start)
         return carry
 
     lax.fori_loop(0, LEVELS * SEND // unroll, step, 0)
@@ -271,7 +279,7 @@
 def outer(sends, rows, counts, q, g, own, recv, done):
     far = (LEVELS * PART, 2 * WIDE)
     return pl.pallas_call(
-        functools.partial(outer_kernel, 2),
+        functools.partial(outer_kernel, 10),
         out_shape=[
             pltpu.HBM((OWN, WIDE), BF16),
             pltpu.HBM((OWN, WIDE), BF16),
@@ -326,6 +334,7 @@
     parts = split(key_rows, value_rows)
     parts = [shifted(x, *o) if o != (0, 0) else x for x, o in zip(parts, OFFSETS)]
     q = query_rows.reshape(mine, heads, WIDE).transpose(1, 0, 2)
+    parts[0], rows, counts = lax.optimization_barrier((parts[0], rows, counts))
     own, *outgoing = pick(sends, parts)
     q, own = lax.optimization_barrier((q, own))
     q = lax.all_to_all(q, "head", 0, 0, tiled=True).reshape(OWN, WIDE)
@@ -335,6 +344,7 @@
     arrived = [swapped(back[b], b) for b in range(LEVELS)]
     attended = lax.all_to_all(attended.reshape(heads, mine, WIDE), "head", 0, 0, tiled=True)
     attended = attended.transpose(1, 0, 2).reshape(mine, heads * WIDE)
+    attended, arrived[0] = lax.optimization_barrier((attended, arrived[0]))
     key_grad, value_grad = join(sends, acc, arrived)
     return attended, query_grad, key_grad, value_grad
 

time: 91 us -> 80.1 us (0.88)
  Pallas kernels: 33.3 us -> 22.9 us
  waiting for transfers between devices: 14.3 us -> 7.39 us
  starting transfers between devices: 37.8 us -> 42.8 us
  local copies, waits for them, and re-layouts: 4.37 us -> 5.41 us
    pallas_call x2, Pallas kernels: 27.5 us -> 17.2 us  [the longest x1 9.46 us: outer(): pl.pallas_call(functools.partial(outer_kernel, 10), out_shape=[pltpu.HBM(...]
    ppermute x10, waiting for transfers between devices: 8.58 us -> 4.66 us  [swapped(): return lax.ppermute(block, 'pix', route)]
    ppermute x7, waiting for transfers between devices: 5.75 us -> 2.73 us  [shifted(): return lax.ppermute(block, 'head', route)]
    ppermute x10, starting transfers between devices: 19.8 us -> 22.5 us  [swapped(): return lax.ppermute(block, 'pix', route)]
    all_to_all x1, starting transfers between devices: 4.68 us -> 7.07 us  [body(): q = lax.all_to_all(q, 'head', 0, 0, tiled=True).reshape(OWN, WIDE)]
    reshape x1, local copies, waits for them, and re-layouts: 0.88 us -> 1.92 us  [body(): attended = attended.transpose(1, 0, 2).reshape(mine, heads * WIDE)]
  transfers between devices with their start and end apart: 19 -> 19, of which waited for: 4 -> 4; matrix products, arithmetic and copies ran while one was open for 4% -> 7% of each run, Pallas kernels for 15% -> 10%
where the time goes in v3:
time: 80.1 us; the launch traced here: 79.3 us
  starting transfers between devices  42.8 us (53%)
  Pallas kernels  22.9 us (29%)
  waiting for transfers between devices  7.39 us (9%)
  local copies, waits for them, and re-layouts  5.41 us (7%)
    ppermute x10, starting transfers between devices, swapped(): return lax.ppermute(block, 'pix', route)  22.5 us
    pallas_call x1, Pallas kernels, outer(): pl.pallas_call(functools.partial(outer_kernel, 10), out_shape=[pltpu.HBM(...  9.46 us
    ppermute x7, starting transfers between devices, shifted(): return lax.ppermute(block, 'head', route)  8.48 us
    pallas_call x1, Pallas kernels, inner(): pl.pallas_call(functools.partial(inner_kernel, 12), out_shape=[pltpu.HBM(...  7.71 us
    all_to_all x1, starting transfers between devices, body(): q = lax.all_to_all(q, 'head', 0, 0, tiled=True).reshape(OWN, WIDE)  7.07 us
    all_to_all x1, starting transfers between devices, body(): lax.all_to_all(attended.reshape(heads, mine, WIDE), 'head', 0, 0, tiled=T...  4.81 us
    ppermute x10, waiting for transfers between devices, swapped(): return lax.ppermute(block, 'pix', route)  4.66 us
    ppermute x7, waiting for transfers between devices, shifted(): return lax.ppermute(block, 'head', route)  2.73 us
  transfers between devices with their start and end apart: 19, of which 4 were waited for; matrix products, arithmetic and copies ran while one was open for 7% of the time, Pallas kernels for 10%

profile of v3, /device:TPU:8, one launch (start us, length us, event | category | flops | bytes accessed | tf_op | source)
XLA Modules:
  0.0 79.3 jit_solution(771453726960720815)
XLA Ops:
  0.6 0.0 copy-start
  0.6 1.5 %split_keys_values.1 = (bf16[256,256]{1,0:T(8,128)(2,1)S(1)}, bf16[256,256]{1,0:T(8,128)(2,1)S(1)}, bf16[256,256]{1,0:T(8,128)(2,1)S(1)}, bf16[256,256]{1,0:T(8,...) custom-call(bf16[256,1024]{1,0:T(8,128)(2,1)} %key_ref.1, ...), custom_call_target="tpu_custom_call" | custom-call | bytes 2097152 | tf_op jit(solution)/shard_map/split_keys_values/pallas_call | solution.py:74
  2.1 1.7 %collective-permute-start = (bf16[256,256]{1,0:T(8,128)(2,1)S(1)}, bf16[256,256]{1,0:T(8,128)(2,1)S(1)}, u32[]{:S(2)}, u32[]{:S(2)}) collective-permute-start(bf16[256,256]{1,0:T(8,128)(2,1)S(1)} %get-tuple-element.40), channel_id=1, source_target_pairs={{0,2},{1,3},{2,4},{3,5},{4,6},{5,7},{6,0},{7,1},{8,10},{9,11},{10,... | collective-permute-start | bytes 393224 | tf_op jit(solution)/shard_map/ppermute | solution.py:47
  3.8 0.7 collective-permute-start.1
  4.5 0.2 collective-permute-start.2
  4.7 1.5 %collective-permute-start.3 = (bf16[256,256]{1,0:T(8,128)(2,1)S(1)}, bf16[256,256]{1,0:T(8,128)(2,1)S(1)}, u32[]{:S(2)}, u32[]{:S(2)}) collective-permute-start(bf16[256,256]{1,0:T(8,128)(2,1)S(1)} %get-tuple-element.46), channel_id=1, source_target_pairs={{0,7},{1,6},{2,1},{3,0},{4,3},{5,2},{6,5},{7,4},{8,15},{9,14},{10,... | collective-permute-start | bytes 393224 | tf_op jit(solution)/shard_map/ppermute | solution.py:47
  6.2 2.0 %collective-permute-start.4 = (bf16[256,256]{1,0:T(8,128)(2,1)S(1)}, bf16[256,256]{1,0:T(8,128)(2,1)S(1)}, u32[]{:S(2)}, u32[]{:S(2)}) collective-permute-start(bf16[256,256]{1,0:T(8,128)(2,1)S(1)} %get-tuple-element.47), channel_id=1, source_target_pairs={{0,4},{1,5},{2,6},{3,7},{4,0},{5,1},{6,2},{7,3},{8,12},{9,13},{10,... | collective-permute-start | bytes 393224 | tf_op jit(solution)/shard_map/ppermute | solution.py:47
  8.3 0.8 constant_dynamic-slice_fusion
  9.0 0.8 dynamic_slice.12.counts_ref
  9.8 0.1 copy.21.rows_ref
  9.9 0.8 constant_dynamic-slice_fusion.1
  10.7 0.1 copy.14
  10.8 0.1 copy.18.sends_ref
  10.9 0.0 collective-permute-done.refs_0_
  10.9 2.3 %collective-permute-start.5 = (bf16[256,256]{1,0:T(8,128)(2,1)S(1)}, bf16[256,256]{1,0:T(8,128)(2,1)S(1)}, u32[]{:S(2)}, u32[]{:S(2)}) collective-permute-start(bf16[256,256]{1,0:T(8,128)(2,1)S(1)} %get-tuple-element.48), channel_id=1, source_target_pairs={{0,5},{1,4},{2,7},{3,6},{4,1},{5,0},{6,3},{7,2},{8,13},{9,12},{10,... | collective-permute-start | bytes 393224 | tf_op jit(solution)/shard_map/ppermute | solution.py:47
  13.2 0.0 collective-permute-done.1.refs_1_
  13.2 0.0 collective-permute-start.6
  13.2 0.0 copy-done
  13.2 0.9 %bitcast_bitcast_fusion = bf16[8,256,128]{2,1,0:T(8,128)(2,1)} fusion(bf16[256,1024]{1,0:T(8,128)(2,1)S(1)} %copy-done), kind=kLoop, calls=%fused_computation.1 | loop fusion | bytes 1048576 | tf_op jit(solution)/shard_map/transpose | solution.py:336
  14.1 0.0 collective-permute-done.2.refs_2_
  14.1 0.0 collective-permute-done.3.refs_3_
  14.1 0.5 collective-permute-done.4.refs_4_
  14.6 2.2 %collective-permute-done.5.refs_5_ = bf16[256,256]{1,0:T(8,128)(2,1)S(1)} collective-permute-done((bf16[256,256]{1,0:T(8,128)(2,1)S(1)}, bf16[256,256]{1,0:T(8,128)(2,1)S(1)}, u32[]{:S(2)}, u32[]{:S(2)}) %collective-permute-start.5) | collective-permute-done | bytes 131104 | tf_op jit(solution)/shard_map/ppermute | solution.py:47
  16.8 0.0 collective-permute-done.6.refs_6_
  16.8 2.5 %pick_boundary.1 = (bf16[2048,256]{1,0:T(8,128)(2,1)}, bf16[256,256]{1,0:T(8,128)(2,1)}, bf16[256,256]{1,0:T(8,128)(2,1)}, bf16[256,256]{1,0:T(8,128)(2,1)}, bf1...) custom-call(s32[5,4]{1,0:T(8,128)S(1)} %copy.18.sends_ref, bf16[256,256]{1,0:T(8,128)(2,1)S(1)} %collective-permute-done.refs_0_, ...), custom_call_target="tpu_custom_call" | custom-call | bytes 4194304 | tf_op jit(solution)/shard_map/pick_boundary/pallas_call | solution.py:106
  19.4 7.1 %all-to-all-start = ((bf16[8,256,128]{2,1,0:T(8,128)(2,1)}), bf16[8,256,128]{2,1,0:T(8,128)(2,1)S(1)}, u32[]{:S(2)}, u32[]{:S(2)}) async-start(bf16[8,256,128]{2,1,0:T(8,128)(2,1)} %bitcast_bitcast_fusion), calls=%async_computation | async-start | bytes 1048576 | tf_op jit(solution)/shard_map/all_to_all | solution.py:340
  26.4 0.9 %collective-permute-start.7 = (bf16[256,256]{1,0:T(8,128)(2,1)}, bf16[256,256]{1,0:T(8,128)(2,1)S(1)}, u32[]{:S(2)}, u32[]{:S(2)}) collective-permute-start(bf16[256,256]{1,0:T(8,128)(2,1)} %get-tuple-element.56), channel_id=1, source_target_pairs={{0,8},{8,0},{16,24},{24,16},{32,40},{40,32},{48,56},{56,48},{64,72... | collective-permute-start | bytes 393224 | tf_op jit(solution)/shard_map/ppermute | solution.py:33
  27.3 3.3 %collective-permute-start.8 = (bf16[256,256]{1,0:T(8,128)(2,1)}, bf16[256,256]{1,0:T(8,128)(2,1)}, u32[]{:S(2)}, u32[]{:S(2)}) collective-permute-start(bf16[256,256]{1,0:T(8,128)(2,1)} %get-tuple-element.57), channel_id=1, source_target_pairs={{0,16},{8,24},{16,0},{24,8},{32,48},{40,56},{48,32},{56,40},{64,80... | collective-permute-start | bytes 393224 | tf_op jit(solution)/shard_map/ppermute | solution.py:33
  30.6 4.5 %collective-permute-start.9 = (bf16[256,256]{1,0:T(8,128)(2,1)}, bf16[256,256]{1,0:T(8,128)(2,1)}, u32[]{:S(2)}, u32[]{:S(2)}) collective-permute-start(bf16[256,256]{1,0:T(8,128)(2,1)} %get-tuple-element.58), channel_id=1, source_target_pairs={{0,32},{8,40},{16,48},{24,56},{32,0},{40,8},{48,16},{56,24},{64,96... | collective-permute-start | bytes 393224 | tf_op jit(solution)/shard_map/ppermute | solution.py:33
  35.1 1.5 %collective-permute-start.10 = (bf16[256,256]{1,0:T(8,128)(2,1)}, bf16[256,256]{1,0:T(8,128)(2,1)}, u32[]{:S(2)}, u32[]{:S(2)}) collective-permute-start(bf16[256,256]{1,0:T(8,128)(2,1)} %get-tuple-element.59), channel_id=1, source_target_pairs={{0,64},{8,72},{16,80},{24,88},{32,96},{40,104},{48,112},{56,120},{... | collective-permute-start | bytes 393224 | tf_op jit(solution)/shard_map/ppermute | solution.py:33
  36.6 2.7 %collective-permute-start.11 = (bf16[256,256]{1,0:T(8,128)(2,1)S(1)}, bf16[256,256]{1,0:T(8,128)(2,1)}, u32[]{:S(2)}, u32[]{:S(2)}) collective-permute-start(bf16[256,256]{1,0:T(8,128)(2,1)S(1)} %get-tuple-element.60), channel_id=1, source_target_pairs={{0,128},{8,136},{16,144},{24,152},{32,160},{40,168},{48,176},{56,1... | collective-permute-start | bytes 393224 | tf_op jit(solution)/shard_map/ppermute | solution.py:33
  39.3 0.0 all-to-all-done
  39.3 7.7 %attend_inner.1 = (bf16[2048,128]{1,0:T(8,128)(2,1)}, bf16[2048,128]{1,0:T(8,128)(2,1)}, f32[2048,256]{1,0:T(8,128)S(1)}, bf16[2048,256]{1,0:T(8,128)(2,1)S(1)}, bf16[2048,128]{1,0:T(8,128)(2,1)S(1)}) custom-call(s32[32,9]{1,0:T(8,128)S(1)} %copy.21.rows_ref, s32[32]{0:T(128)S(1)} %dynamic_slice.12.counts_ref, bf16[2048,128]{1,0:T(8,128)(2,1)S(1)} %bitcast.16, ...), custom_call_target="tpu_custom_call" | custom-call | flops 4000000000 | bytes 8388608 | tf_op jit(solution)/shard_map/attend_inner/pallas_call | solution.py:220
  47.0 0.0 collective-permute-done.7.refs_0_
  47.0 0.0 collective-permute-done.8.refs_1_
  47.1 0.0 collective-permute-done.9.refs_2_
  47.1 0.0 collective-permute-done.10.refs_3_
  47.1 0.0 collective-permute-done.11.refs_4_
  47.1 9.5 %attend_outer.1 = (bf16[2048,128]{1,0:T(8,128)(2,1)}, bf16[2048,128]{1,0:T(8,128)(2,1)}, f32[2048,256]{1,0:T(8,128)S(1)}, bf16[256,256]{1,0:T(8,128)(2,1)}, bf16...) custom-call(s32[5,4]{1,0:T(8,128)S(1)} %copy.18.sends_ref, ...), custom_call_target="tpu_custom_call", output_to_operand_aliasing={{0}: (11, {}), {1}: (12, {}), {2}: (13, {})} | custom-call | flops 8000000000 | bytes 8388608 | tf_op jit(solution)/shard_map/attend_outer/pallas_call | solution.py:281
  56.5 4.8 %all-to-all-start.1 = ((bf16[8,256,128]{2,1,0:T(8,128)(2,1)}), bf16[8,256,128]{2,1,0:T(8,128)(2,1)}, u32[]{:S(2)}, u32[]{:S(2)}) async-start(bf16[8,256,128]{2,1,0:T(8,128)(2,1)} %bitcast.18), calls=%async_computation.1 | async-start | bytes 1048576 | tf_op jit(solution)/shard_map/all_to_all | solution.py:345
  61.4 1.0 %collective-permute-start.12 = (bf16[256,256]{1,0:T(8,128)(2,1)}, bf16[256,256]{1,0:T(8,128)(2,1)S(1)}, u32[]{:S(2)}, u32[]{:S(2)}) collective-permute-start(bf16[256,256]{1,0:T(8,128)(2,1)} %get-tuple-element.65), channel_id=1, source_target_pairs={{0,8},{8,0},{16,24},{24,16},{32,40},{40,32},{48,56},{56,48},{64,72... | collective-permute-start | bytes 393224 | tf_op jit(solution)/shard_map/ppermute | solution.py:33
  62.4 1.5 %collective-permute-start.13 = (bf16[256,256]{1,0:T(8,128)(2,1)}, bf16[256,256]{1,0:T(8,128)(2,1)S(1)}, u32[]{:S(2)}, u32[]{:S(2)}) collective-permute-start(bf16[256,256]{1,0:T(8,128)(2,1)} %get-tuple-element.70), channel_id=1, source_target_pairs={{0,16},{8,24},{16,0},{24,8},{32,48},{40,56},{48,32},{56,40},{64,80... | collective-permute-start | bytes 393224 | tf_op jit(solution)/shard_map/ppermute | solution.py:33
  63.8 2.9 %collective-permute-start.14 = (bf16[256,256]{1,0:T(8,128)(2,1)}, bf16[256,256]{1,0:T(8,128)(2,1)S(1)}, u32[]{:S(2)}, u32[]{:S(2)}) collective-permute-start(bf16[256,256]{1,0:T(8,128)(2,1)} %get-tuple-element.71), channel_id=1, source_target_pairs={{0,32},{8,40},{16,48},{24,56},{32,0},{40,8},{48,16},{56,24},{64,96... | collective-permute-start | bytes 393224 | tf_op jit(solution)/shard_map/ppermute | solution.py:33
  66.7 1.5 %collective-permute-start.15 = (bf16[256,256]{1,0:T(8,128)(2,1)}, bf16[256,256]{1,0:T(8,128)(2,1)S(1)}, u32[]{:S(2)}, u32[]{:S(2)}) collective-permute-start(bf16[256,256]{1,0:T(8,128)(2,1)} %get-tuple-element.72), channel_id=1, source_target_pairs={{0,64},{8,72},{16,80},{24,88},{32,96},{40,104},{48,112},{56,120},{... | collective-permute-start | bytes 393224 | tf_op jit(solution)/shard_map/ppermute | solution.py:33
  68.2 2.7 %collective-permute-start.16 = (bf16[256,256]{1,0:T(8,128)(2,1)}, bf16[256,256]{1,0:T(8,128)(2,1)S(1)}, u32[]{:S(2)}, u32[]{:S(2)}) collective-permute-start(bf16[256,256]{1,0:T(8,128)(2,1)} %get-tuple-element.73), channel_id=1, source_target_pairs={{0,128},{8,136},{16,144},{24,152},{32,160},{40,168},{48,176},{56,1... | collective-permute-start | bytes 393224 | tf_op jit(solution)/shard_map/ppermute | solution.py:33
  70.9 0.0 all-to-all-done.1
  70.9 1.9 %copy_bitcast_fusion = bf16[256,1024]{1,0:T(8,128)(2,1)} fusion(bf16[8,256,128]{2,1,0:T(8,128)(2,1)} %all-to-all-done.1), kind=kLoop, calls=%fused_computation | loop fusion | bytes 1048576 | tf_op jit(solution)/shard_map/reshape | solution.py:346
  72.9 0.0 collective-permute-done.12.refs_0_
  72.9 4.4 %collective-permute-done.13.refs_1_ = bf16[256,256]{1,0:T(8,128)(2,1)S(1)} collective-permute-done((bf16[256,256]{1,0:T(8,128)(2,1)}, bf16[256,256]{1,0:T(8,128)(2,1)S(1)}, u32[]{:S(2)}, u32[]{:S(2)}) %collective-permute-start.13) | collective-permute-done | bytes 131104 | tf_op jit(solution)/shard_map/ppermute | solution.py:33
  77.2 0.3 collective-permute-done.14.refs_2_
  77.5 0.0 collective-permute-done.15.refs_3_
  77.5 0.0 collective-permute-done.16.refs_4_
  77.5 1.8 %join_gradients.1 = (bf16[2048,128]{1,0:T(8,128)(2,1)}, bf16[2048,128]{1,0:T(8,128)(2,1)}) custom-call(s32[5,4]{1,0:T(8,128)S(1)} %copy.18.sends_ref, f32[2048,256]{1,0:T(8,128)S(1)} %get-tuple-element.68.acc_ref, bf16[256,256]{1,0:T(8,128)(2,1)S(1)} %collective-permute-done.12.refs_0_, bf16[256,256]{1,0:T(8,128)(2,1)S(1)} %collective-permute-done.13.refs_1_, ...), custom_call_target="tpu_custom_call" | custom-call | flops 1000000 | bytes 4194304 | tf_op jit(solution)/shard_map/join_gradients/pallas_call | solution.py:315
Async XLA Ops:
  0.6 12.6 %copy-start = (bf16[256,1024]{1,0:T(8,128)(2,1)S(1)}, bf16[256,1024]{1,0:T(8,128)(2,1)}, u32[]{:S(2)}) copy-start(bf16[256,1024]{1,0:T(8,128)(2,1)} %param.7) | copy-start | bytes 1572868
  2.1 8.7 %collective-permute-start = (bf16[256,256]{1,0:T(8,128)(2,1)S(1)}, bf16[256,256]{1,0:T(8,128)(2,1)S(1)}, u32[]{:S(2)}, u32[]{:S(2)}) collective-permute-start(bf16[256,256]{1,0:T(8,128)(2,1)S(1)} %get-tuple-element.40), channel_id=1, source_target_pairs={{0,2},{1,3},{2,4},{3,5},{4,6},{5,7},{6,0},{7,1},{8,10},{9,11},{10,... | collective-permute-start | bytes 393224 | tf_op jit(solution)/shard_map/ppermute | solution.py:47
  3.8 9.4 %collective-permute-start.1 = (bf16[256,256]{1,0:T(8,128)(2,1)S(1)}, bf16[256,256]{1,0:T(8,128)(2,1)S(1)}, u32[]{:S(2)}, u32[]{:S(2)}) collective-permute-start(bf16[256,256]{1,0:T(8,128)(2,1)S(1)} %get-tuple-element.44), channel_id=1, source_target_pairs={{0,6},{1,7},{2,0},{3,1},{4,2},{5,3},{6,4},{7,5},{8,14},{9,15},{10,... | collective-permute-start | bytes 393224 | tf_op jit(solution)/shard_map/ppermute | solution.py:47
  4.5 9.6 %collective-permute-start.2 = (bf16[256,256]{1,0:T(8,128)(2,1)S(1)}, bf16[256,256]{1,0:T(8,128)(2,1)S(1)}, u32[]{:S(2)}, u32[]{:S(2)}) collective-permute-start(bf16[256,256]{1,0:T(8,128)(2,1)S(1)} %get-tuple-element.45), channel_id=1, source_target_pairs={{0,3},{1,2},{2,5},{3,4},{4,7},{5,6},{6,1},{7,0},{8,11},{9,10},{10,... | collective-permute-start | bytes 393224 | tf_op jit(solution)/shard_map/ppermute | solution.py:47
  4.7 9.4 %collective-permute-start.3 = (bf16[256,256]{1,0:T(8,128)(2,1)S(1)}, bf16[256,256]{1,0:T(8,128)(2,1)S(1)}, u32[]{:S(2)}, u32[]{:S(2)}) collective-permute-start(bf16[256,256]{1,0:T(8,128)(2,1)S(1)} %get-tuple-element.46), channel_id=1, source_target_pairs={{0,7},{1,6},{2,1},{3,0},{4,3},{5,2},{6,5},{7,4},{8,15},{9,14},{10,... | collective-permute-start | bytes 393224 | tf_op jit(solution)/shard_map/ppermute | solution.py:47
  6.2 8.4 %collective-permute-start.4 = (bf16[256,256]{1,0:T(8,128)(2,1)S(1)}, bf16[256,256]{1,0:T(8,128)(2,1)S(1)}, u32[]{:S(2)}, u32[]{:S(2)}) collective-permute-start(bf16[256,256]{1,0:T(8,128)(2,1)S(1)} %get-tuple-element.47), channel_id=1, source_target_pairs={{0,4},{1,5},{2,6},{3,7},{4,0},{5,1},{6,2},{7,3},{8,12},{9,13},{10,... | collective-permute-start | bytes 393224 | tf_op jit(solution)/shard_map/ppermute | solution.py:47
  10.9 6.0 %collective-permute-start.5 = (bf16[256,256]{1,0:T(8,128)(2,1)S(1)}, bf16[256,256]{1,0:T(8,128)(2,1)S(1)}, u32[]{:S(2)}, u32[]{:S(2)}) collective-permute-start(bf16[256,256]{1,0:T(8,128)(2,1)S(1)} %get-tuple-element.48), channel_id=1, source_target_pairs={{0,5},{1,4},{2,7},{3,6},{4,1},{5,0},{6,3},{7,2},{8,13},{9,12},{10,... | collective-permute-start | bytes 393224 | tf_op jit(solution)/shard_map/ppermute | solution.py:47
  13.2 3.6 %collective-permute-start.6 = (bf16[256,256]{1,0:T(8,128)(2,1)S(1)}, bf16[256,256]{1,0:T(8,128)(2,1)S(1)}, u32[]{:S(2)}, u32[]{:S(2)}) collective-permute-start(bf16[256,256]{1,0:T(8,128)(2,1)S(1)} %get-tuple-element.49), channel_id=1, source_target_pairs={{0,1},{1,0},{2,3},{3,2},{4,5},{5,4},{6,7},{7,6},{8,9},{9,8},{10,11... | collective-permute-start | bytes 393224 | tf_op jit(solution)/shard_map/ppermute | solution.py:47
  19.4 20.0 %all-to-all-start = ((bf16[8,256,128]{2,1,0:T(8,128)(2,1)}), bf16[8,256,128]{2,1,0:T(8,128)(2,1)S(1)}, u32[]{:S(2)}, u32[]{:S(2)}) async-start(bf16[8,256,128]{2,1,0:T(8,128)(2,1)} %bitcast_bitcast_fusion), calls=%async_computation | async-start | bytes 1048576 | tf_op jit(solution)/shard_map/all_to_all | solution.py:340
  26.4 20.6 %collective-permute-start.7 = (bf16[256,256]{1,0:T(8,128)(2,1)}, bf16[256,256]{1,0:T(8,128)(2,1)S(1)}, u32[]{:S(2)}, u32[]{:S(2)}) collective-permute-start(bf16[256,256]{1,0:T(8,128)(2,1)} %get-tuple-element.56), channel_id=1, source_target_pairs={{0,8},{8,0},{16,24},{24,16},{32,40},{40,32},{48,56},{56,48},{64,72... | collective-permute-start | bytes 393224 | tf_op jit(solution)/shard_map/ppermute | solution.py:33
  27.3 19.7 %collective-permute-start.8 = (bf16[256,256]{1,0:T(8,128)(2,1)}, bf16[256,256]{1,0:T(8,128)(2,1)}, u32[]{:S(2)}, u32[]{:S(2)}) collective-permute-start(bf16[256,256]{1,0:T(8,128)(2,1)} %get-tuple-element.57), channel_id=1, source_target_pairs={{0,16},{8,24},{16,0},{24,8},{32,48},{40,56},{48,32},{56,40},{64,80... | collective-permute-start | bytes 393224 | tf_op jit(solution)/shard_map/ppermute | solution.py:33
  30.6 16.5 %collective-permute-start.9 = (bf16[256,256]{1,0:T(8,128)(2,1)}, bf16[256,256]{1,0:T(8,128)(2,1)}, u32[]{:S(2)}, u32[]{:S(2)}) collective-permute-start(bf16[256,256]{1,0:T(8,128)(2,1)} %get-tuple-element.58), channel_id=1, source_target_pairs={{0,32},{8,40},{16,48},{24,56},{32,0},{40,8},{48,16},{56,24},{64,96... | collective-permute-start | bytes 393224 | tf_op jit(solution)/shard_map/ppermute | solution.py:33
  35.1 12.0 %collective-permute-start.10 = (bf16[256,256]{1,0:T(8,128)(2,1)}, bf16[256,256]{1,0:T(8,128)(2,1)}, u32[]{:S(2)}, u32[]{:S(2)}) collective-permute-start(bf16[256,256]{1,0:T(8,128)(2,1)} %get-tuple-element.59), channel_id=1, source_target_pairs={{0,64},{8,72},{16,80},{24,88},{32,96},{40,104},{48,112},{56,120},{... | collective-permute-start | bytes 393224 | tf_op jit(solution)/shard_map/ppermute | solution.py:33
  36.6 10.5 %collective-permute-start.11 = (bf16[256,256]{1,0:T(8,128)(2,1)S(1)}, bf16[256,256]{1,0:T(8,128)(2,1)}, u32[]{:S(2)}, u32[]{:S(2)}) collective-permute-start(bf16[256,256]{1,0:T(8,128)(2,1)S(1)} %get-tuple-element.60), channel_id=1, source_target_pairs={{0,128},{8,136},{16,144},{24,152},{32,160},{40,168},{48,176},{56,1... | collective-permute-start | bytes 393224 | tf_op jit(solution)/shard_map/ppermute | solution.py:33
  56.5 14.4 %all-to-all-start.1 = ((bf16[8,256,128]{2,1,0:T(8,128)(2,1)}), bf16[8,256,128]{2,1,0:T(8,128)(2,1)}, u32[]{:S(2)}, u32[]{:S(2)}) async-start(bf16[8,256,128]{2,1,0:T(8,128)(2,1)} %bitcast.18), calls=%async_computation.1 | async-start | bytes 1048576 | tf_op jit(solution)/shard_map/all_to_all | solution.py:345
  61.4 11.5 %collective-permute-start.12 = (bf16[256,256]{1,0:T(8,128)(2,1)}, bf16[256,256]{1,0:T(8,128)(2,1)S(1)}, u32[]{:S(2)}, u32[]{:S(2)}) collective-permute-start(bf16[256,256]{1,0:T(8,128)(2,1)} %get-tuple-element.65), channel_id=1, source_target_pairs={{0,8},{8,0},{16,24},{24,16},{32,40},{40,32},{48,56},{56,48},{64,72... | collective-permute-start | bytes 393224 | tf_op jit(solution)/shard_map/ppermute | solution.py:33
  62.4 14.9 %collective-permute-start.13 = (bf16[256,256]{1,0:T(8,128)(2,1)}, bf16[256,256]{1,0:T(8,128)(2,1)S(1)}, u32[]{:S(2)}, u32[]{:S(2)}) collective-permute-start(bf16[256,256]{1,0:T(8,128)(2,1)} %get-tuple-element.70), channel_id=1, source_target_pairs={{0,16},{8,24},{16,0},{24,8},{32,48},{40,56},{48,32},{56,40},{64,80... | collective-permute-start | bytes 393224 | tf_op jit(solution)/shard_map/ppermute | solution.py:33
  63.8 13.7 %collective-permute-start.14 = (bf16[256,256]{1,0:T(8,128)(2,1)}, bf16[256,256]{1,0:T(8,128)(2,1)S(1)}, u32[]{:S(2)}, u32[]{:S(2)}) collective-permute-start(bf16[256,256]{1,0:T(8,128)(2,1)} %get-tuple-element.71), channel_id=1, source_target_pairs={{0,32},{8,40},{16,48},{24,56},{32,0},{40,8},{48,16},{56,24},{64,96... | collective-permute-start | bytes 393224 | tf_op jit(solution)/shard_map/ppermute | solution.py:33
  66.7 10.8 %collective-permute-start.15 = (bf16[256,256]{1,0:T(8,128)(2,1)}, bf16[256,256]{1,0:T(8,128)(2,1)S(1)}, u32[]{:S(2)}, u32[]{:S(2)}) collective-permute-start(bf16[256,256]{1,0:T(8,128)(2,1)} %get-tuple-element.72), channel_id=1, source_target_pairs={{0,64},{8,72},{16,80},{24,88},{32,96},{40,104},{48,112},{56,120},{... | collective-permute-start | bytes 393224 | tf_op jit(solution)/shard_map/ppermute | solution.py:33
  68.2 9.3 %collective-permute-start.16 = (bf16[256,256]{1,0:T(8,128)(2,1)}, bf16[256,256]{1,0:T(8,128)(2,1)S(1)}, u32[]{:S(2)}, u32[]{:S(2)}) collective-permute-start(bf16[256,256]{1,0:T(8,128)(2,1)} %get-tuple-element.73), channel_id=1, source_target_pairs={{0,128},{8,136},{16,144},{24,152},{32,160},{40,168},{48,176},{56,1... | collective-permute-start | bytes 393224 | tf_op jit(solution)/shard_map/ppermute | solution.py:33

commit v4 on v3

--- a/solution.py
+++ b/solution.py
@@ -17,6 +17,7 @@
 PART = SEND * BLK
 FILL = -1e30
 CHUNKS = 8
+LEVEL_GROUPS = ((0, 1, 2, 3, 4),)
 HEAD_DEVICES = 8
 OFFSETS = ((1, 0), (3, 0), (1, 1), (3, 1), (2, 0), (2, 1), (0, 1), (0, 0))
 F32 = jnp.float32
@@ -83,32 +84,29 @@
     )(pltpu.with_memory_space_constraint(keys, pltpu.HBM), pltpu.with_memory_space_constraint(values, pltpu.HBM))
 
 
-def pick_kernel(sends_ref, *refs):
-    parts, refs = refs[:HEAD_DEVICES], refs[HEAD_DEVICES:]
-    own_ref, out_refs, held_ref, sems = refs[0], refs[1 : 1 + LEVELS], refs[-2], refs[-1]
+def gather_parts(parts, held_ref):
     me = lax.axis_index("head")
     mine = OWN // HEAD_DEVICES
-    copies = []
-    for t, (steps, core) in enumerate(OFFSETS):
+    for part, (steps, core) in zip(parts, OFFSETS):
         source = offset_index(me, HEAD_DEVICES // 2 - steps, core)
-        at = pl.ds(pl.multiple_of(source * mine, mine), mine)
-        copies.append(pltpu.make_async_copy(parts[t], own_ref.at[at, :], sems.at[t]))
-        copies[-1].start()
-        held_ref[at, :] = parts[t][...]
+        held_ref[pl.ds(pl.multiple_of(source * mine, mine), mine), :] = part[...]
+
+
+def pick_kernel(sends_ref, *refs):
+    parts, out_refs, held_ref = refs[:HEAD_DEVICES], refs[HEAD_DEVICES:-1], refs[-1]
+    gather_parts(parts, held_ref)
     for b in range(LEVELS):
         for s in range(SEND):
             out_refs[b][s * BLK : (s + 1) * BLK, :] = held_ref[rows_of(sends_ref[b, s]), :]
-    for copy in copies:
-        copy.wait()
 
 
 def pick(sends, parts):
     return pl.pallas_call(
         pick_kernel,
-        out_shape=[pltpu.HBM((OWN, 2 * WIDE), BF16)] + [pltpu.VMEM((PART, 2 * WIDE), BF16)] * LEVELS,
+        out_shape=[pltpu.VMEM((PART, 2 * WIDE), BF16)] * LEVELS,
         in_specs=[SM] + [VM] * HEAD_DEVICES,
-        out_specs=[HB] + [VM] * LEVELS,
-        scratch_shapes=[pltpu.VMEM((OWN, 2 * WIDE), BF16), pltpu.SemaphoreType.DMA((HEAD_DEVICES,))],
+        out_specs=[VM] * LEVELS,
+        scratch_shapes=[pltpu.VMEM((OWN, 2 * WIDE), BF16)],
         compiler_params=limits(8),
         cost_estimate=pl.CostEstimate(flops=0, bytes_accessed=4 * 2**20, transcendentals=0),
         name="pick_boundary",
@@ -160,12 +158,14 @@
     yield
 
 
-def run_staged(blocks):
+def run_staged(blocks, ready=None):
     stages = 4
     for t in range(len(blocks) + stages - 1):
         for k in reversed(range(stages)):
             if 0 <= t - k < len(blocks):
                 next(blocks[t - k])
+                if ready and k == 2 and t - k in ready:
+                    ready[t - k].start()
 
 
 def row_copies(at, staged, outs, sems):
@@ -175,15 +175,16 @@
     ]
 
 
-def inner_kernel(unroll, rows_ref, counts_ref, q_ref, far_g_ref, far_own_ref, *refs):
+def inner_kernel(unroll, rows_ref, counts_ref, q_ref, far_g_ref, *refs):
+    parts, refs = refs[:HEAD_DEVICES], refs[HEAD_DEVICES:]
     att_ref, qg_ref, acc_ref, own_ref, g_ref, list_ref = refs[:6]
     staged, sems, in_sems = refs[6:8], refs[8], refs[9]
     loads = []
-    for n, (x, y) in enumerate(((far_own_ref, own_ref), (far_g_ref, g_ref))):
-        for c in range(CHUNKS):
-            part = pl.ds(c * (OWN // CHUNKS), OWN // CHUNKS)
-            loads.append(pltpu.make_async_copy(x.at[part, :], y.at[part, :], in_sems.at[n, c]))
-            loads[-1].start()
+    for c in range(CHUNKS):
+        part = pl.ds(c * (OWN // CHUNKS), OWN // CHUNKS)
+        loads.append(pltpu.make_async_copy(far_g_ref.at[part, :], g_ref.at[part, :], in_sems.at[c]))
+        loads[-1].start()
+    gather_parts(parts, own_ref)
     outs = lambda i: row_copies(i, staged, (att_ref, qg_ref), sems)
     steps = NBLK - LEVELS * SEND
     acc_ref[...] = jnp.zeros_like(acc_ref)
@@ -216,7 +217,7 @@
     lax.fori_loop(0, steps, settle, 0)
 
 
-def inner(rows, counts, q, g, own):
+def inner(rows, counts, q, g, parts):
     return pl.pallas_call(
         functools.partial(inner_kernel, 12),
         out_shape=[
@@ -226,97 +227,92 @@
             pltpu.VMEM((OWN, 2 * WIDE), BF16),
             pltpu.VMEM((OWN, WIDE), BF16),
         ],
-        in_specs=[SM, SM, VM, HB, HB],
+        in_specs=[SM, SM, VM, HB] + [VM] * HEAD_DEVICES,
         out_specs=[HB, HB, VM, VM, VM],
         scratch_shapes=[pltpu.SMEM((NBLK + 1,), jnp.int32)]
         + [pltpu.VMEM((OWN, WIDE), BF16)] * 2
-        + [pltpu.SemaphoreType.DMA((2, NBLK)), pltpu.SemaphoreType.DMA((2, CHUNKS))],
+        + [pltpu.SemaphoreType.DMA((2, NBLK)), pltpu.SemaphoreType.DMA((CHUNKS,))],
         compiler_params=limits(16),
         cost_estimate=pl.CostEstimate(flops=4 * 10**9, bytes_accessed=8 * 2**20, transcendentals=10**6),
         name="attend_inner",
-    )(rows, counts, q, *(pltpu.with_memory_space_constraint(x, pltpu.HBM) for x in (g, own)))
-
-
-def outer_kernel(unroll, sends_ref, rows_ref, counts_ref, q_ref, g_ref, own_ref, *refs):
-    recv_refs, refs = refs[:LEVELS], refs[LEVELS + 3 :]
+    )(rows, counts, q, pltpu.with_memory_space_constraint(g, pltpu.HBM), *parts)
+
+
+def outer_kernel(levels, sends_ref, rows_ref, counts_ref, q_ref, g_ref, own_ref, *refs):
+    recv_refs, refs = refs[: len(levels)], refs[len(levels) + 3 :]
     att_ref, qg_ref, acc_ref = refs[:3]
-    back_refs, refs = refs[3 : 3 + LEVELS], refs[3 + LEVELS :]
-    far_ref, back_ref, staged, sems, back_sems = refs[0], refs[1], refs[2:4], refs[4], refs[5]
+    back_refs, refs = refs[3 : 3 + len(levels)], refs[3 + len(levels) :]
+    held, staged, sems, back_sems = refs[: len(levels)], refs[-4:-2], refs[-2], refs[-1]
     outs = lambda i: row_copies(i, staged, (att_ref, qg_ref), sems)
-    backs = [
-        pltpu.make_async_copy(back_ref.at[b * PART : (b + 1) * PART, :], back_refs[b], back_sems.at[b])
-        for b in range(LEVELS)
-    ]
-    for b in range(LEVELS):
-        far_ref[b * PART : (b + 1) * PART, :] = recv_refs[b][...]
-
-    def step(t, carry):
-        blocks = []
-        for u in range(unroll):
-            e = t * unroll + u
-            i = sends_ref[e // SEND, e % SEND]
+    backs = [pltpu.make_async_copy(x, y, back_sems.at[n]) for n, (x, y) in enumerate(zip(held, back_refs))]
+    blocks, ready = [], {}
+    for n, b in enumerate(levels):
+        for s in range(SEND):
+            i = sends_ref[b, s]
             at = [rows_of(rows_ref[i, j]) if j != 1 else None for j in range(NNB)]
-            far = (far_ref.at[rows_of(e), :], back_ref.at[rows_of(e), :])
+            place = slice(s * BLK, (s + 1) * BLK)
+            far = (recv_refs[n].at[place, :], held[n].at[place, :])
             live = counts_ref[i] > NNB - 1
             blocks.append(staged_block(i, live, at, far, q_ref, g_ref, own_ref, acc_ref, staged, outs))
-        run_staged(blocks)
-        for b in range(LEVELS):
-            pl.when(t == ((b + 1) * SEND - 1) // unroll)(backs[b].start)
-        return carry
-
-    lax.fori_loop(0, LEVELS * SEND // unroll, step, 0)
-
-    def settle(e, carry):
-        for copy in outs(sends_ref[e // SEND, e % SEND]):
-            copy.wait()
-        return carry
-
-    lax.fori_loop(0, LEVELS * SEND, settle, 0)
+        ready[len(blocks) - 1] = backs[n]
+    run_staged(blocks, ready)
+    for b in levels:
+        for s in range(SEND):
+            for copy in outs(sends_ref[b, s]):
+                copy.wait()
     for copy in backs:
         copy.wait()
 
 
-def outer(sends, rows, counts, q, g, own, recv, done):
-    far = (LEVELS * PART, 2 * WIDE)
-    return pl.pallas_call(
-        functools.partial(outer_kernel, 10),
+def outer(levels, sends, rows, counts, q, g, own, recv, done):
+    recv = [recv[b] for b in levels]
+    return pl.pallas_call(
+        functools.partial(outer_kernel, levels),
         out_shape=[
             pltpu.HBM((OWN, WIDE), BF16),
             pltpu.HBM((OWN, WIDE), BF16),
             pltpu.VMEM((OWN, 2 * WIDE), F32),
         ]
-        + [pltpu.HBM((PART, 2 * WIDE), BF16)] * LEVELS,
-        in_specs=[SM] * 3 + [VM] * (3 + LEVELS) + [HB, HB, VM],
-        out_specs=[HB, HB, VM] + [HB] * LEVELS,
-        scratch_shapes=[pltpu.VMEM(far, BF16), pltpu.VMEM(far, BF16)]
+        + [pltpu.HBM((PART, 2 * WIDE), BF16)] * len(levels),
+        in_specs=[SM] * 3 + [VM] * (3 + len(levels)) + [HB, HB, VM],
+        out_specs=[HB, HB, VM] + [HB] * len(levels),
+        scratch_shapes=[pltpu.VMEM((PART, 2 * WIDE), BF16)] * len(levels)
         + [pltpu.VMEM((OWN, WIDE), BF16)] * 2
-        + [pltpu.SemaphoreType.DMA((2, NBLK)), pltpu.SemaphoreType.DMA((LEVELS,))],
-        input_output_aliases={6 + LEVELS + n: n for n in range(3)},
+        + [pltpu.SemaphoreType.DMA((2, NBLK)), pltpu.SemaphoreType.DMA((len(levels),))],
+        input_output_aliases={6 + len(levels) + n: n for n in range(3)},
         compiler_params=limits(16),
-        cost_estimate=pl.CostEstimate(flops=8 * 10**9, bytes_accessed=8 * 2**20, transcendentals=2 * 10**6),
+        cost_estimate=pl.CostEstimate(flops=4 * 10**9, bytes_accessed=4 * 2**20, transcendentals=10**6),
         name="attend_outer",
     )(sends, rows, counts, q, g, own, *recv, *done)
 
 
 def join_kernel(sends_ref, acc_ref, *refs):
-    arrived_refs = refs[:LEVELS]
-    key_ref, value_ref = refs[LEVELS : LEVELS + 2]
-    key_ref[...] = acc_ref[:, :WIDE].astype(BF16)
-    value_ref[...] = acc_ref[:, WIDE:].astype(BF16)
+    arrived_refs, refs = refs[:LEVELS], refs[LEVELS:]
+    outs, sum_ref, staged, sems = refs[:2], refs[2], refs[3:5], refs[5]
+    sum_ref[...] = acc_ref[...]
     for b in range(LEVELS):
         for s in range(SEND):
-            at = rows_of(sends_ref[b, s])
-            both = acc_ref[at, :] + arrived_refs[b][s * BLK : (s + 1) * BLK, :].astype(F32)
-            key_ref[at, :] = both[:, :WIDE].astype(BF16)
-            value_ref[at, :] = both[:, WIDE:].astype(BF16)
+            sum_ref[rows_of(sends_ref[b, s]), :] += arrived_refs[b][s * BLK : (s + 1) * BLK, :].astype(F32)
+    copies = []
+    for c in range(CHUNKS):
+        part = pl.ds(c * (OWN // CHUNKS), OWN // CHUNKS)
+        for n in range(2):
+            staged[n][part, :] = sum_ref[part, n * WIDE : (n + 1) * WIDE].astype(BF16)
+            copies.append(pltpu.make_async_copy(staged[n].at[part, :], outs[n].at[part, :], sems.at[n, c]))
+            copies[-1].start()
+    for copy in copies:
+        copy.wait()
 
 
 def join(sends, acc, arrived):
     return pl.pallas_call(
         join_kernel,
-        out_shape=[jax.ShapeDtypeStruct((OWN, WIDE), BF16)] * 2,
+        out_shape=[pltpu.HBM((OWN, WIDE), BF16)] * 2,
         in_specs=[SM] + [VM] * (1 + LEVELS),
-        out_specs=[VM] * 2,
+        out_specs=[HB] * 2,
+        scratch_shapes=[pltpu.VMEM((OWN, 2 * WIDE), F32)]
+        + [pltpu.VMEM((OWN, WIDE), BF16)] * 2
+        + [pltpu.SemaphoreType.DMA((2, CHUNKS))],
         compiler_params=limits(10),
         cost_estimate=pl.CostEstimate(flops=10**6, bytes_accessed=4 * 2**20, transcendentals=0),
         name="join_gradients",
@@ -335,13 +331,17 @@
     parts = [shifted(x, *o) if o != (0, 0) else x for x, o in zip(parts, OFFSETS)]
     q = query_rows.reshape(mine, heads, WIDE).transpose(1, 0, 2)
     parts[0], rows, counts = lax.optimization_barrier((parts[0], rows, counts))
-    own, *outgoing = pick(sends, parts)
-    q, own = lax.optimization_barrier((q, own))
+    outgoing = pick(sends, parts)
+    q, outgoing = lax.optimization_barrier((q, outgoing))
     q = lax.all_to_all(q, "head", 0, 0, tiled=True).reshape(OWN, WIDE)
     recv = [swapped(outgoing[b], b) for b in range(LEVELS)]
-    *done, own, grad = inner(rows, counts, q, out_grad, own)
-    attended, query_grad, acc, *back = outer(sends, rows, counts, q, grad, own, recv, done)
-    arrived = [swapped(back[b], b) for b in range(LEVELS)]
+    *done, own, grad = inner(rows, counts, q, out_grad, parts)
+    arrived = []
+    for levels in LEVEL_GROUPS:
+        done = outer(levels, sends, rows, counts, q, grad, own, recv, done)
+        arrived += [swapped(x, b) for x, b in zip(done[3:], levels)]
+        done = done[:3]
+    attended, query_grad, acc = done
     attended = lax.all_to_all(attended.reshape(heads, mine, WIDE), "head", 0, 0, tiled=True)
     attended = attended.transpose(1, 0, 2).reshape(mine, heads * WIDE)
     attended, arrived[0] = lax.optimization_barrier((attended, arrived[0]))

time: 80.1 us -> 85 us (1.061)
  local copies, waits for them, and re-layouts: 5.41 us -> 11.3 us
  Pallas kernels: 22.9 us -> 21.6 us
    unnamed x2 -> x24, local copies, waits for them, and re-layouts: 0.01 us -> 5.26 us
    pallas_call x3, Pallas kernels: 13.8 us -> 12.7 us  [the longest x1 9.13 us: outer(): pl.pallas_call(functools.partial(outer_kernel, levels), out_shape=[pltpu....]
  transfers between devices with their start and end apart: 19 -> 19, of which waited for: 4 -> 3; matrix products, arithmetic and copies ran while one was open for 7% -> 7% of each run, Pallas kernels for 10% -> 9%
where the time goes in v4:
time: 85 us; the launch traced here: 84 us
  starting transfers between devices  42.9 us (50%)
  Pallas kernels  21.6 us (25%)
  local copies, waits for them, and re-layouts  11.3 us (13%)
  waiting for transfers between devices  7.31 us (9%)
  between operations  0.96 us (1%)
    ppermute x10, starting transfers between devices, swapped(): return lax.ppermute(block, 'pix', route)  22.4 us
    pallas_call x1, Pallas kernels, outer(): pl.pallas_call(functools.partial(outer_kernel, levels), out_shape=[pltpu....  9.13 us
    ppermute x7, starting transfers between devices, shifted(): return lax.ppermute(block, 'head', route)  8.48 us
    pallas_call x1, Pallas kernels, inner(): pl.pallas_call(functools.partial(inner_kernel, 12), out_shape=[pltpu.HBM(...  7.44 us
    all_to_all x1, starting transfers between devices, body(): q = lax.all_to_all(q, 'head', 0, 0, tiled=True).reshape(OWN, WIDE)  7.11 us
    unnamed x24, local copies, waits for them, and re-layouts  5.26 us
    all_to_all x1, starting transfers between devices, body(): lax.all_to_all(attended.reshape(heads, mine, WIDE), 'head', 0, 0, tiled=T...  4.82 us
    ppermute x10, waiting for transfers between devices, swapped(): return lax.ppermute(block, 'pix', route)  4.67 us
  transfers between devices with their start and end apart: 19, of which 3 were waited for; matrix products, arithmetic and copies ran while one was open for 7% of the time, Pallas kernels for 9%

profile of v4, /device:TPU:8, one launch (start us, length us, event | category | flops | bytes accessed | tf_op | source)
XLA Modules:
  0.0 84.0 jit_solution(4687859288902678400)
XLA Ops:
  0.6 0.0 copy-start
  0.6 1.5 %split_keys_values.1 = (bf16[256,256]{1,0:T(8,128)(2,1)S(1)}, bf16[256,256]{1,0:T(8,128)(2,1)S(1)}, bf16[256,256]{1,0:T(8,128)(2,1)S(1)}, bf16[256,256]{1,0:T(8,...) custom-call(bf16[256,1024]{1,0:T(8,128)(2,1)} %key_ref.1, ...), custom_call_target="tpu_custom_call" | custom-call | bytes 2097152 | tf_op jit(solution)/shard_map/split_keys_values/pallas_call | solution.py:75
  2.1 1.7 %collective-permute-start = (bf16[256,256]{1,0:T(8,128)(2,1)S(1)}, bf16[256,256]{1,0:T(8,128)(2,1)S(1)}, u32[]{:S(2)}, u32[]{:S(2)}) collective-permute-start(bf16[256,256]{1,0:T(8,128)(2,1)S(1)} %get-tuple-element.43), channel_id=1, source_target_pairs={{0,2},{1,3},{2,4},{3,5},{4,6},{5,7},{6,0},{7,1},{8,10},{9,11},{10,... | collective-permute-start | bytes 393224 | tf_op jit(solution)/shard_map/ppermute | solution.py:48
  3.8 0.7 collective-permute-start.1
  4.5 0.2 collective-permute-start.2
  4.7 1.5 %collective-permute-start.3 = (bf16[256,256]{1,0:T(8,128)(2,1)S(1)}, bf16[256,256]{1,0:T(8,128)(2,1)S(1)}, u32[]{:S(2)}, u32[]{:S(2)}) collective-permute-start(bf16[256,256]{1,0:T(8,128)(2,1)S(1)} %get-tuple-element.49), channel_id=1, source_target_pairs={{0,7},{1,6},{2,1},{3,0},{4,3},{5,2},{6,5},{7,4},{8,15},{9,14},{10,... | collective-permute-start | bytes 393224 | tf_op jit(solution)/shard_map/ppermute | solution.py:48
  6.2 2.0 %collective-permute-start.4 = (bf16[256,256]{1,0:T(8,128)(2,1)S(1)}, bf16[256,256]{1,0:T(8,128)(2,1)S(1)}, u32[]{:S(2)}, u32[]{:S(2)}) collective-permute-start(bf16[256,256]{1,0:T(8,128)(2,1)S(1)} %get-tuple-element.50), channel_id=1, source_target_pairs={{0,4},{1,5},{2,6},{3,7},{4,0},{5,1},{6,2},{7,3},{8,12},{9,13},{10,... | collective-permute-start | bytes 393224 | tf_op jit(solution)/shard_map/ppermute | solution.py:48
  8.3 0.8 constant_dynamic-slice_fusion
  9.0 0.8 dynamic_slice.12.counts_ref
  9.8 0.7 copy.21.rows_ref
  10.5 0.8 constant_dynamic-slice_fusion.1
  11.3 0.1 copy.14
  11.4 0.1 copy.18.sends_ref
  11.5 0.0 collective-permute-done.refs_0_
  11.5 2.3 %collective-permute-start.5 = (bf16[256,256]{1,0:T(8,128)(2,1)S(1)}, bf16[256,256]{1,0:T(8,128)(2,1)S(1)}, u32[]{:S(2)}, u32[]{:S(2)}) collective-permute-start(bf16[256,256]{1,0:T(8,128)(2,1)S(1)} %get-tuple-element.51), channel_id=1, source_target_pairs={{0,5},{1,4},{2,7},{3,6},{4,1},{5,0},{6,3},{7,2},{8,13},{9,12},{10,... | collective-permute-start | bytes 393224 | tf_op jit(solution)/shard_map/ppermute | solution.py:48
  13.8 0.0 collective-permute-done.1.refs_1_
  13.8 0.0 collective-permute-start.6
  13.8 0.9 %bitcast_bitcast_fusion = bf16[8,256,128]{2,1,0:T(8,128)(2,1)} fusion(bf16[256,1024]{1,0:T(8,128)(2,1)S(1)} %copy-done), kind=kLoop, calls=%fused_computation.1 | loop fusion | bytes 1048576 | tf_op jit(solution)/shard_map/transpose | solution.py:332
  14.7 0.0 collective-permute-done.2.refs_2_
  14.7 0.0 collective-permute-done.3.refs_3_
  14.7 0.0 copy-start.3
  14.7 0.0 collective-permute-done.4.refs_4_
  14.7 0.0 copy-start.5
  14.8 2.6 %collective-permute-done.5.refs_5_ = bf16[256,256]{1,0:T(8,128)(2,1)S(1)} collective-permute-done((bf16[256,256]{1,0:T(8,128)(2,1)S(1)}, bf16[256,256]{1,0:T(8,128)(2,1)S(1)}, u32[]{:S(2)}, u32[]{:S(2)}) %collective-permute-start.5) | collective-permute-done | bytes 131104 | tf_op jit(solution)/shard_map/ppermute | solution.py:48
  17.4 0.0 collective-permute-done.6.refs_6_
  17.4 1.6 %pick_boundary.1 = (bf16[256,256]{1,0:T(8,128)(2,1)}, bf16[256,256]{1,0:T(8,128)(2,1)}, bf16[256,256]{1,0:T(8,128)(2,1)}, bf16[256,256]{1,0:T(8,128)(2,1)}, bf16[256,256]{1,0:T(8,128)(2,1)}) custom-call(s32[5,4]{1,0:T(8,128)S(1)} %copy.18.sends_ref, bf16[256,256]{1,0:T(8,128)(2,1)S(1)} %collective-permute-done.refs_0_, ...), custom_call_target="tpu_custom_call" | custom-call | bytes 4194304 | tf_op jit(solution)/shard_map/pick_boundary/pallas_call | solution.py:104
  19.0 7.1 %all-to-all-start = ((bf16[8,256,128]{2,1,0:T(8,128)(2,1)}), bf16[8,256,128]{2,1,0:T(8,128)(2,1)S(1)}, u32[]{:S(2)}, u32[]{:S(2)}) async-start(bf16[8,256,128]{2,1,0:T(8,128)(2,1)} %bitcast_bitcast_fusion), calls=%async_computation | async-start | bytes 1048576 | tf_op jit(solution)/shard_map/all_to_all | solution.py:336
  26.1 0.9 %collective-permute-start.7 = (bf16[256,256]{1,0:T(8,128)(2,1)}, bf16[256,256]{1,0:T(8,128)(2,1)}, u32[]{:S(2)}, u32[]{:S(2)}) collective-permute-start(bf16[256,256]{1,0:T(8,128)(2,1)} %get-tuple-element.62), channel_id=1, source_target_pairs={{0,8},{8,0},{16,24},{24,16},{32,40},{40,32},{48,56},{56,48},{64,72... | collective-permute-start | bytes 393224 | tf_op jit(solution)/shard_map/ppermute | solution.py:34
  27.0 3.3 %collective-permute-start.8 = (bf16[256,256]{1,0:T(8,128)(2,1)}, bf16[256,256]{1,0:T(8,128)(2,1)}, u32[]{:S(2)}, u32[]{:S(2)}) collective-permute-start(bf16[256,256]{1,0:T(8,128)(2,1)} %get-tuple-element.63), channel_id=1, source_target_pairs={{0,16},{8,24},{16,0},{24,8},{32,48},{40,56},{48,32},{56,40},{64,80... | collective-permute-start | bytes 393224 | tf_op jit(solution)/shard_map/ppermute | solution.py:34
  30.2 4.5 %collective-permute-start.9 = (bf16[256,256]{1,0:T(8,128)(2,1)}, bf16[256,256]{1,0:T(8,128)(2,1)}, u32[]{:S(2)}, u32[]{:S(2)}) collective-permute-start(bf16[256,256]{1,0:T(8,128)(2,1)} %get-tuple-element.64), channel_id=1, source_target_pairs={{0,32},{8,40},{16,48},{24,56},{32,0},{40,8},{48,16},{56,24},{64,96... | collective-permute-start | bytes 393224 | tf_op jit(solution)/shard_map/ppermute | solution.py:34
  34.7 1.5 %collective-permute-start.10 = (bf16[256,256]{1,0:T(8,128)(2,1)}, bf16[256,256]{1,0:T(8,128)(2,1)}, u32[]{:S(2)}, u32[]{:S(2)}) collective-permute-start(bf16[256,256]{1,0:T(8,128)(2,1)} %get-tuple-element.65), channel_id=1, source_target_pairs={{0,64},{8,72},{16,80},{24,88},{32,96},{40,104},{48,112},{56,120},{... | collective-permute-start | bytes 393224 | tf_op jit(solution)/shard_map/ppermute | solution.py:34
  36.2 2.7 %collective-permute-start.11 = (bf16[256,256]{1,0:T(8,128)(2,1)}, bf16[256,256]{1,0:T(8,128)(2,1)}, u32[]{:S(2)}, u32[]{:S(2)}) collective-permute-start(bf16[256,256]{1,0:T(8,128)(2,1)} %get-tuple-element.66), channel_id=1, source_target_pairs={{0,128},{8,136},{16,144},{24,152},{32,160},{40,168},{48,176},{56,1... | collective-permute-start | bytes 393224 | tf_op jit(solution)/shard_map/ppermute | solution.py:34
  39.0 0.0 all-to-all-done
  39.0 0.0 copy-done.5
  39.0 0.0 copy-done.7
  39.0 0.0 copy-done.9
  39.0 0.0 copy-start.2
  39.0 0.9 %copy-done.2 = bf16[256,256]{1,0:T(8,128)(2,1)S(1)} copy-done((bf16[256,256]{1,0:T(8,128)(2,1)S(1)}, bf16[256,256]{1,0:T(8,128)(2,1)}, u32[]{:S(2)}) %copy-start.2) | copy-done | bytes 131096
  39.9 0.9 %copy-done.4 = bf16[256,256]{1,0:T(8,128)(2,1)S(1)} copy-done((bf16[256,256]{1,0:T(8,128)(2,1)S(1)}, bf16[256,256]{1,0:T(8,128)(2,1)}, u32[]{:S(2)}) %copy-start.4) | copy-done | bytes 131096
  40.8 0.9 %copy-done.6 = bf16[256,256]{1,0:T(8,128)(2,1)S(1)} copy-done((bf16[256,256]{1,0:T(8,128)(2,1)S(1)}, bf16[256,256]{1,0:T(8,128)(2,1)}, u32[]{:S(2)}) %copy-start.6) | copy-done | bytes 131096
  41.7 0.9 %copy-done.8 = bf16[256,256]{1,0:T(8,128)(2,1)S(1)} copy-done((bf16[256,256]{1,0:T(8,128)(2,1)S(1)}, bf16[256,256]{1,0:T(8,128)(2,1)}, u32[]{:S(2)}) %copy-start.8) | copy-done | bytes 131096
  42.6 0.9 %copy-done.10 = bf16[256,256]{1,0:T(8,128)(2,1)S(1)} copy-done((bf16[256,256]{1,0:T(8,128)(2,1)S(1)}, bf16[256,256]{1,0:T(8,128)(2,1)}, u32[]{:S(2)}) %copy-start.10) | copy-done | bytes 131096
  43.5 0.7 copy-done.11
  44.2 7.4 %attend_inner.1 = (bf16[2048,128]{1,0:T(8,128)(2,1)}, bf16[2048,128]{1,0:T(8,128)(2,1)}, f32[2048,256]{1,0:T(8,128)S(1)}, bf16[2048,256]{1,0:T(8,128)(2,1)S(1)}, bf16[2048,128]{1,0:T(8,128)(2,1)S(1)}) custom-call(s32[32,9]{1,0:T(8,128)S(1)} %copy-done.11, s32[32]{0:T(128)S(1)} %dynamic_slice.12.counts_ref, bf16[2048,128]{1,0:T(8,128)(2,1)S(1)} %bitcast.16, ...), custom_call_target="tpu_custom_call" | custom-call | flops 4000000000 | bytes 8388608 | tf_op jit(solution)/shard_map/attend_inner/pallas_call | solution.py:221
  51.7 0.0 collective-permute-done.7.refs_0_
  51.7 0.0 collective-permute-done.8.refs_1_
  51.7 0.0 collective-permute-done.9.refs_2_
  51.7 0.0 collective-permute-done.10.refs_3_
  51.7 0.0 collective-permute-done.11.refs_4_
  51.7 9.1 %attend_outer.1 = (bf16[2048,128]{1,0:T(8,128)(2,1)}, bf16[2048,128]{1,0:T(8,128)(2,1)}, f32[2048,256]{1,0:T(8,128)S(1)}, bf16[256,256]{1,0:T(8,128)(2,1)}, bf16...) custom-call(s32[5,4]{1,0:T(8,128)S(1)} %copy.18.sends_ref, ...), custom_call_target="tpu_custom_call", output_to_operand_aliasing={{0}: (11, {}), {1}: (12, {}), {2}: (13, {})} | custom-call | flops 4000000000 | bytes 4194304 | tf_op jit(solution)/shard_map/attend_outer/pallas_call | solution.py:269
  60.9 4.8 %all-to-all-start.1 = ((bf16[8,256,128]{2,1,0:T(8,128)(2,1)}), bf16[8,256,128]{2,1,0:T(8,128)(2,1)}, u32[]{:S(2)}, u32[]{:S(2)}) async-start(bf16[8,256,128]{2,1,0:T(8,128)(2,1)} %bitcast.18), calls=%async_computation.1 | async-start | bytes 1048576 | tf_op jit(solution)/shard_map/all_to_all | solution.py:345
  65.7 1.0 %collective-permute-start.12 = (bf16[256,256]{1,0:T(8,128)(2,1)}, bf16[256,256]{1,0:T(8,128)(2,1)S(1)}, u32[]{:S(2)}, u32[]{:S(2)}) collective-permute-start(bf16[256,256]{1,0:T(8,128)(2,1)} %get-tuple-element.71), channel_id=1, source_target_pairs={{0,8},{8,0},{16,24},{24,16},{32,40},{40,32},{48,56},{56,48},{64,72... | collective-permute-start | bytes 393224 | tf_op jit(solution)/shard_map/ppermute | solution.py:34
  66.7 1.5 %collective-permute-start.13 = (bf16[256,256]{1,0:T(8,128)(2,1)}, bf16[256,256]{1,0:T(8,128)(2,1)S(1)}, u32[]{:S(2)}, u32[]{:S(2)}) collective-permute-start(bf16[256,256]{1,0:T(8,128)(2,1)} %get-tuple-element.76), channel_id=1, source_target_pairs={{0,16},{8,24},{16,0},{24,8},{32,48},{40,56},{48,32},{56,40},{64,80... | collective-permute-start | bytes 393224 | tf_op jit(solution)/shard_map/ppermute | solution.py:34
  68.2 2.9 %collective-permute-start.14 = (bf16[256,256]{1,0:T(8,128)(2,1)}, bf16[256,256]{1,0:T(8,128)(2,1)S(1)}, u32[]{:S(2)}, u32[]{:S(2)}) collective-permute-start(bf16[256,256]{1,0:T(8,128)(2,1)} %get-tuple-element.77), channel_id=1, source_target_pairs={{0,32},{8,40},{16,48},{24,56},{32,0},{40,8},{48,16},{56,24},{64,96... | collective-permute-start | bytes 393224 | tf_op jit(solution)/shard_map/ppermute | solution.py:34
  71.0 1.5 %collective-permute-start.15 = (bf16[256,256]{1,0:T(8,128)(2,1)}, bf16[256,256]{1,0:T(8,128)(2,1)S(1)}, u32[]{:S(2)}, u32[]{:S(2)}) collective-permute-start(bf16[256,256]{1,0:T(8,128)(2,1)} %get-tuple-element.78), channel_id=1, source_target_pairs={{0,64},{8,72},{16,80},{24,88},{32,96},{40,104},{48,112},{56,120},{... | collective-permute-start | bytes 393224 | tf_op jit(solution)/shard_map/ppermute | solution.py:34
  72.5 2.7 %collective-permute-start.16 = (bf16[256,256]{1,0:T(8,128)(2,1)}, bf16[256,256]{1,0:T(8,128)(2,1)S(1)}, u32[]{:S(2)}, u32[]{:S(2)}) collective-permute-start(bf16[256,256]{1,0:T(8,128)(2,1)} %get-tuple-element.79), channel_id=1, source_target_pairs={{0,128},{8,136},{16,144},{24,152},{32,160},{40,168},{48,176},{56,1... | collective-permute-start | bytes 393224 | tf_op jit(solution)/shard_map/ppermute | solution.py:34
  75.3 0.0 all-to-all-done.1
  75.3 1.9 %copy_bitcast_fusion = bf16[256,1024]{1,0:T(8,128)(2,1)} fusion(bf16[8,256,128]{2,1,0:T(8,128)(2,1)} %all-to-all-done.1), kind=kLoop, calls=%fused_computation | loop fusion | bytes 1048576 | tf_op jit(solution)/shard_map/reshape | solution.py:346
  77.2 0.0 collective-permute-done.12.refs_0_
  77.2 4.4 %collective-permute-done.13.refs_1_ = bf16[256,256]{1,0:T(8,128)(2,1)S(1)} collective-permute-done((bf16[256,256]{1,0:T(8,128)(2,1)}, bf16[256,256]{1,0:T(8,128)(2,1)S(1)}, u32[]{:S(2)}, u32[]{:S(2)}) %collective-permute-start.13) | collective-permute-done | bytes 131104 | tf_op jit(solution)/shard_map/ppermute | solution.py:34
  81.6 0.3 collective-permute-done.14.refs_2_
  81.8 0.0 collective-permute-done.15.refs_3_
  81.8 0.0 collective-permute-done.16.refs_4_
  81.8 2.0 %join_gradients.1 = (bf16[2048,128]{1,0:T(8,128)(2,1)}, bf16[2048,128]{1,0:T(8,128)(2,1)}) custom-call(s32[5,4]{1,0:T(8,128)S(1)} %copy.18.sends_ref, f32[2048,256]{1,0:T(8,128)S(1)} %get-tuple-element.74.acc_ref, bf16[256,256]{1,0:T(8,128)(2,1)S(1)} %collective-permute-done.12.refs_0_, bf16[256,256]{1,0:T(8,128)(2,1)S(1)} %collective-permute-done.13.refs_1_, ...), custom_call_target="tpu_custom_call" | custom-call | flops 1000000 | bytes 4194304 | tf_op jit(solution)/shard_map/join_gradients/pallas_call | solution.py:308
  (11 shorter events, 0.0 us)
Async XLA Ops:
  0.6 13.2 %copy-start = (bf16[256,1024]{1,0:T(8,128)(2,1)S(1)}, bf16[256,1024]{1,0:T(8,128)(2,1)}, u32[]{:S(2)}) copy-start(bf16[256,1024]{1,0:T(8,128)(2,1)} %param.7) | copy-start | bytes 1572868
  2.1 9.3 %collective-permute-start = (bf16[256,256]{1,0:T(8,128)(2,1)S(1)}, bf16[256,256]{1,0:T(8,128)(2,1)S(1)}, u32[]{:S(2)}, u32[]{:S(2)}) collective-permute-start(bf16[256,256]{1,0:T(8,128)(2,1)S(1)} %get-tuple-element.43), channel_id=1, source_target_pairs={{0,2},{1,3},{2,4},{3,5},{4,6},{5,7},{6,0},{7,1},{8,10},{9,11},{10,... | collective-permute-start | bytes 393224 | tf_op jit(solution)/shard_map/ppermute | solution.py:48
  3.8 10.0 %collective-permute-start.1 = (bf16[256,256]{1,0:T(8,128)(2,1)S(1)}, bf16[256,256]{1,0:T(8,128)(2,1)S(1)}, u32[]{:S(2)}, u32[]{:S(2)}) collective-permute-start(bf16[256,256]{1,0:T(8,128)(2,1)S(1)} %get-tuple-element.47), channel_id=1, source_target_pairs={{0,6},{1,7},{2,0},{3,1},{4,2},{5,3},{6,4},{7,5},{8,14},{9,15},{10,... | collective-permute-start | bytes 393224 | tf_op jit(solution)/shard_map/ppermute | solution.py:48
  4.5 10.2 %collective-permute-start.2 = (bf16[256,256]{1,0:T(8,128)(2,1)S(1)}, bf16[256,256]{1,0:T(8,128)(2,1)S(1)}, u32[]{:S(2)}, u32[]{:S(2)}) collective-permute-start(bf16[256,256]{1,0:T(8,128)(2,1)S(1)} %get-tuple-element.48), channel_id=1, source_target_pairs={{0,3},{1,2},{2,5},{3,4},{4,7},{5,6},{6,1},{7,0},{8,11},{9,10},{10,... | collective-permute-start | bytes 393224 | tf_op jit(solution)/shard_map/ppermute | solution.py:48
  4.7 10.0 %collective-permute-start.3 = (bf16[256,256]{1,0:T(8,128)(2,1)S(1)}, bf16[256,256]{1,0:T(8,128)(2,1)S(1)}, u32[]{:S(2)}, u32[]{:S(2)}) collective-permute-start(bf16[256,256]{1,0:T(8,128)(2,1)S(1)} %get-tuple-element.49), channel_id=1, source_target_pairs={{0,7},{1,6},{2,1},{3,0},{4,3},{5,2},{6,5},{7,4},{8,15},{9,14},{10,... | collective-permute-start | bytes 393224 | tf_op jit(solution)/shard_map/ppermute | solution.py:48
  6.2 8.5 %collective-permute-start.4 = (bf16[256,256]{1,0:T(8,128)(2,1)S(1)}, bf16[256,256]{1,0:T(8,128)(2,1)S(1)}, u32[]{:S(2)}, u32[]{:S(2)}) collective-permute-start(bf16[256,256]{1,0:T(8,128)(2,1)S(1)} %get-tuple-element.50), channel_id=1, source_target_pairs={{0,4},{1,5},{2,6},{3,7},{4,0},{5,1},{6,2},{7,3},{8,12},{9,13},{10,... | collective-permute-start | bytes 393224 | tf_op jit(solution)/shard_map/ppermute | solution.py:48
  11.5 5.9 %collective-permute-start.5 = (bf16[256,256]{1,0:T(8,128)(2,1)S(1)}, bf16[256,256]{1,0:T(8,128)(2,1)S(1)}, u32[]{:S(2)}, u32[]{:S(2)}) collective-permute-start(bf16[256,256]{1,0:T(8,128)(2,1)S(1)} %get-tuple-element.51), channel_id=1, source_target_pairs={{0,5},{1,4},{2,7},{3,6},{4,1},{5,0},{6,3},{7,2},{8,13},{9,12},{10,... | collective-permute-start | bytes 393224 | tf_op jit(solution)/shard_map/ppermute | solution.py:48
  13.8 3.6 %collective-permute-start.6 = (bf16[256,256]{1,0:T(8,128)(2,1)S(1)}, bf16[256,256]{1,0:T(8,128)(2,1)S(1)}, u32[]{:S(2)}, u32[]{:S(2)}) collective-permute-start(bf16[256,256]{1,0:T(8,128)(2,1)S(1)} %get-tuple-element.52), channel_id=1, source_target_pairs={{0,1},{1,0},{2,3},{3,2},{4,5},{5,4},{6,7},{7,6},{8,9},{9,8},{10,11... | collective-permute-start | bytes 393224 | tf_op jit(solution)/shard_map/ppermute | solution.py:48
  14.7 24.2 %copy-start.1 = (bf16[256,256]{1,0:T(8,128)(2,1)}, bf16[256,256]{1,0:T(8,128)(2,1)S(1)}, u32[]{:S(2)}) copy-start(bf16[256,256]{1,0:T(8,128)(2,1)S(1)} %collective-permute-done.2.refs_2_) | copy-start | bytes 393220
  14.7 24.2 %copy-start.3 = (bf16[256,256]{1,0:T(8,128)(2,1)}, bf16[256,256]{1,0:T(8,128)(2,1)S(1)}, u32[]{:S(2)}) copy-start(bf16[256,256]{1,0:T(8,128)(2,1)S(1)} %collective-permute-done.3.refs_3_) | copy-start | bytes 393220
  14.7 24.2 %copy-start.5 = (bf16[256,256]{1,0:T(8,128)(2,1)}, bf16[256,256]{1,0:T(8,128)(2,1)S(1)}, u32[]{:S(2)}) copy-start(bf16[256,256]{1,0:T(8,128)(2,1)S(1)} %collective-permute-done.4.refs_4_) | copy-start | bytes 393220
  17.4 21.6 %copy-start.7 = (bf16[256,256]{1,0:T(8,128)(2,1)}, bf16[256,256]{1,0:T(8,128)(2,1)S(1)}, u32[]{:S(2)}) copy-start(bf16[256,256]{1,0:T(8,128)(2,1)S(1)} %collective-permute-done.5.refs_5_) | copy-start | bytes 393220
  17.4 21.6 %copy-start.9 = (bf16[256,256]{1,0:T(8,128)(2,1)}, bf16[256,256]{1,0:T(8,128)(2,1)S(1)}, u32[]{:S(2)}) copy-start(bf16[256,256]{1,0:T(8,128)(2,1)S(1)} %collective-permute-done.6.refs_6_) | copy-start | bytes 393220
  19.0 20.0 %all-to-all-start = ((bf16[8,256,128]{2,1,0:T(8,128)(2,1)}), bf16[8,256,128]{2,1,0:T(8,128)(2,1)S(1)}, u32[]{:S(2)}, u32[]{:S(2)}) async-start(bf16[8,256,128]{2,1,0:T(8,128)(2,1)} %bitcast_bitcast_fusion), calls=%async_computation | async-start | bytes 1048576 | tf_op jit(solution)/shard_map/all_to_all | solution.py:336
  26.1 25.6 %collective-permute-start.7 = (bf16[256,256]{1,0:T(8,128)(2,1)}, bf16[256,256]{1,0:T(8,128)(2,1)}, u32[]{:S(2)}, u32[]{:S(2)}) collective-permute-start(bf16[256,256]{1,0:T(8,128)(2,1)} %get-tuple-element.62), channel_id=1, source_target_pairs={{0,8},{8,0},{16,24},{24,16},{32,40},{40,32},{48,56},{56,48},{64,72... | collective-permute-start | bytes 393224 | tf_op jit(solution)/shard_map/ppermute | solution.py:34
  27.0 24.7 %collective-permute-start.8 = (bf16[256,256]{1,0:T(8,128)(2,1)}, bf16[256,256]{1,0:T(8,128)(2,1)}, u32[]{:S(2)}, u32[]{:S(2)}) collective-permute-start(bf16[256,256]{1,0:T(8,128)(2,1)} %get-tuple-element.63), channel_id=1, source_target_pairs={{0,16},{8,24},{16,0},{24,8},{32,48},{40,56},{48,32},{56,40},{64,80... | collective-permute-start | bytes 393224 | tf_op jit(solution)/shard_map/ppermute | solution.py:34
  30.2 21.5 %collective-permute-start.9 = (bf16[256,256]{1,0:T(8,128)(2,1)}, bf16[256,256]{1,0:T(8,128)(2,1)}, u32[]{:S(2)}, u32[]{:S(2)}) collective-permute-start(bf16[256,256]{1,0:T(8,128)(2,1)} %get-tuple-element.64), channel_id=1, source_target_pairs={{0,32},{8,40},{16,48},{24,56},{32,0},{40,8},{48,16},{56,24},{64,96... | collective-permute-start | bytes 393224 | tf_op jit(solution)/shard_map/ppermute | solution.py:34
  34.7 17.0 %collective-permute-start.10 = (bf16[256,256]{1,0:T(8,128)(2,1)}, bf16[256,256]{1,0:T(8,128)(2,1)}, u32[]{:S(2)}, u32[]{:S(2)}) collective-permute-start(bf16[256,256]{1,0:T(8,128)(2,1)} %get-tuple-element.65), channel_id=1, source_target_pairs={{0,64},{8,72},{16,80},{24,88},{32,96},{40,104},{48,112},{56,120},{... | collective-permute-start | bytes 393224 | tf_op jit(solution)/shard_map/ppermute | solution.py:34
  36.2 15.5 %collective-permute-start.11 = (bf16[256,256]{1,0:T(8,128)(2,1)}, bf16[256,256]{1,0:T(8,128)(2,1)}, u32[]{:S(2)}, u32[]{:S(2)}) collective-permute-start(bf16[256,256]{1,0:T(8,128)(2,1)} %get-tuple-element.66), channel_id=1, source_target_pairs={{0,128},{8,136},{16,144},{24,152},{32,160},{40,168},{48,176},{56,1... | collective-permute-start | bytes 393224 | tf_op jit(solution)/shard_map/ppermute | solution.py:34
  39.0 0.9 %copy-start.2 = (bf16[256,256]{1,0:T(8,128)(2,1)S(1)}, bf16[256,256]{1,0:T(8,128)(2,1)}, u32[]{:S(2)}) copy-start(bf16[256,256]{1,0:T(8,128)(2,1)} %copy-done.1) | copy-start | bytes 393220
  39.9 0.9 %copy-start.4 = (bf16[256,256]{1,0:T(8,128)(2,1)S(1)}, bf16[256,256]{1,0:T(8,128)(2,1)}, u32[]{:S(2)}) copy-start(bf16[256,256]{1,0:T(8,128)(2,1)} %copy-done.3) | copy-start | bytes 393220
  40.8 0.9 %copy-start.6 = (bf16[256,256]{1,0:T(8,128)(2,1)S(1)}, bf16[256,256]{1,0:T(8,128)(2,1)}, u32[]{:S(2)}) copy-start(bf16[256,256]{1,0:T(8,128)(2,1)} %copy-done.5) | copy-start | bytes 393220
  41.7 0.9 %copy-start.8 = (bf16[256,256]{1,0:T(8,128)(2,1)S(1)}, bf16[256,256]{1,0:T(8,128)(2,1)}, u32[]{:S(2)}) copy-start(bf16[256,256]{1,0:T(8,128)(2,1)} %copy-done.7) | copy-start | bytes 393220
  42.6 0.9 %copy-start.10 = (bf16[256,256]{1,0:T(8,128)(2,1)S(1)}, bf16[256,256]{1,0:T(8,128)(2,1)}, u32[]{:S(2)}) copy-start(bf16[256,256]{1,0:T(8,128)(2,1)} %copy-done.9) | copy-start | bytes 393220
  43.5 0.7 copy-start.11
  60.9 14.4 %all-to-all-start.1 = ((bf16[8,256,128]{2,1,0:T(8,128)(2,1)}), bf16[8,256,128]{2,1,0:T(8,128)(2,1)}, u32[]{:S(2)}, u32[]{:S(2)}) async-start(bf16[8,256,128]{2,1,0:T(8,128)(2,1)} %bitcast.18), calls=%async_computation.1 | async-start | bytes 1048576 | tf_op jit(solution)/shard_map/all_to_all | solution.py:345
  65.7 11.5 %collective-permute-start.12 = (bf16[256,256]{1,0:T(8,128)(2,1)}, bf16[256,256]{1,0:T(8,128)(2,1)S(1)}, u32[]{:S(2)}, u32[]{:S(2)}) collective-permute-start(bf16[256,256]{1,0:T(8,128)(2,1)} %get-tuple-element.71), channel_id=1, source_target_pairs={{0,8},{8,0},{16,24},{24,16},{32,40},{40,32},{48,56},{56,48},{64,72... | collective-permute-start | bytes 393224 | tf_op jit(solution)/shard_map/ppermute | solution.py:34
  66.7 14.9 %collective-permute-start.13 = (bf16[256,256]{1,0:T(8,128)(2,1)}, bf16[256,256]{1,0:T(8,128)(2,1)S(1)}, u32[]{:S(2)}, u32[]{:S(2)}) collective-permute-start(bf16[256,256]{1,0:T(8,128)(2,1)} %get-tuple-element.76), channel_id=1, source_target_pairs={{0,16},{8,24},{16,0},{24,8},{32,48},{40,56},{48,32},{56,40},{64,80... | collective-permute-start | bytes 393224 | tf_op jit(solution)/shard_map/ppermute | solution.py:34
  68.2 13.7 %collective-permute-start.14 = (bf16[256,256]{1,0:T(8,128)(2,1)}, bf16[256,256]{1,0:T(8,128)(2,1)S(1)}, u32[]{:S(2)}, u32[]{:S(2)}) collective-permute-start(bf16[256,256]{1,0:T(8,128)(2,1)} %get-tuple-element.77), channel_id=1, source_target_pairs={{0,32},{8,40},{16,48},{24,56},{32,0},{40,8},{48,16},{56,24},{64,96... | collective-permute-start | bytes 393224 | tf_op jit(solution)/shard_map/ppermute | solution.py:34
  71.0 10.8 %collective-permute-start.15 = (bf16[256,256]{1,0:T(8,128)(2,1)}, bf16[256,256]{1,0:T(8,128)(2,1)S(1)}, u32[]{:S(2)}, u32[]{:S(2)}) collective-permute-start(bf16[256,256]{1,0:T(8,128)(2,1)} %get-tuple-element.78), channel_id=1, source_target_pairs={{0,64},{8,72},{16,80},{24,88},{32,96},{40,104},{48,112},{56,120},{... | collective-permute-start | bytes 393224 | tf_op jit(solution)/shard_map/ppermute | solution.py:34
  72.5 9.3 %collective-permute-start.16 = (bf16[256,256]{1,0:T(8,128)(2,1)}, bf16[256,256]{1,0:T(8,128)(2,1)S(1)}, u32[]{:S(2)}, u32[]{:S(2)}) collective-permute-start(bf16[256,256]{1,0:T(8,128)(2,1)} %get-tuple-element.79), channel_id=1, source_target_pairs={{0,128},{8,136},{16,144},{24,152},{32,160},{40,168},{48,176},{56,1... | collective-permute-start | bytes 393224 | tf_op jit(solution)/shard_map/ppermute | solution.py:34

commit v5 on v3

--- a/solution.py
+++ b/solution.py
@@ -23,7 +23,6 @@
 BF16 = jnp.bfloat16
 
 VM = pl.BlockSpec(memory_space=pltpu.VMEM)
-SM = pl.BlockSpec(memory_space=pltpu.SMEM)
 HB = pl.BlockSpec(memory_space=pltpu.HBM)
 
 
@@ -83,9 +82,26 @@
     )(pltpu.with_memory_space_constraint(keys, pltpu.HBM), pltpu.with_memory_space_constraint(values, pltpu.HBM))
 
 
-def pick_kernel(sends_ref, *refs):
+def index_loads(sources, targets, sems):
+    loads = [pltpu.make_async_copy(x, y, sems.at[n]) for n, (x, y) in enumerate(zip(sources, targets))]
+    for load in loads:
+        load.start()
+    return loads
+
+
+def in_hbm(*arrays):
+    return [pltpu.with_memory_space_constraint(x, pltpu.HBM) for x in arrays]
+
+
+def index_scratch(*arrays):
+    return [pltpu.SMEM(x.shape, x.dtype) for x in arrays] + [pltpu.SemaphoreType.DMA((len(arrays),))]
+
+
+def pick_kernel(far_sends_ref, *refs):
     parts, refs = refs[:HEAD_DEVICES], refs[HEAD_DEVICES:]
-    own_ref, out_refs, held_ref, sems = refs[0], refs[1 : 1 + LEVELS], refs[-2], refs[-1]
+    own_ref, out_refs, held_ref, sems = refs[0], refs[1 : 1 + LEVELS], refs[-4], refs[-3]
+    sends_ref, index_sems = refs[-2:]
+    (index,) = index_loads((far_sends_ref,), (sends_ref,), index_sems)
     me = lax.axis_index("head")
     mine = OWN // HEAD_DEVICES
     copies = []
@@ -95,6 +111,7 @@
         copies.append(pltpu.make_async_copy(parts[t], own_ref.at[at, :], sems.at[t]))
         copies[-1].start()
         held_ref[at, :] = parts[t][...]
+    index.wait()
     for b in range(LEVELS):
         for s in range(SEND):
             out_refs[b][s * BLK : (s + 1) * BLK, :] = held_ref[rows_of(sends_ref[b, s]), :]
@@ -106,13 +123,14 @@
     return pl.pallas_call(
         pick_kernel,
         out_shape=[pltpu.HBM((OWN, 2 * WIDE), BF16)] + [pltpu.VMEM((PART, 2 * WIDE), BF16)] * LEVELS,
-        in_specs=[SM] + [VM] * HEAD_DEVICES,
+        in_specs=[HB] + [VM] * HEAD_DEVICES,
         out_specs=[HB] + [VM] * LEVELS,
-        scratch_shapes=[pltpu.VMEM((OWN, 2 * WIDE), BF16), pltpu.SemaphoreType.DMA((HEAD_DEVICES,))],
+        scratch_shapes=[pltpu.VMEM((OWN, 2 * WIDE), BF16), pltpu.SemaphoreType.DMA((HEAD_DEVICES,))]
+        + index_scratch(sends),
         compiler_params=limits(8),
         cost_estimate=pl.CostEstimate(flops=0, bytes_accessed=4 * 2**20, transcendentals=0),
         name="pick_boundary",
-    )(sends, *parts)
+    )(*in_hbm(sends), *parts)
 
 
 def staged_block(i, live, at, far, q_ref, g_ref, own_ref, acc_ref, staged, outs):
@@ -160,12 +178,14 @@
     yield
 
 
-def run_staged(blocks):
+def run_staged(blocks, ready=None):
     stages = 4
     for t in range(len(blocks) + stages - 1):
         for k in reversed(range(stages)):
             if 0 <= t - k < len(blocks):
                 next(blocks[t - k])
+                if ready and k == 2 and t - k in ready:
+                    ready[t - k].start()
 
 
 def row_copies(at, staged, outs, sems):
@@ -175,9 +195,11 @@
     ]
 
 
-def inner_kernel(unroll, rows_ref, counts_ref, q_ref, far_g_ref, far_own_ref, *refs):
+def inner_kernel(unroll, far_rows_ref, far_counts_ref, q_ref, far_g_ref, far_own_ref, *refs):
     att_ref, qg_ref, acc_ref, own_ref, g_ref, list_ref = refs[:6]
     staged, sems, in_sems = refs[6:8], refs[8], refs[9]
+    rows_ref, counts_ref, index_sems = refs[10:]
+    indices = index_loads((far_rows_ref, far_counts_ref), (rows_ref, counts_ref), index_sems)
     loads = []
     for n, (x, y) in enumerate(((far_own_ref, own_ref), (far_g_ref, g_ref))):
         for c in range(CHUNKS):
@@ -188,6 +210,9 @@
     steps = NBLK - LEVELS * SEND
     acc_ref[...] = jnp.zeros_like(acc_ref)
 
+    for load in indices:
+        load.wait()
+
     def note(i, count):
         list_ref[count] = i
         return count + (rows_ref[i, 1] < NBLK).astype(jnp.int32)
@@ -226,83 +251,82 @@
             pltpu.VMEM((OWN, 2 * WIDE), BF16),
             pltpu.VMEM((OWN, WIDE), BF16),
         ],
-        in_specs=[SM, SM, VM, HB, HB],
+        in_specs=[HB, HB, VM, HB, HB],
         out_specs=[HB, HB, VM, VM, VM],
         scratch_shapes=[pltpu.SMEM((NBLK + 1,), jnp.int32)]
         + [pltpu.VMEM((OWN, WIDE), BF16)] * 2
-        + [pltpu.SemaphoreType.DMA((2, NBLK)), pltpu.SemaphoreType.DMA((2, CHUNKS))],
+        + [pltpu.SemaphoreType.DMA((2, NBLK)), pltpu.SemaphoreType.DMA((2, CHUNKS))]
+        + index_scratch(rows, counts),
         compiler_params=limits(16),
         cost_estimate=pl.CostEstimate(flops=4 * 10**9, bytes_accessed=8 * 2**20, transcendentals=10**6),
         name="attend_inner",
-    )(rows, counts, q, *(pltpu.with_memory_space_constraint(x, pltpu.HBM) for x in (g, own)))
-
-
-def outer_kernel(unroll, sends_ref, rows_ref, counts_ref, q_ref, g_ref, own_ref, *refs):
-    recv_refs, refs = refs[:LEVELS], refs[LEVELS + 3 :]
+    )(*in_hbm(rows, counts), q, *in_hbm(g, own))
+
+
+def outer_kernel(levels, far_sends_ref, far_rows_ref, far_counts_ref, q_ref, g_ref, own_ref, *refs):
+    recv_refs, refs = refs[: len(levels)], refs[len(levels) + 3 :]
+    sends_ref, rows_ref, counts_ref, index_sems = refs[-4:]
+    refs = refs[:-4]
+    indices = index_loads(
+        (far_sends_ref, far_rows_ref, far_counts_ref), (sends_ref, rows_ref, counts_ref), index_sems
+    )
+    for load in indices:
+        load.wait()
     att_ref, qg_ref, acc_ref = refs[:3]
-    back_refs, refs = refs[3 : 3 + LEVELS], refs[3 + LEVELS :]
-    far_ref, back_ref, staged, sems, back_sems = refs[0], refs[1], refs[2:4], refs[4], refs[5]
+    back_refs, refs = refs[3 : 3 + len(levels)], refs[3 + len(levels) :]
+    held, staged, sems, back_sems = refs[: len(levels)], refs[-4:-2], refs[-2], refs[-1]
     outs = lambda i: row_copies(i, staged, (att_ref, qg_ref), sems)
-    backs = [
-        pltpu.make_async_copy(back_ref.at[b * PART : (b + 1) * PART, :], back_refs[b], back_sems.at[b])
-        for b in range(LEVELS)
-    ]
-    for b in range(LEVELS):
-        far_ref[b * PART : (b + 1) * PART, :] = recv_refs[b][...]
-
-    def step(t, carry):
-        blocks = []
-        for u in range(unroll):
-            e = t * unroll + u
-            i = sends_ref[e // SEND, e % SEND]
+    backs = [pltpu.make_async_copy(x, y, back_sems.at[n]) for n, (x, y) in enumerate(zip(held, back_refs))]
+    blocks, ready = [], {}
+    for n, b in enumerate(levels):
+        for s in range(SEND):
+            i = sends_ref[b, s]
             at = [rows_of(rows_ref[i, j]) if j != 1 else None for j in range(NNB)]
-            far = (far_ref.at[rows_of(e), :], back_ref.at[rows_of(e), :])
+            place = slice(s * BLK, (s + 1) * BLK)
+            far = (recv_refs[n].at[place, :], held[n].at[place, :])
             live = counts_ref[i] > NNB - 1
             blocks.append(staged_block(i, live, at, far, q_ref, g_ref, own_ref, acc_ref, staged, outs))
-        run_staged(blocks)
-        for b in range(LEVELS):
-            pl.when(t == ((b + 1) * SEND - 1) // unroll)(backs[b].start)
-        return carry
-
-    lax.fori_loop(0, LEVELS * SEND // unroll, step, 0)
-
-    def settle(e, carry):
-        for copy in outs(sends_ref[e // SEND, e % SEND]):
-            copy.wait()
-        return carry
-
-    lax.fori_loop(0, LEVELS * SEND, settle, 0)
+        ready[len(blocks) - 1] = backs[n]
+    run_staged(blocks, ready)
+    for b in levels:
+        for s in range(SEND):
+            for copy in outs(sends_ref[b, s]):
+                copy.wait()
     for copy in backs:
         copy.wait()
 
 
-def outer(sends, rows, counts, q, g, own, recv, done):
-    far = (LEVELS * PART, 2 * WIDE)
-    return pl.pallas_call(
-        functools.partial(outer_kernel, 10),
+def outer(levels, sends, rows, counts, q, g, own, recv, done):
+    recv = [recv[b] for b in levels]
+    return pl.pallas_call(
+        functools.partial(outer_kernel, levels),
         out_shape=[
             pltpu.HBM((OWN, WIDE), BF16),
             pltpu.HBM((OWN, WIDE), BF16),
             pltpu.VMEM((OWN, 2 * WIDE), F32),
         ]
-        + [pltpu.HBM((PART, 2 * WIDE), BF16)] * LEVELS,
-        in_specs=[SM] * 3 + [VM] * (3 + LEVELS) + [HB, HB, VM],
-        out_specs=[HB, HB, VM] + [HB] * LEVELS,
-        scratch_shapes=[pltpu.VMEM(far, BF16), pltpu.VMEM(far, BF16)]
+        + [pltpu.HBM((PART, 2 * WIDE), BF16)] * len(levels),
+        in_specs=[HB] * 3 + [VM] * (3 + len(levels)) + [HB, HB, VM],
+        out_specs=[HB, HB, VM] + [HB] * len(levels),
+        scratch_shapes=[pltpu.VMEM((PART, 2 * WIDE), BF16)] * len(levels)
         + [pltpu.VMEM((OWN, WIDE), BF16)] * 2
-        + [pltpu.SemaphoreType.DMA((2, NBLK)), pltpu.SemaphoreType.DMA((LEVELS,))],
-        input_output_aliases={6 + LEVELS + n: n for n in range(3)},
+        + [pltpu.SemaphoreType.DMA((2, NBLK)), pltpu.SemaphoreType.DMA((len(levels),))]
+        + index_scratch(sends, rows, counts),
+        input_output_aliases={6 + len(levels) + n: n for n in range(3)},
         compiler_params=limits(16),
-        cost_estimate=pl.CostEstimate(flops=8 * 10**9, bytes_accessed=8 * 2**20, transcendentals=2 * 10**6),
+        cost_estimate=pl.CostEstimate(flops=4 * 10**9, bytes_accessed=4 * 2**20, transcendentals=10**6),
         name="attend_outer",
-    )(sends, rows, counts, q, g, own, *recv, *done)
-
-
-def join_kernel(sends_ref, acc_ref, *refs):
+    )(*in_hbm(sends, rows, counts), q, g, own, *recv, *done)
+
+
+def join_kernel(far_sends_ref, acc_ref, *refs):
+    sends_ref, index_sems = refs[-2:]
+    (index,) = index_loads((far_sends_ref,), (sends_ref,), index_sems)
     arrived_refs = refs[:LEVELS]
     key_ref, value_ref = refs[LEVELS : LEVELS + 2]
     key_ref[...] = acc_ref[:, :WIDE].astype(BF16)
     value_ref[...] = acc_ref[:, WIDE:].astype(BF16)
+    index.wait()
     for b in range(LEVELS):
         for s in range(SEND):
             at = rows_of(sends_ref[b, s])
@@ -315,12 +339,13 @@
     return pl.pallas_call(
         join_kernel,
         out_shape=[jax.ShapeDtypeStruct((OWN, WIDE), BF16)] * 2,
-        in_specs=[SM] + [VM] * (1 + LEVELS),
+        in_specs=[HB] + [VM] * (1 + LEVELS),
         out_specs=[VM] * 2,
+        scratch_shapes=index_scratch(sends),
         compiler_params=limits(10),
         cost_estimate=pl.CostEstimate(flops=10**6, bytes_accessed=4 * 2**20, transcendentals=0),
         name="join_gradients",
-    )(sends, acc, *arrived)
+    )(*in_hbm(sends), acc, *arrived)
 
 
 def body(query_rows, key_rows, value_rows, out_grad, boundary_send_blocks, neighbours, live_count):
@@ -340,7 +365,8 @@
     q = lax.all_to_all(q, "head", 0, 0, tiled=True).reshape(OWN, WIDE)
     recv = [swapped(outgoing[b], b) for b in range(LEVELS)]
     *done, own, grad = inner(rows, counts, q, out_grad, own)
-    attended, query_grad, acc, *back = outer(sends, rows, counts, q, grad, own, recv, done)
+    levels = tuple(range(LEVELS))
+    attended, query_grad, acc, *back = outer(levels, sends, rows, counts, q, grad, own, recv, done)
     arrived = [swapped(back[b], b) for b in range(LEVELS)]
     attended = lax.all_to_all(attended.reshape(heads, mine, WIDE), "head", 0, 0, tiled=True)
     attended = attended.transpose(1, 0, 2).reshape(mine, heads * WIDE)

time: 80.1 us -> 80.7 us (level)
  local copies, waits for them, and re-layouts: 5.41 us -> 7.12 us
  Pallas kernels: 22.9 us -> 21.5 us
    pallas_call x1, Pallas kernels: 7.71 us -> 6.74 us  [inner(): pl.pallas_call(functools.partial(inner_kernel, 12), out_shape=[pltpu.HBM(...]
  transfers between devices with their start and end apart: 19 -> 19, of which waited for: 4 -> 3; matrix products, arithmetic and copies ran while one was open for 7% -> 9% of each run, Pallas kernels for 10% -> 8%
where the time goes in v5:
time: 80.7 us; the launch traced here: 79.8 us
  starting transfers between devices  42.9 us (53%)
  Pallas kernels  21.5 us (27%)
  waiting for transfers between devices  7.34 us (9%)
  local copies, waits for them, and re-layouts  7.12 us (9%)
  between operations  0.9 us (1%)
    ppermute x10, starting transfers between devices, swapped(): return lax.ppermute(block, 'pix', route)  22.5 us
    pallas_call x1, Pallas kernels, outer(): pl.pallas_call(functools.partial(outer_kernel, levels), out_shape=[pltpu....  9.71 us
    ppermute x7, starting transfers between devices, shifted(): return lax.ppermute(block, 'head', route)  8.47 us
    all_to_all x1, starting transfers between devices, body(): q = lax.all_to_all(q, 'head', 0, 0, tiled=True).reshape(OWN, WIDE)  7.12 us
    pallas_call x1, Pallas kernels, inner(): pl.pallas_call(functools.partial(inner_kernel, 12), out_shape=[pltpu.HBM(...  6.74 us
    all_to_all x1, starting transfers between devices, body(): lax.all_to_all(attended.reshape(heads, mine, WIDE), 'head', 0, 0, tiled=T...  4.81 us
    ppermute x10, waiting for transfers between devices, swapped(): return lax.ppermute(block, 'pix', route)  4.67 us
    ppermute x7, waiting for transfers between devices, shifted(): return lax.ppermute(block, 'head', route)  2.67 us
  transfers between devices with their start and end apart: 19, of which 3 were waited for; matrix products, arithmetic and copies ran while one was open for 9% of the time, Pallas kernels for 8%

profile of v5, /device:TPU:8, one launch (start us, length us, event | category | flops | bytes accessed | tf_op | source)
XLA Modules:
  0.0 79.8 jit_solution(6810841561582251563)
XLA Ops:
  0.6 0.0 copy-start
  0.6 1.5 %split_keys_values.1 = (bf16[256,256]{1,0:T(8,128)(2,1)S(1)}, bf16[256,256]{1,0:T(8,128)(2,1)S(1)}, bf16[256,256]{1,0:T(8,128)(2,1)S(1)}, bf16[256,256]{1,0:T(8,...) custom-call(bf16[256,1024]{1,0:T(8,128)(2,1)} %key_ref.1, ...), custom_call_target="tpu_custom_call" | custom-call | bytes 2097152 | tf_op jit(solution)/shard_map/split_keys_values/pallas_call | solution.py:73
  2.1 1.7 %collective-permute-start = (bf16[256,256]{1,0:T(8,128)(2,1)S(1)}, bf16[256,256]{1,0:T(8,128)(2,1)S(1)}, u32[]{:S(2)}, u32[]{:S(2)}) collective-permute-start(bf16[256,256]{1,0:T(8,128)(2,1)S(1)} %get-tuple-element.40), channel_id=1, source_target_pairs={{0,2},{1,3},{2,4},{3,5},{4,6},{5,7},{6,0},{7,1},{8,10},{9,11},{10,... | collective-permute-start | bytes 393224 | tf_op jit(solution)/shard_map/ppermute | solution.py:46
  3.8 0.7 collective-permute-start.1
  4.5 0.2 collective-permute-start.2
  4.7 1.5 %collective-permute-start.3 = (bf16[256,256]{1,0:T(8,128)(2,1)S(1)}, bf16[256,256]{1,0:T(8,128)(2,1)S(1)}, u32[]{:S(2)}, u32[]{:S(2)}) collective-permute-start(bf16[256,256]{1,0:T(8,128)(2,1)S(1)} %get-tuple-element.46), channel_id=1, source_target_pairs={{0,7},{1,6},{2,1},{3,0},{4,3},{5,2},{6,5},{7,4},{8,15},{9,14},{10,... | collective-permute-start | bytes 393224 | tf_op jit(solution)/shard_map/ppermute | solution.py:46
  6.2 2.0 %collective-permute-start.4 = (bf16[256,256]{1,0:T(8,128)(2,1)S(1)}, bf16[256,256]{1,0:T(8,128)(2,1)S(1)}, u32[]{:S(2)}, u32[]{:S(2)}) collective-permute-start(bf16[256,256]{1,0:T(8,128)(2,1)S(1)} %get-tuple-element.47), channel_id=1, source_target_pairs={{0,4},{1,5},{2,6},{3,7},{4,0},{5,1},{6,2},{7,3},{8,12},{9,13},{10,... | collective-permute-start | bytes 393224 | tf_op jit(solution)/shard_map/ppermute | solution.py:46
  8.3 0.8 constant_dynamic-slice_fusion
  9.0 1.3 %dynamic_slice.12.far_counts_ref = s32[32]{0:T(128)} dynamic-slice(s32[1024]{0:T(1024)} %param.13, s32[]{:T(128)S(6)} %select_n.9), dynamic_slice_sizes={32} | dynamic-slice | bytes 260 | tf_op jit(solution)/shard_map/dynamic_slice | solution.py:357
  10.3 0.7 copy.21.far_rows_ref
  11.0 0.8 constant_dynamic-slice_fusion.1
  11.8 0.1 copy.14
  11.9 0.7 copy.18.far_sends_ref
  12.6 0.0 collective-permute-done.refs_0_
  12.6 2.3 %collective-permute-start.5 = (bf16[256,256]{1,0:T(8,128)(2,1)S(1)}, bf16[256,256]{1,0:T(8,128)(2,1)S(1)}, u32[]{:S(2)}, u32[]{:S(2)}) collective-permute-start(bf16[256,256]{1,0:T(8,128)(2,1)S(1)} %get-tuple-element.48), channel_id=1, source_target_pairs={{0,5},{1,4},{2,7},{3,6},{4,1},{5,0},{6,3},{7,2},{8,13},{9,12},{10,... | collective-permute-start | bytes 393224 | tf_op jit(solution)/shard_map/ppermute | solution.py:46
  14.9 0.0 collective-permute-done.1.refs_1_
  14.9 0.0 collective-permute-start.6
  14.9 0.0 copy-done
  14.9 0.9 %bitcast_bitcast_fusion = bf16[8,256,128]{2,1,0:T(8,128)(2,1)} fusion(bf16[256,1024]{1,0:T(8,128)(2,1)S(1)} %copy-done), kind=kLoop, calls=%fused_computation.1 | loop fusion | bytes 1048576 | tf_op jit(solution)/shard_map/transpose | solution.py:361
  15.8 0.0 collective-permute-done.2.refs_2_
  15.8 0.0 collective-permute-done.3.refs_3_
  15.8 0.0 collective-permute-done.4.refs_4_
  15.8 2.7 %collective-permute-done.5.refs_5_ = bf16[256,256]{1,0:T(8,128)(2,1)S(1)} collective-permute-done((bf16[256,256]{1,0:T(8,128)(2,1)S(1)}, bf16[256,256]{1,0:T(8,128)(2,1)S(1)}, u32[]{:S(2)}, u32[]{:S(2)}) %collective-permute-start.5) | collective-permute-done | bytes 131104 | tf_op jit(solution)/shard_map/ppermute | solution.py:46
  18.5 0.0 collective-permute-done.6.refs_6_
  18.5 1.8 %pick_boundary.1 = (bf16[2048,256]{1,0:T(8,128)(2,1)}, bf16[256,256]{1,0:T(8,128)(2,1)}, bf16[256,256]{1,0:T(8,128)(2,1)}, bf16[256,256]{1,0:T(8,128)(2,1)}, bf1...) custom-call(s32[5,4]{1,0:T(8,128)} %copy.18.far_sends_ref, bf16[256,256]{1,0:T(8,128)(2,1)S(1)} %collective-permute-done.refs_0_, ...), custom_call_target="tpu_custom_call" | custom-call | bytes 4194304 | tf_op jit(solution)/shard_map/pick_boundary/pallas_call | solution.py:123
  20.3 7.1 %all-to-all-start = ((bf16[8,256,128]{2,1,0:T(8,128)(2,1)}), bf16[8,256,128]{2,1,0:T(8,128)(2,1)S(1)}, u32[]{:S(2)}, u32[]{:S(2)}) async-start(bf16[8,256,128]{2,1,0:T(8,128)(2,1)} %bitcast_bitcast_fusion), calls=%async_computation | async-start | bytes 1048576 | tf_op jit(solution)/shard_map/all_to_all | solution.py:365
  27.5 0.9 %collective-permute-start.7 = (bf16[256,256]{1,0:T(8,128)(2,1)}, bf16[256,256]{1,0:T(8,128)(2,1)S(1)}, u32[]{:S(2)}, u32[]{:S(2)}) collective-permute-start(bf16[256,256]{1,0:T(8,128)(2,1)} %get-tuple-element.56), channel_id=1, source_target_pairs={{0,8},{8,0},{16,24},{24,16},{32,40},{40,32},{48,56},{56,48},{64,72... | collective-permute-start | bytes 393224 | tf_op jit(solution)/shard_map/ppermute | solution.py:32
  28.4 3.3 %collective-permute-start.8 = (bf16[256,256]{1,0:T(8,128)(2,1)}, bf16[256,256]{1,0:T(8,128)(2,1)}, u32[]{:S(2)}, u32[]{:S(2)}) collective-permute-start(bf16[256,256]{1,0:T(8,128)(2,1)} %get-tuple-element.57), channel_id=1, source_target_pairs={{0,16},{8,24},{16,0},{24,8},{32,48},{40,56},{48,32},{56,40},{64,80... | collective-permute-start | bytes 393224 | tf_op jit(solution)/shard_map/ppermute | solution.py:32
  31.6 4.5 %collective-permute-start.9 = (bf16[256,256]{1,0:T(8,128)(2,1)}, bf16[256,256]{1,0:T(8,128)(2,1)}, u32[]{:S(2)}, u32[]{:S(2)}) collective-permute-start(bf16[256,256]{1,0:T(8,128)(2,1)} %get-tuple-element.58), channel_id=1, source_target_pairs={{0,32},{8,40},{16,48},{24,56},{32,0},{40,8},{48,16},{56,24},{64,96... | collective-permute-start | bytes 393224 | tf_op jit(solution)/shard_map/ppermute | solution.py:32
  36.1 1.5 %collective-permute-start.10 = (bf16[256,256]{1,0:T(8,128)(2,1)S(1)}, bf16[256,256]{1,0:T(8,128)(2,1)}, u32[]{:S(2)}, u32[]{:S(2)}) collective-permute-start(bf16[256,256]{1,0:T(8,128)(2,1)S(1)} %get-tuple-element.59), channel_id=1, source_target_pairs={{0,64},{8,72},{16,80},{24,88},{32,96},{40,104},{48,112},{56,120},{... | collective-permute-start | bytes 393224 | tf_op jit(solution)/shard_map/ppermute | solution.py:32
  37.6 2.7 %collective-permute-start.11 = (bf16[256,256]{1,0:T(8,128)(2,1)S(1)}, bf16[256,256]{1,0:T(8,128)(2,1)}, u32[]{:S(2)}, u32[]{:S(2)}) collective-permute-start(bf16[256,256]{1,0:T(8,128)(2,1)S(1)} %get-tuple-element.60), channel_id=1, source_target_pairs={{0,128},{8,136},{16,144},{24,152},{32,160},{40,168},{48,176},{56,1... | collective-permute-start | bytes 393224 | tf_op jit(solution)/shard_map/ppermute | solution.py:32
  40.4 0.0 all-to-all-done
  40.4 6.7 %attend_inner.1 = (bf16[2048,128]{1,0:T(8,128)(2,1)}, bf16[2048,128]{1,0:T(8,128)(2,1)}, f32[2048,256]{1,0:T(8,128)S(1)}, bf16[2048,256]{1,0:T(8,128)(2,1)S(1)}, bf16[2048,128]{1,0:T(8,128)(2,1)S(1)}) custom-call(s32[32,9]{1,0:T(8,128)} %copy.21.far_rows_ref, s32[32]{0:T(128)} %dynamic_slice.12.far_counts_ref, bf16[2048,128]{1,0:T(8,128)(2,1)S(1)} %bitcast.16, ...), custom_call_target="tpu_custom_call" | custom-call | flops 4000000000 | bytes 8388608 | tf_op jit(solution)/shard_map/attend_inner/pallas_call | solution.py:245
  47.1 0.0 collective-permute-done.7.refs_0_
  47.1 0.0 collective-permute-done.8.refs_1_
  47.1 0.0 collective-permute-done.9.refs_2_
  47.1 0.0 collective-permute-done.10.refs_3_
  47.2 0.0 collective-permute-done.11.refs_4_
  47.2 9.7 %attend_outer.1 = (bf16[2048,128]{1,0:T(8,128)(2,1)}, bf16[2048,128]{1,0:T(8,128)(2,1)}, f32[2048,256]{1,0:T(8,128)S(1)}, bf16[256,256]{1,0:T(8,128)(2,1)}, bf16...) custom-call(s32[5,4]{1,0:T(8,128)} %copy.18.far_sends_ref, ...), custom_call_target="tpu_custom_call", output_to_operand_aliasing={{0}: (11, {}), {1}: (12, {}), {2}: (13, {})} | custom-call | flops 4000000000 | bytes 4194304 | tf_op jit(solution)/shard_map/attend_outer/pallas_call | solution.py:301
  56.9 4.8 %all-to-all-start.1 = ((bf16[8,256,128]{2,1,0:T(8,128)(2,1)}), bf16[8,256,128]{2,1,0:T(8,128)(2,1)}, u32[]{:S(2)}, u32[]{:S(2)}) async-start(bf16[8,256,128]{2,1,0:T(8,128)(2,1)} %bitcast.18), calls=%async_computation.1 | async-start | bytes 1048576 | tf_op jit(solution)/shard_map/all_to_all | solution.py:371
  61.7 1.0 %collective-permute-start.12 = (bf16[256,256]{1,0:T(8,128)(2,1)}, bf16[256,256]{1,0:T(8,128)(2,1)S(1)}, u32[]{:S(2)}, u32[]{:S(2)}) collective-permute-start(bf16[256,256]{1,0:T(8,128)(2,1)} %get-tuple-element.65), channel_id=1, source_target_pairs={{0,8},{8,0},{16,24},{24,16},{32,40},{40,32},{48,56},{56,48},{64,72... | collective-permute-start | bytes 393224 | tf_op jit(solution)/shard_map/ppermute | solution.py:32
  62.7 1.4 %collective-permute-start.13 = (bf16[256,256]{1,0:T(8,128)(2,1)}, bf16[256,256]{1,0:T(8,128)(2,1)S(1)}, u32[]{:S(2)}, u32[]{:S(2)}) collective-permute-start(bf16[256,256]{1,0:T(8,128)(2,1)} %get-tuple-element.70), channel_id=1, source_target_pairs={{0,16},{8,24},{16,0},{24,8},{32,48},{40,56},{48,32},{56,40},{64,80... | collective-permute-start | bytes 393224 | tf_op jit(solution)/shard_map/ppermute | solution.py:32
  64.2 2.9 %collective-permute-start.14 = (bf16[256,256]{1,0:T(8,128)(2,1)}, bf16[256,256]{1,0:T(8,128)(2,1)S(1)}, u32[]{:S(2)}, u32[]{:S(2)}) collective-permute-start(bf16[256,256]{1,0:T(8,128)(2,1)} %get-tuple-element.71), channel_id=1, source_target_pairs={{0,32},{8,40},{16,48},{24,56},{32,0},{40,8},{48,16},{56,24},{64,96... | collective-permute-start | bytes 393224 | tf_op jit(solution)/shard_map/ppermute | solution.py:32
  67.0 1.5 %collective-permute-start.15 = (bf16[256,256]{1,0:T(8,128)(2,1)}, bf16[256,256]{1,0:T(8,128)(2,1)S(1)}, u32[]{:S(2)}, u32[]{:S(2)}) collective-permute-start(bf16[256,256]{1,0:T(8,128)(2,1)} %get-tuple-element.72), channel_id=1, source_target_pairs={{0,64},{8,72},{16,80},{24,88},{32,96},{40,104},{48,112},{56,120},{... | collective-permute-start | bytes 393224 | tf_op jit(solution)/shard_map/ppermute | solution.py:32
  68.5 2.7 %collective-permute-start.16 = (bf16[256,256]{1,0:T(8,128)(2,1)}, bf16[256,256]{1,0:T(8,128)(2,1)S(1)}, u32[]{:S(2)}, u32[]{:S(2)}) collective-permute-start(bf16[256,256]{1,0:T(8,128)(2,1)} %get-tuple-element.73), channel_id=1, source_target_pairs={{0,128},{8,136},{16,144},{24,152},{32,160},{40,168},{48,176},{56,1... | collective-permute-start | bytes 393224 | tf_op jit(solution)/shard_map/ppermute | solution.py:32
  71.3 0.0 all-to-all-done.1
  71.3 1.9 %copy_bitcast_fusion = bf16[256,1024]{1,0:T(8,128)(2,1)} fusion(bf16[8,256,128]{2,1,0:T(8,128)(2,1)} %all-to-all-done.1), kind=kLoop, calls=%fused_computation | loop fusion | bytes 1048576 | tf_op jit(solution)/shard_map/reshape | solution.py:372
  73.2 0.0 collective-permute-done.12.refs_0_
  73.2 4.4 %collective-permute-done.13.refs_1_ = bf16[256,256]{1,0:T(8,128)(2,1)S(1)} collective-permute-done((bf16[256,256]{1,0:T(8,128)(2,1)}, bf16[256,256]{1,0:T(8,128)(2,1)S(1)}, u32[]{:S(2)}, u32[]{:S(2)}) %collective-permute-start.13) | collective-permute-done | bytes 131104 | tf_op jit(solution)/shard_map/ppermute | solution.py:32
  77.6 0.3 collective-permute-done.14.refs_2_
  77.8 0.0 collective-permute-done.15.refs_3_
  77.8 0.0 collective-permute-done.16.refs_4_
  77.8 1.8 %join_gradients.1 = (bf16[2048,128]{1,0:T(8,128)(2,1)}, bf16[2048,128]{1,0:T(8,128)(2,1)}) custom-call(s32[5,4]{1,0:T(8,128)} %copy.18.far_sends_ref, f32[2048,256]{1,0:T(8,128)S(1)} %get-tuple-element.68.acc_ref, bf16[256,256]{1,0:T(8,128)(2,1)S(1)} %collective-permute-done.12.refs_0_, bf16[256,256]{1,0:T(8,128)(2,1)S(1)} %collective-permute-done.13.refs_1_, ...), custom_call_target="tpu_custom_call" | custom-call | flops 1000000 | bytes 4194304 | tf_op jit(solution)/shard_map/join_gradients/pallas_call | solution.py:339
Async XLA Ops:
  0.6 14.3 %copy-start = (bf16[256,1024]{1,0:T(8,128)(2,1)S(1)}, bf16[256,1024]{1,0:T(8,128)(2,1)}, u32[]{:S(2)}) copy-start(bf16[256,1024]{1,0:T(8,128)(2,1)} %param.7) | copy-start | bytes 1572868
  2.1 10.5 %collective-permute-start = (bf16[256,256]{1,0:T(8,128)(2,1)S(1)}, bf16[256,256]{1,0:T(8,128)(2,1)S(1)}, u32[]{:S(2)}, u32[]{:S(2)}) collective-permute-start(bf16[256,256]{1,0:T(8,128)(2,1)S(1)} %get-tuple-element.40), channel_id=1, source_target_pairs={{0,2},{1,3},{2,4},{3,5},{4,6},{5,7},{6,0},{7,1},{8,10},{9,11},{10,... | collective-permute-start | bytes 393224 | tf_op jit(solution)/shard_map/ppermute | solution.py:46
  3.8 11.1 %collective-permute-start.1 = (bf16[256,256]{1,0:T(8,128)(2,1)S(1)}, bf16[256,256]{1,0:T(8,128)(2,1)S(1)}, u32[]{:S(2)}, u32[]{:S(2)}) collective-permute-start(bf16[256,256]{1,0:T(8,128)(2,1)S(1)} %get-tuple-element.44), channel_id=1, source_target_pairs={{0,6},{1,7},{2,0},{3,1},{4,2},{5,3},{6,4},{7,5},{8,14},{9,15},{10,... | collective-permute-start | bytes 393224 | tf_op jit(solution)/shard_map/ppermute | solution.py:46
  4.5 11.3 %collective-permute-start.2 = (bf16[256,256]{1,0:T(8,128)(2,1)S(1)}, bf16[256,256]{1,0:T(8,128)(2,1)S(1)}, u32[]{:S(2)}, u32[]{:S(2)}) collective-permute-start(bf16[256,256]{1,0:T(8,128)(2,1)S(1)} %get-tuple-element.45), channel_id=1, source_target_pairs={{0,3},{1,2},{2,5},{3,4},{4,7},{5,6},{6,1},{7,0},{8,11},{9,10},{10,... | collective-permute-start | bytes 393224 | tf_op jit(solution)/shard_map/ppermute | solution.py:46
  4.7 11.1 %collective-permute-start.3 = (bf16[256,256]{1,0:T(8,128)(2,1)S(1)}, bf16[256,256]{1,0:T(8,128)(2,1)S(1)}, u32[]{:S(2)}, u32[]{:S(2)}) collective-permute-start(bf16[256,256]{1,0:T(8,128)(2,1)S(1)} %get-tuple-element.46), channel_id=1, source_target_pairs={{0,7},{1,6},{2,1},{3,0},{4,3},{5,2},{6,5},{7,4},{8,15},{9,14},{10,... | collective-permute-start | bytes 393224 | tf_op jit(solution)/shard_map/ppermute | solution.py:46
  6.2 9.6 %collective-permute-start.4 = (bf16[256,256]{1,0:T(8,128)(2,1)S(1)}, bf16[256,256]{1,0:T(8,128)(2,1)S(1)}, u32[]{:S(2)}, u32[]{:S(2)}) collective-permute-start(bf16[256,256]{1,0:T(8,128)(2,1)S(1)} %get-tuple-element.47), channel_id=1, source_target_pairs={{0,4},{1,5},{2,6},{3,7},{4,0},{5,1},{6,2},{7,3},{8,12},{9,13},{10,... | collective-permute-start | bytes 393224 | tf_op jit(solution)/shard_map/ppermute | solution.py:46
  12.6 5.9 %collective-permute-start.5 = (bf16[256,256]{1,0:T(8,128)(2,1)S(1)}, bf16[256,256]{1,0:T(8,128)(2,1)S(1)}, u32[]{:S(2)}, u32[]{:S(2)}) collective-permute-start(bf16[256,256]{1,0:T(8,128)(2,1)S(1)} %get-tuple-element.48), channel_id=1, source_target_pairs={{0,5},{1,4},{2,7},{3,6},{4,1},{5,0},{6,3},{7,2},{8,13},{9,12},{10,... | collective-permute-start | bytes 393224 | tf_op jit(solution)/shard_map/ppermute | solution.py:46
  14.9 3.6 %collective-permute-start.6 = (bf16[256,256]{1,0:T(8,128)(2,1)S(1)}, bf16[256,256]{1,0:T(8,128)(2,1)S(1)}, u32[]{:S(2)}, u32[]{:S(2)}) collective-permute-start(bf16[256,256]{1,0:T(8,128)(2,1)S(1)} %get-tuple-element.49), channel_id=1, source_target_pairs={{0,1},{1,0},{2,3},{3,2},{4,5},{5,4},{6,7},{7,6},{8,9},{9,8},{10,11... | collective-permute-start | bytes 393224 | tf_op jit(solution)/shard_map/ppermute | solution.py:46
  20.3 20.0 %all-to-all-start = ((bf16[8,256,128]{2,1,0:T(8,128)(2,1)}), bf16[8,256,128]{2,1,0:T(8,128)(2,1)S(1)}, u32[]{:S(2)}, u32[]{:S(2)}) async-start(bf16[8,256,128]{2,1,0:T(8,128)(2,1)} %bitcast_bitcast_fusion), calls=%async_computation | async-start | bytes 1048576 | tf_op jit(solution)/shard_map/all_to_all | solution.py:365
  27.5 19.6 %collective-permute-start.7 = (bf16[256,256]{1,0:T(8,128)(2,1)}, bf16[256,256]{1,0:T(8,128)(2,1)S(1)}, u32[]{:S(2)}, u32[]{:S(2)}) collective-permute-start(bf16[256,256]{1,0:T(8,128)(2,1)} %get-tuple-element.56), channel_id=1, source_target_pairs={{0,8},{8,0},{16,24},{24,16},{32,40},{40,32},{48,56},{56,48},{64,72... | collective-permute-start | bytes 393224 | tf_op jit(solution)/shard_map/ppermute | solution.py:32
  28.4 18.7 %collective-permute-start.8 = (bf16[256,256]{1,0:T(8,128)(2,1)}, bf16[256,256]{1,0:T(8,128)(2,1)}, u32[]{:S(2)}, u32[]{:S(2)}) collective-permute-start(bf16[256,256]{1,0:T(8,128)(2,1)} %get-tuple-element.57), channel_id=1, source_target_pairs={{0,16},{8,24},{16,0},{24,8},{32,48},{40,56},{48,32},{56,40},{64,80... | collective-permute-start | bytes 393224 | tf_op jit(solution)/shard_map/ppermute | solution.py:32
  31.6 15.5 %collective-permute-start.9 = (bf16[256,256]{1,0:T(8,128)(2,1)}, bf16[256,256]{1,0:T(8,128)(2,1)}, u32[]{:S(2)}, u32[]{:S(2)}) collective-permute-start(bf16[256,256]{1,0:T(8,128)(2,1)} %get-tuple-element.58), channel_id=1, source_target_pairs={{0,32},{8,40},{16,48},{24,56},{32,0},{40,8},{48,16},{56,24},{64,96... | collective-permute-start | bytes 393224 | tf_op jit(solution)/shard_map/ppermute | solution.py:32
  36.1 11.0 %collective-permute-start.10 = (bf16[256,256]{1,0:T(8,128)(2,1)S(1)}, bf16[256,256]{1,0:T(8,128)(2,1)}, u32[]{:S(2)}, u32[]{:S(2)}) collective-permute-start(bf16[256,256]{1,0:T(8,128)(2,1)S(1)} %get-tuple-element.59), channel_id=1, source_target_pairs={{0,64},{8,72},{16,80},{24,88},{32,96},{40,104},{48,112},{56,120},{... | collective-permute-start | bytes 393224 | tf_op jit(solution)/shard_map/ppermute | solution.py:32
  37.6 9.5 %collective-permute-start.11 = (bf16[256,256]{1,0:T(8,128)(2,1)S(1)}, bf16[256,256]{1,0:T(8,128)(2,1)}, u32[]{:S(2)}, u32[]{:S(2)}) collective-permute-start(bf16[256,256]{1,0:T(8,128)(2,1)S(1)} %get-tuple-element.60), channel_id=1, source_target_pairs={{0,128},{8,136},{16,144},{24,152},{32,160},{40,168},{48,176},{56,1... | collective-permute-start | bytes 393224 | tf_op jit(solution)/shard_map/ppermute | solution.py:32
  56.9 14.4 %all-to-all-start.1 = ((bf16[8,256,128]{2,1,0:T(8,128)(2,1)}), bf16[8,256,128]{2,1,0:T(8,128)(2,1)}, u32[]{:S(2)}, u32[]{:S(2)}) async-start(bf16[8,256,128]{2,1,0:T(8,128)(2,1)} %bitcast.18), calls=%async_computation.1 | async-start | bytes 1048576 | tf_op jit(solution)/shard_map/all_to_all | solution.py:371
  61.7 11.5 %collective-permute-start.12 = (bf16[256,256]{1,0:T(8,128)(2,1)}, bf16[256,256]{1,0:T(8,128)(2,1)S(1)}, u32[]{:S(2)}, u32[]{:S(2)}) collective-permute-start(bf16[256,256]{1,0:T(8,128)(2,1)} %get-tuple-element.65), channel_id=1, source_target_pairs={{0,8},{8,0},{16,24},{24,16},{32,40},{40,32},{48,56},{56,48},{64,72... | collective-permute-start | bytes 393224 | tf_op jit(solution)/shard_map/ppermute | solution.py:32
  62.7 14.9 %collective-permute-start.13 = (bf16[256,256]{1,0:T(8,128)(2,1)}, bf16[256,256]{1,0:T(8,128)(2,1)S(1)}, u32[]{:S(2)}, u32[]{:S(2)}) collective-permute-start(bf16[256,256]{1,0:T(8,128)(2,1)} %get-tuple-element.70), channel_id=1, source_target_pairs={{0,16},{8,24},{16,0},{24,8},{32,48},{40,56},{48,32},{56,40},{64,80... | collective-permute-start | bytes 393224 | tf_op jit(solution)/shard_map/ppermute | solution.py:32
  64.2 13.7 %collective-permute-start.14 = (bf16[256,256]{1,0:T(8,128)(2,1)}, bf16[256,256]{1,0:T(8,128)(2,1)S(1)}, u32[]{:S(2)}, u32[]{:S(2)}) collective-permute-start(bf16[256,256]{1,0:T(8,128)(2,1)} %get-tuple-element.71), channel_id=1, source_target_pairs={{0,32},{8,40},{16,48},{24,56},{32,0},{40,8},{48,16},{56,24},{64,96... | collective-permute-start | bytes 393224 | tf_op jit(solution)/shard_map/ppermute | solution.py:32
  67.0 10.8 %collective-permute-start.15 = (bf16[256,256]{1,0:T(8,128)(2,1)}, bf16[256,256]{1,0:T(8,128)(2,1)S(1)}, u32[]{:S(2)}, u32[]{:S(2)}) collective-permute-start(bf16[256,256]{1,0:T(8,128)(2,1)} %get-tuple-element.72), channel_id=1, source_target_pairs={{0,64},{8,72},{16,80},{24,88},{32,96},{40,104},{48,112},{56,120},{... | collective-permute-start | bytes 393224 | tf_op jit(solution)/shard_map/ppermute | solution.py:32
  68.5 9.3 %collective-permute-start.16 = (bf16[256,256]{1,0:T(8,128)(2,1)}, bf16[256,256]{1,0:T(8,128)(2,1)S(1)}, u32[]{:S(2)}, u32[]{:S(2)}) collective-permute-start(bf16[256,256]{1,0:T(8,128)(2,1)} %get-tuple-element.73), channel_id=1, source_target_pairs={{0,128},{8,136},{16,144},{24,152},{32,160},{40,168},{48,176},{56,1... | collective-permute-start | bytes 393224 | tf_op jit(solution)/shard_map/ppermute | solution.py:32

commit v6 on v5

--- a/solution.py
+++ b/solution.py
@@ -17,6 +17,7 @@
 PART = SEND * BLK
 FILL = -1e30
 CHUNKS = 8
+LANES = 128
 HEAD_DEVICES = 8
 OFFSETS = ((1, 0), (3, 0), (1, 1), (3, 1), (2, 0), (2, 1), (0, 1), (0, 0))
 F32 = jnp.float32
@@ -82,26 +83,57 @@
     )(pltpu.with_memory_space_constraint(keys, pltpu.HBM), pltpu.with_memory_space_constraint(values, pltpu.HBM))
 
 
-def index_loads(sources, targets, sems):
-    loads = [pltpu.make_async_copy(x, y, sems.at[n]) for n, (x, y) in enumerate(zip(sources, targets))]
-    for load in loads:
-        load.start()
-    return loads
+class Table:
+    def __init__(self, ref, place):
+        self.ref, self.place = ref, place
+
+    def __getitem__(self, index):
+        return self.ref[self.place(*index) if isinstance(index, tuple) else self.place(index)]
+
+
+def sends_load(whole_ref, held_ref, sem):
+    load = pltpu.make_async_copy(whole_ref, held_ref, sem)
+    load.start()
+    mine = lax.axis_index("pix")
+    return load, Table(held_ref, lambda b, s: (b, s, mine))
+
+
+def rows_load(whole_ref, held_ref, sem):
+    mine = lax.axis_index("pix")
+    per = LANES // NBLK
+    columns = pl.ds(pl.multiple_of(mine // per * LANES, LANES), LANES)
+    load = pltpu.make_async_copy(whole_ref.at[:, columns], held_ref, sem)
+    load.start()
+    return load, Table(held_ref, lambda i, j: (j, mine % per * NBLK + i))
+
+
+def counts_load(whole_ref, held_ref, sem):
+    load = pltpu.make_async_copy(whole_ref, held_ref, sem)
+    load.start()
+    mine = lax.axis_index("pix")
+    return load, Table(held_ref, lambda i: mine * NBLK + i)
+
+
+def sends_scratch(sends):
+    return [pltpu.SMEM(sends.shape, jnp.int32), pltpu.SemaphoreType.DMA]
+
+
+def block_scratch(counts):
+    return [
+        pltpu.SMEM((NNB, LANES), jnp.int32),
+        pltpu.SMEM(counts.shape, jnp.int32),
+        pltpu.SemaphoreType.DMA((2,)),
+    ]
 
 
 def in_hbm(*arrays):
     return [pltpu.with_memory_space_constraint(x, pltpu.HBM) for x in arrays]
-
-
-def index_scratch(*arrays):
-    return [pltpu.SMEM(x.shape, x.dtype) for x in arrays] + [pltpu.SemaphoreType.DMA((len(arrays),))]
 
 
 def pick_kernel(far_sends_ref, *refs):
     parts, refs = refs[:HEAD_DEVICES], refs[HEAD_DEVICES:]
     own_ref, out_refs, held_ref, sems = refs[0], refs[1 : 1 + LEVELS], refs[-4], refs[-3]
-    sends_ref, index_sems = refs[-2:]
-    (index,) = index_loads((far_sends_ref,), (sends_ref,), index_sems)
+    index, sends_ref = sends_load(far_sends_ref, *refs[-2:])
     me = lax.axis_index("head")
     mine = OWN // HEAD_DEVICES
     copies = []
@@ -126,7 +158,7 @@
         in_specs=[HB] + [VM] * HEAD_DEVICES,
         out_specs=[HB] + [VM] * LEVELS,
         scratch_shapes=[pltpu.VMEM((OWN, 2 * WIDE), BF16), pltpu.SemaphoreType.DMA((HEAD_DEVICES,))]
-        + index_scratch(sends),
+        + sends_scratch(sends),
         compiler_params=limits(8),
         cost_estimate=pl.CostEstimate(flops=0, bytes_accessed=4 * 2**20, transcendentals=0),
         name="pick_boundary",
@@ -198,8 +230,10 @@
 def inner_kernel(unroll, far_rows_ref, far_counts_ref, q_ref, far_g_ref, far_own_ref, *refs):
     att_ref, qg_ref, acc_ref, own_ref, g_ref, list_ref = refs[:6]
     staged, sems, in_sems = refs[6:8], refs[8], refs[9]
-    rows_ref, counts_ref, index_sems = refs[10:]
-    indices = index_loads((far_rows_ref, far_counts_ref), (rows_ref, counts_ref), index_sems)
+    rows_held, counts_held, index_sems = refs[10:]
+    rows_index, rows_ref = rows_load(far_rows_ref, rows_held, index_sems.at[0])
+    counts_index, counts_ref = counts_load(far_counts_ref, counts_held, index_sems.at[1])
+    indices = [rows_index, counts_index]
     loads = []
     for n, (x, y) in enumerate(((far_own_ref, own_ref), (far_g_ref, g_ref))):
         for c in range(CHUNKS):
@@ -256,7 +290,7 @@
         scratch_shapes=[pltpu.SMEM((NBLK + 1,), jnp.int32)]
         + [pltpu.VMEM((OWN, WIDE), BF16)] * 2
         + [pltpu.SemaphoreType.DMA((2, NBLK)), pltpu.SemaphoreType.DMA((2, CHUNKS))]
-        + index_scratch(rows, counts),
+        + block_scratch(counts),
         compiler_params=limits(16),
         cost_estimate=pl.CostEstimate(flops=4 * 10**9, bytes_accessed=8 * 2**20, transcendentals=10**6),
         name="attend_inner",
@@ -265,11 +299,12 @@
 
 def outer_kernel(levels, far_sends_ref, far_rows_ref, far_counts_ref, q_ref, g_ref, own_ref, *refs):
     recv_refs, refs = refs[: len(levels)], refs[len(levels) + 3 :]
-    sends_ref, rows_ref, counts_ref, index_sems = refs[-4:]
-    refs = refs[:-4]
-    indices = index_loads(
-        (far_sends_ref, far_rows_ref, far_counts_ref), (sends_ref, rows_ref, counts_ref), index_sems
-    )
+    sends_held, sends_sem, rows_held, counts_held, index_sems = refs[-5:]
+    refs = refs[:-5]
+    sends_index, sends_ref = sends_load(far_sends_ref, sends_held, sends_sem)
+    rows_index, rows_ref = rows_load(far_rows_ref, rows_held, index_sems.at[0])
+    counts_index, counts_ref = counts_load(far_counts_ref, counts_held, index_sems.at[1])
+    indices = [sends_index, rows_index, counts_index]
     for load in indices:
         load.wait()
     att_ref, qg_ref, acc_ref = refs[:3]
@@ -311,7 +346,8 @@
         scratch_shapes=[pltpu.VMEM((PART, 2 * WIDE), BF16)] * len(levels)
         + [pltpu.VMEM((OWN, WIDE), BF16)] * 2
         + [pltpu.SemaphoreType.DMA((2, NBLK)), pltpu.SemaphoreType.DMA((len(levels),))]
-        + index_scratch(sends, rows, counts),
+        + sends_scratch(sends)
+        + block_scratch(counts),
         input_output_aliases={6 + len(levels) + n: n for n in range(3)},
         compiler_params=limits(16),
         cost_estimate=pl.CostEstimate(flops=4 * 10**9, bytes_accessed=4 * 2**20, transcendentals=10**6),
@@ -320,8 +356,7 @@
 
 
 def join_kernel(far_sends_ref, acc_ref, *refs):
-    sends_ref, index_sems = refs[-2:]
-    (index,) = index_loads((far_sends_ref,), (sends_ref,), index_sems)
+    index, sends_ref = sends_load(far_sends_ref, *refs[-2:])
     arrived_refs = refs[:LEVELS]
     key_ref, value_ref = refs[LEVELS : LEVELS + 2]
     key_ref[...] = acc_ref[:, :WIDE].astype(BF16)
@@ -341,7 +376,7 @@
         out_shape=[jax.ShapeDtypeStruct((OWN, WIDE), BF16)] * 2,
         in_specs=[HB] + [VM] * (1 + LEVELS),
         out_specs=[VM] * 2,
-        scratch_shapes=index_scratch(sends),
+        scratch_shapes=sends_scratch(sends),
         compiler_params=limits(10),
         cost_estimate=pl.CostEstimate(flops=10**6, bytes_accessed=4 * 2**20, transcendentals=0),
         name="join_gradients",
@@ -351,15 +386,11 @@
 def body(query_rows, key_rows, value_rows, out_grad, boundary_send_blocks, neighbours, live_count):
     heads = lax.axis_size("head")
     mine = query_rows.shape[0]
-    my_range = lax.axis_index("pix")
-    sends = lax.dynamic_index_in_dim(boundary_send_blocks, my_range, 0, keepdims=False)
-    rows = lax.dynamic_slice_in_dim(neighbours, my_range * NBLK, NBLK, 0)
-    counts = lax.dynamic_slice_in_dim(live_count, my_range * NBLK, NBLK, 0)
+    sends, rows, counts = boundary_send_blocks.transpose(1, 2, 0), neighbours.T, live_count
 
     parts = split(key_rows, value_rows)
     parts = [shifted(x, *o) if o != (0, 0) else x for x, o in zip(parts, OFFSETS)]
     q = query_rows.reshape(mine, heads, WIDE).transpose(1, 0, 2)
-    parts[0], rows, counts = lax.optimization_barrier((parts[0], rows, counts))
     own, *outgoing = pick(sends, parts)
     q, own = lax.optimization_barrier((q, own))
     q = lax.all_to_all(q, "head", 0, 0, tiled=True).reshape(OWN, WIDE)

time: 80.7 us -> 77.7 us (0.963)
  local copies, waits for them, and re-layouts: 7.12 us -> 2.82 us
  waiting for transfers between devices: 7.34 us -> 11.4 us
  starting transfers between devices: 42.9 us -> 40.1 us
    ppermute x7, waiting for transfers between devices: 2.67 us -> 6.74 us  [shifted(): return lax.ppermute(block, 'head', route)]
    dynamic_slice x4 -> x0, local copies, waits for them, and re-layouts: 2.94 us -> none  [the longest x1 1.28 us: body(): counts = lax.dynamic_slice_in_dim(live_count, my_range * NBLK, NBLK, 0)]
    all_to_all x1, starting transfers between devices: 7.12 us -> 4.69 us  [body(): q = lax.all_to_all(q, 'head', 0, 0, tiled=True).reshape(OWN, WIDE)]
  transfers between devices with their start and end apart: 19 -> 19, of which waited for: 3 -> 4; matrix products, arithmetic and copies ran while one was open for 9% -> 4% of each run, Pallas kernels for 8% -> 9%
where the time goes in v6:
time: 77.7 us; the launch traced here: 76.9 us
  starting transfers between devices  40.1 us (52%)
  Pallas kernels  21.7 us (28%)
  waiting for transfers between devices  11.4 us (15%)
  local copies, waits for them, and re-layouts  2.82 us (4%)
  between operations  0.89 us (1%)
    ppermute x10, starting transfers between devices, swapped(): return lax.ppermute(block, 'pix', route)  22.1 us
    pallas_call x1, Pallas kernels, outer(): pl.pallas_call(functools.partial(outer_kernel, levels), out_shape=[pltpu....  9.7 us
    ppermute x7, starting transfers between devices, shifted(): return lax.ppermute(block, 'head', route)  8.47 us
    ppermute x7, waiting for transfers between devices, shifted(): return lax.ppermute(block, 'head', route)  6.74 us
    pallas_call x1, Pallas kernels, inner(): pl.pallas_call(functools.partial(inner_kernel, 12), out_shape=[pltpu.HBM(...  6.73 us
    all_to_all x1, starting transfers between devices, body(): lax.all_to_all(attended.reshape(heads, mine, WIDE), 'head', 0, 0, tiled=T...  4.82 us
    all_to_all x1, starting transfers between devices, body(): q = lax.all_to_all(q, 'head', 0, 0, tiled=True).reshape(OWN, WIDE)  4.69 us
    ppermute x10, waiting for transfers between devices, swapped(): return lax.ppermute(block, 'pix', route)  4.67 us
  transfers between devices with their start and end apart: 19, of which 4 were waited for; matrix products, arithmetic and copies ran while one was open for 4% of the time, Pallas kernels for 9%

profile of v6, /device:TPU:8, one launch (start us, length us, event | category | flops | bytes accessed | tf_op | source)
XLA Modules:
  0.0 76.9 jit_solution(16381932560633292705)
XLA Ops:
  0.6 0.0 copy-start
  0.6 1.5 %split_keys_values.1 = (bf16[256,256]{1,0:T(8,128)(2,1)S(1)}, bf16[256,256]{1,0:T(8,128)(2,1)S(1)}, bf16[256,256]{1,0:T(8,128)(2,1)S(1)}, bf16[256,256]{1,0:T(8,...) custom-call(bf16[256,1024]{1,0:T(8,128)(2,1)} %key_ref.1, ...), custom_call_target="tpu_custom_call" | custom-call | bytes 2097152 | tf_op jit(solution)/shard_map/split_keys_values/pallas_call | solution.py:74
  2.1 1.7 %collective-permute-start = (bf16[256,256]{1,0:T(8,128)(2,1)S(1)}, bf16[256,256]{1,0:T(8,128)(2,1)S(1)}, u32[]{:S(2)}, u32[]{:S(2)}) collective-permute-start(bf16[256,256]{1,0:T(8,128)(2,1)S(1)} %get-tuple-element.37), channel_id=1, source_target_pairs={{0,2},{1,3},{2,4},{3,5},{4,6},{5,7},{6,0},{7,1},{8,10},{9,11},{10,... | collective-permute-start | bytes 393224 | tf_op jit(solution)/shard_map/ppermute | solution.py:47
  3.8 0.7 collective-permute-start.1
  4.5 0.2 collective-permute-start.2
  4.7 1.5 %collective-permute-start.3 = (bf16[256,256]{1,0:T(8,128)(2,1)S(1)}, bf16[256,256]{1,0:T(8,128)(2,1)S(1)}, u32[]{:S(2)}, u32[]{:S(2)}) collective-permute-start(bf16[256,256]{1,0:T(8,128)(2,1)S(1)} %get-tuple-element.40), channel_id=1, source_target_pairs={{0,7},{1,6},{2,1},{3,0},{4,3},{5,2},{6,5},{7,4},{8,15},{9,14},{10,... | collective-permute-start | bytes 393224 | tf_op jit(solution)/shard_map/ppermute | solution.py:47
  6.2 2.0 %collective-permute-start.4 = (bf16[256,256]{1,0:T(8,128)(2,1)S(1)}, bf16[256,256]{1,0:T(8,128)(2,1)S(1)}, u32[]{:S(2)}, u32[]{:S(2)}) collective-permute-start(bf16[256,256]{1,0:T(8,128)(2,1)S(1)} %get-tuple-element.41), channel_id=1, source_target_pairs={{0,4},{1,5},{2,6},{3,7},{4,0},{5,1},{6,2},{7,3},{8,12},{9,13},{10,... | collective-permute-start | bytes 393224 | tf_op jit(solution)/shard_map/ppermute | solution.py:47
  8.3 0.0 collective-permute-done.refs_0_
  8.3 2.3 %collective-permute-start.5 = (bf16[256,256]{1,0:T(8,128)(2,1)S(1)}, bf16[256,256]{1,0:T(8,128)(2,1)S(1)}, u32[]{:S(2)}, u32[]{:S(2)}) collective-permute-start(bf16[256,256]{1,0:T(8,128)(2,1)S(1)} %get-tuple-element.42), channel_id=1, source_target_pairs={{0,5},{1,4},{2,7},{3,6},{4,1},{5,0},{6,3},{7,2},{8,13},{9,12},{10,... | collective-permute-start | bytes 393224 | tf_op jit(solution)/shard_map/ppermute | solution.py:47
  10.6 0.0 collective-permute-done.1.refs_1_
  10.6 0.0 collective-permute-start.6
  10.6 0.0 copy-done
  10.6 0.9 %bitcast_bitcast_fusion = bf16[8,256,128]{2,1,0:T(8,128)(2,1)} fusion(bf16[256,1024]{1,0:T(8,128)(2,1)S(1)} %copy-done), kind=kLoop, calls=%fused_computation.1 | loop fusion | bytes 1048576 | tf_op jit(solution)/shard_map/transpose | solution.py:393
  11.5 0.0 collective-permute-done.2.refs_2_
  11.5 0.0 collective-permute-done.3.refs_3_
  11.5 3.1 %collective-permute-done.4.refs_4_ = bf16[256,256]{1,0:T(8,128)(2,1)S(1)} collective-permute-done((bf16[256,256]{1,0:T(8,128)(2,1)S(1)}, bf16[256,256]{1,0:T(8,128)(2,1)S(1)}, u32[]{:S(2)}, u32[]{:S(2)}) %collective-permute-start.4) | collective-permute-done | bytes 131104 | tf_op jit(solution)/shard_map/ppermute | solution.py:47
  14.6 3.6 %collective-permute-done.5.refs_5_ = bf16[256,256]{1,0:T(8,128)(2,1)S(1)} collective-permute-done((bf16[256,256]{1,0:T(8,128)(2,1)S(1)}, bf16[256,256]{1,0:T(8,128)(2,1)S(1)}, u32[]{:S(2)}, u32[]{:S(2)}) %collective-permute-start.5) | collective-permute-done | bytes 131104 | tf_op jit(solution)/shard_map/ppermute | solution.py:47
  18.2 0.0 collective-permute-done.6.refs_6_
  18.2 1.8 %pick_boundary.1 = (bf16[2048,256]{1,0:T(8,128)(2,1)}, bf16[256,256]{1,0:T(8,128)(2,1)}, bf16[256,256]{1,0:T(8,128)(2,1)}, bf16[256,256]{1,0:T(8,128)(2,1)}, bf1...) custom-call(s32[5,4,32]{2,1,0:T(4,128)} %bitcast.20, bf16[256,256]{1,0:T(8,128)(2,1)S(1)} %collective-permute-done.refs_0_, ...), custom_call_target="tpu_custom_call" | custom-call | bytes 4194304 | tf_op jit(solution)/shard_map/pick_boundary/pallas_call | solution.py:155
  20.1 4.7 %all-to-all-start = ((bf16[8,256,128]{2,1,0:T(8,128)(2,1)}), bf16[8,256,128]{2,1,0:T(8,128)(2,1)S(1)}, u32[]{:S(2)}, u32[]{:S(2)}) async-start(bf16[8,256,128]{2,1,0:T(8,128)(2,1)} %bitcast_bitcast_fusion), calls=%async_computation | async-start | bytes 1048576 | tf_op jit(solution)/shard_map/all_to_all | solution.py:396
  24.8 0.5 collective-permute-start.7
  25.3 3.3 %collective-permute-start.8 = (bf16[256,256]{1,0:T(8,128)(2,1)}, bf16[256,256]{1,0:T(8,128)(2,1)}, u32[]{:S(2)}, u32[]{:S(2)}) collective-permute-start(bf16[256,256]{1,0:T(8,128)(2,1)} %get-tuple-element.51), channel_id=1, source_target_pairs={{0,16},{8,24},{16,0},{24,8},{32,48},{40,56},{48,32},{56,40},{64,80... | collective-permute-start | bytes 393224 | tf_op jit(solution)/shard_map/ppermute | solution.py:33
  28.6 4.5 %collective-permute-start.9 = (bf16[256,256]{1,0:T(8,128)(2,1)}, bf16[256,256]{1,0:T(8,128)(2,1)}, u32[]{:S(2)}, u32[]{:S(2)}) collective-permute-start(bf16[256,256]{1,0:T(8,128)(2,1)} %get-tuple-element.52), channel_id=1, source_target_pairs={{0,32},{8,40},{16,48},{24,56},{32,0},{40,8},{48,16},{56,24},{64,96... | collective-permute-start | bytes 393224 | tf_op jit(solution)/shard_map/ppermute | solution.py:33
  33.1 1.5 %collective-permute-start.10 = (bf16[256,256]{1,0:T(8,128)(2,1)S(1)}, bf16[256,256]{1,0:T(8,128)(2,1)}, u32[]{:S(2)}, u32[]{:S(2)}) collective-permute-start(bf16[256,256]{1,0:T(8,128)(2,1)S(1)} %get-tuple-element.53), channel_id=1, source_target_pairs={{0,64},{8,72},{16,80},{24,88},{32,96},{40,104},{48,112},{56,120},{... | collective-permute-start | bytes 393224 | tf_op jit(solution)/shard_map/ppermute | solution.py:33
  34.6 2.7 %collective-permute-start.11 = (bf16[256,256]{1,0:T(8,128)(2,1)S(1)}, bf16[256,256]{1,0:T(8,128)(2,1)}, u32[]{:S(2)}, u32[]{:S(2)}) collective-permute-start(bf16[256,256]{1,0:T(8,128)(2,1)S(1)} %get-tuple-element.54), channel_id=1, source_target_pairs={{0,128},{8,136},{16,144},{24,152},{32,160},{40,168},{48,176},{56,1... | collective-permute-start | bytes 393224 | tf_op jit(solution)/shard_map/ppermute | solution.py:33
  37.3 0.0 all-to-all-done
  37.3 6.7 %attend_inner.1 = (bf16[2048,128]{1,0:T(8,128)(2,1)}, bf16[2048,128]{1,0:T(8,128)(2,1)}, f32[2048,256]{1,0:T(8,128)S(1)}, bf16[2048,256]{1,0:T(8,128)(2,1)S(1)}, bf16[2048,128]{1,0:T(8,128)(2,1)S(1)}) custom-call(s32[9,1024]{1,0:T(8,128)} %bitcast.23, s32[1024]{0:T(1024)} %far_counts_ref.3, bf16[2048,128]{1,0:T(8,128)(2,1)S(1)} %bitcast.17, ...), custom_call_target="tpu_custom_call" | custom-call | flops 4000000000 | bytes 8388608 | tf_op jit(solution)/shard_map/attend_inner/pallas_call | solution.py:279
  44.0 0.0 collective-permute-done.7.refs_0_
  44.0 0.0 collective-permute-done.8.refs_1_
  44.0 0.0 collective-permute-done.9.refs_2_
  44.1 0.0 collective-permute-done.10.refs_3_
  44.1 0.0 collective-permute-done.11.refs_4_
  44.1 9.7 %attend_outer.1 = (bf16[2048,128]{1,0:T(8,128)(2,1)}, bf16[2048,128]{1,0:T(8,128)(2,1)}, f32[2048,256]{1,0:T(8,128)S(1)}, bf16[256,256]{1,0:T(8,128)(2,1)}, bf16...) custom-call(s32[5,4,32]{2,1,0:T(4,128)} %bitcast.21, ...), custom_call_target="tpu_custom_call", output_to_operand_aliasing={{0}: (11, {}), {1}: (12, {}), {2}: (13, {})} | custom-call | flops 4000000000 | bytes 4194304 | tf_op jit(solution)/shard_map/attend_outer/pallas_call | solution.py:336
  53.8 4.8 %all-to-all-start.1 = ((bf16[8,256,128]{2,1,0:T(8,128)(2,1)}), bf16[8,256,128]{2,1,0:T(8,128)(2,1)}, u32[]{:S(2)}, u32[]{:S(2)}) async-start(bf16[8,256,128]{2,1,0:T(8,128)(2,1)} %bitcast.19), calls=%async_computation.1 | async-start | bytes 1048576 | tf_op jit(solution)/shard_map/all_to_all | solution.py:402
  58.6 1.0 %collective-permute-start.12 = (bf16[256,256]{1,0:T(8,128)(2,1)}, bf16[256,256]{1,0:T(8,128)(2,1)S(1)}, u32[]{:S(2)}, u32[]{:S(2)}) collective-permute-start(bf16[256,256]{1,0:T(8,128)(2,1)} %get-tuple-element.59), channel_id=1, source_target_pairs={{0,8},{8,0},{16,24},{24,16},{32,40},{40,32},{48,56},{56,48},{64,72... | collective-permute-start | bytes 393224 | tf_op jit(solution)/shard_map/ppermute | solution.py:33
  59.6 1.5 %collective-permute-start.13 = (bf16[256,256]{1,0:T(8,128)(2,1)}, bf16[256,256]{1,0:T(8,128)(2,1)S(1)}, u32[]{:S(2)}, u32[]{:S(2)}) collective-permute-start(bf16[256,256]{1,0:T(8,128)(2,1)} %get-tuple-element.64), channel_id=1, source_target_pairs={{0,16},{8,24},{16,0},{24,8},{32,48},{40,56},{48,32},{56,40},{64,80... | collective-permute-start | bytes 393224 | tf_op jit(solution)/shard_map/ppermute | solution.py:33
  61.1 2.9 %collective-permute-start.14 = (bf16[256,256]{1,0:T(8,128)(2,1)}, bf16[256,256]{1,0:T(8,128)(2,1)S(1)}, u32[]{:S(2)}, u32[]{:S(2)}) collective-permute-start(bf16[256,256]{1,0:T(8,128)(2,1)} %get-tuple-element.65), channel_id=1, source_target_pairs={{0,32},{8,40},{16,48},{24,56},{32,0},{40,8},{48,16},{56,24},{64,96... | collective-permute-start | bytes 393224 | tf_op jit(solution)/shard_map/ppermute | solution.py:33
  64.0 1.5 %collective-permute-start.15 = (bf16[256,256]{1,0:T(8,128)(2,1)}, bf16[256,256]{1,0:T(8,128)(2,1)S(1)}, u32[]{:S(2)}, u32[]{:S(2)}) collective-permute-start(bf16[256,256]{1,0:T(8,128)(2,1)} %get-tuple-element.66), channel_id=1, source_target_pairs={{0,64},{8,72},{16,80},{24,88},{32,96},{40,104},{48,112},{56,120},{... | collective-permute-start | bytes 393224 | tf_op jit(solution)/shard_map/ppermute | solution.py:33
  65.5 2.7 %collective-permute-start.16 = (bf16[256,256]{1,0:T(8,128)(2,1)}, bf16[256,256]{1,0:T(8,128)(2,1)S(1)}, u32[]{:S(2)}, u32[]{:S(2)}) collective-permute-start(bf16[256,256]{1,0:T(8,128)(2,1)} %get-tuple-element.67), channel_id=1, source_target_pairs={{0,128},{8,136},{16,144},{24,152},{32,160},{40,168},{48,176},{56,1... | collective-permute-start | bytes 393224 | tf_op jit(solution)/shard_map/ppermute | solution.py:33
  68.2 0.0 all-to-all-done.1
  68.2 1.9 %copy_bitcast_fusion = bf16[256,1024]{1,0:T(8,128)(2,1)} fusion(bf16[8,256,128]{2,1,0:T(8,128)(2,1)} %all-to-all-done.1), kind=kLoop, calls=%fused_computation | loop fusion | bytes 1048576 | tf_op jit(solution)/shard_map/reshape | solution.py:403
  70.1 0.0 collective-permute-done.12.refs_0_
  70.1 4.4 %collective-permute-done.13.refs_1_ = bf16[256,256]{1,0:T(8,128)(2,1)S(1)} collective-permute-done((bf16[256,256]{1,0:T(8,128)(2,1)}, bf16[256,256]{1,0:T(8,128)(2,1)S(1)}, u32[]{:S(2)}, u32[]{:S(2)}) %collective-permute-start.13) | collective-permute-done | bytes 131104 | tf_op jit(solution)/shard_map/ppermute | solution.py:33
  74.5 0.3 collective-permute-done.14.refs_2_
  74.8 0.0 collective-permute-done.15.refs_3_
  74.8 0.0 collective-permute-done.16.refs_4_
  74.8 1.9 %join_gradients.1 = (bf16[2048,128]{1,0:T(8,128)(2,1)}, bf16[2048,128]{1,0:T(8,128)(2,1)}) custom-call(s32[5,4,32]{2,1,0:T(4,128)} %bitcast.22, f32[2048,256]{1,0:T(8,128)S(1)} %get-tuple-element.62.acc_ref, bf16[256,256]{1,0:T(8,128)(2,1)S(1)} %collective-permute-done.12.refs_0_, bf16[256,256]{1,0:T(8,128)(2,1)S(1)} %collective-permute-done.13.refs_1_, ...), custom_call_target="tpu_custom_call" | custom-call | flops 1000000 | bytes 4194304 | tf_op jit(solution)/shard_map/join_gradients/pallas_call | solution.py:374
Async XLA Ops:
  0.6 10.0 %copy-start = (bf16[256,1024]{1,0:T(8,128)(2,1)S(1)}, bf16[256,1024]{1,0:T(8,128)(2,1)}, u32[]{:S(2)}) copy-start(bf16[256,1024]{1,0:T(8,128)(2,1)} %param.7) | copy-start | bytes 1572868
  2.1 6.1 %collective-permute-start = (bf16[256,256]{1,0:T(8,128)(2,1)S(1)}, bf16[256,256]{1,0:T(8,128)(2,1)S(1)}, u32[]{:S(2)}, u32[]{:S(2)}) collective-permute-start(bf16[256,256]{1,0:T(8,128)(2,1)S(1)} %get-tuple-element.37), channel_id=1, source_target_pairs={{0,2},{1,3},{2,4},{3,5},{4,6},{5,7},{6,0},{7,1},{8,10},{9,11},{10,... | collective-permute-start | bytes 393224 | tf_op jit(solution)/shard_map/ppermute | solution.py:47
  3.8 6.8 %collective-permute-start.1 = (bf16[256,256]{1,0:T(8,128)(2,1)S(1)}, bf16[256,256]{1,0:T(8,128)(2,1)S(1)}, u32[]{:S(2)}, u32[]{:S(2)}) collective-permute-start(bf16[256,256]{1,0:T(8,128)(2,1)S(1)} %get-tuple-element.38), channel_id=1, source_target_pairs={{0,6},{1,7},{2,0},{3,1},{4,2},{5,3},{6,4},{7,5},{8,14},{9,15},{10,... | collective-permute-start | bytes 393224 | tf_op jit(solution)/shard_map/ppermute | solution.py:47
  4.5 7.0 %collective-permute-start.2 = (bf16[256,256]{1,0:T(8,128)(2,1)S(1)}, bf16[256,256]{1,0:T(8,128)(2,1)S(1)}, u32[]{:S(2)}, u32[]{:S(2)}) collective-permute-start(bf16[256,256]{1,0:T(8,128)(2,1)S(1)} %get-tuple-element.39), channel_id=1, source_target_pairs={{0,3},{1,2},{2,5},{3,4},{4,7},{5,6},{6,1},{7,0},{8,11},{9,10},{10,... | collective-permute-start | bytes 393224 | tf_op jit(solution)/shard_map/ppermute | solution.py:47
  4.7 6.8 %collective-permute-start.3 = (bf16[256,256]{1,0:T(8,128)(2,1)S(1)}, bf16[256,256]{1,0:T(8,128)(2,1)S(1)}, u32[]{:S(2)}, u32[]{:S(2)}) collective-permute-start(bf16[256,256]{1,0:T(8,128)(2,1)S(1)} %get-tuple-element.40), channel_id=1, source_target_pairs={{0,7},{1,6},{2,1},{3,0},{4,3},{5,2},{6,5},{7,4},{8,15},{9,14},{10,... | collective-permute-start | bytes 393224 | tf_op jit(solution)/shard_map/ppermute | solution.py:47
  6.2 8.4 %collective-permute-start.4 = (bf16[256,256]{1,0:T(8,128)(2,1)S(1)}, bf16[256,256]{1,0:T(8,128)(2,1)S(1)}, u32[]{:S(2)}, u32[]{:S(2)}) collective-permute-start(bf16[256,256]{1,0:T(8,128)(2,1)S(1)} %get-tuple-element.41), channel_id=1, source_target_pairs={{0,4},{1,5},{2,6},{3,7},{4,0},{5,1},{6,2},{7,3},{8,12},{9,13},{10,... | collective-permute-start | bytes 393224 | tf_op jit(solution)/shard_map/ppermute | solution.py:47
  8.3 10.0 %collective-permute-start.5 = (bf16[256,256]{1,0:T(8,128)(2,1)S(1)}, bf16[256,256]{1,0:T(8,128)(2,1)S(1)}, u32[]{:S(2)}, u32[]{:S(2)}) collective-permute-start(bf16[256,256]{1,0:T(8,128)(2,1)S(1)} %get-tuple-element.42), channel_id=1, source_target_pairs={{0,5},{1,4},{2,7},{3,6},{4,1},{5,0},{6,3},{7,2},{8,13},{9,12},{10,... | collective-permute-start | bytes 393224 | tf_op jit(solution)/shard_map/ppermute | solution.py:47
  10.6 7.6 %collective-permute-start.6 = (bf16[256,256]{1,0:T(8,128)(2,1)S(1)}, bf16[256,256]{1,0:T(8,128)(2,1)S(1)}, u32[]{:S(2)}, u32[]{:S(2)}) collective-permute-start(bf16[256,256]{1,0:T(8,128)(2,1)S(1)} %get-tuple-element.43), channel_id=1, source_target_pairs={{0,1},{1,0},{2,3},{3,2},{4,5},{5,4},{6,7},{7,6},{8,9},{9,8},{10,11... | collective-permute-start | bytes 393224 | tf_op jit(solution)/shard_map/ppermute | solution.py:47
  20.1 17.2 %all-to-all-start = ((bf16[8,256,128]{2,1,0:T(8,128)(2,1)}), bf16[8,256,128]{2,1,0:T(8,128)(2,1)S(1)}, u32[]{:S(2)}, u32[]{:S(2)}) async-start(bf16[8,256,128]{2,1,0:T(8,128)(2,1)} %bitcast_bitcast_fusion), calls=%async_computation | async-start | bytes 1048576 | tf_op jit(solution)/shard_map/all_to_all | solution.py:396
  24.8 19.2 %collective-permute-start.7 = (bf16[256,256]{1,0:T(8,128)(2,1)}, bf16[256,256]{1,0:T(8,128)(2,1)S(1)}, u32[]{:S(2)}, u32[]{:S(2)}) collective-permute-start(bf16[256,256]{1,0:T(8,128)(2,1)} %get-tuple-element.50), channel_id=1, source_target_pairs={{0,8},{8,0},{16,24},{24,16},{32,40},{40,32},{48,56},{56,48},{64,72... | collective-permute-start | bytes 393224 | tf_op jit(solution)/shard_map/ppermute | solution.py:33
  25.3 18.7 %collective-permute-start.8 = (bf16[256,256]{1,0:T(8,128)(2,1)}, bf16[256,256]{1,0:T(8,128)(2,1)}, u32[]{:S(2)}, u32[]{:S(2)}) collective-permute-start(bf16[256,256]{1,0:T(8,128)(2,1)} %get-tuple-element.51), channel_id=1, source_target_pairs={{0,16},{8,24},{16,0},{24,8},{32,48},{40,56},{48,32},{56,40},{64,80... | collective-permute-start | bytes 393224 | tf_op jit(solution)/shard_map/ppermute | solution.py:33
  28.6 15.5 %collective-permute-start.9 = (bf16[256,256]{1,0:T(8,128)(2,1)}, bf16[256,256]{1,0:T(8,128)(2,1)}, u32[]{:S(2)}, u32[]{:S(2)}) collective-permute-start(bf16[256,256]{1,0:T(8,128)(2,1)} %get-tuple-element.52), channel_id=1, source_target_pairs={{0,32},{8,40},{16,48},{24,56},{32,0},{40,8},{48,16},{56,24},{64,96... | collective-permute-start | bytes 393224 | tf_op jit(solution)/shard_map/ppermute | solution.py:33
  33.1 11.0 %collective-permute-start.10 = (bf16[256,256]{1,0:T(8,128)(2,1)S(1)}, bf16[256,256]{1,0:T(8,128)(2,1)}, u32[]{:S(2)}, u32[]{:S(2)}) collective-permute-start(bf16[256,256]{1,0:T(8,128)(2,1)S(1)} %get-tuple-element.53), channel_id=1, source_target_pairs={{0,64},{8,72},{16,80},{24,88},{32,96},{40,104},{48,112},{56,120},{... | collective-permute-start | bytes 393224 | tf_op jit(solution)/shard_map/ppermute | solution.py:33
  34.6 9.5 %collective-permute-start.11 = (bf16[256,256]{1,0:T(8,128)(2,1)S(1)}, bf16[256,256]{1,0:T(8,128)(2,1)}, u32[]{:S(2)}, u32[]{:S(2)}) collective-permute-start(bf16[256,256]{1,0:T(8,128)(2,1)S(1)} %get-tuple-element.54), channel_id=1, source_target_pairs={{0,128},{8,136},{16,144},{24,152},{32,160},{40,168},{48,176},{56,1... | collective-permute-start | bytes 393224 | tf_op jit(solution)/shard_map/ppermute | solution.py:33
  53.8 14.4 %all-to-all-start.1 = ((bf16[8,256,128]{2,1,0:T(8,128)(2,1)}), bf16[8,256,128]{2,1,0:T(8,128)(2,1)}, u32[]{:S(2)}, u32[]{:S(2)}) async-start(bf16[8,256,128]{2,1,0:T(8,128)(2,1)} %bitcast.19), calls=%async_computation.1 | async-start | bytes 1048576 | tf_op jit(solution)/shard_map/all_to_all | solution.py:402
  58.6 11.5 %collective-permute-start.12 = (bf16[256,256]{1,0:T(8,128)(2,1)}, bf16[256,256]{1,0:T(8,128)(2,1)S(1)}, u32[]{:S(2)}, u32[]{:S(2)}) collective-permute-start(bf16[256,256]{1,0:T(8,128)(2,1)} %get-tuple-element.59), channel_id=1, source_target_pairs={{0,8},{8,0},{16,24},{24,16},{32,40},{40,32},{48,56},{56,48},{64,72... | collective-permute-start | bytes 393224 | tf_op jit(solution)/shard_map/ppermute | solution.py:33
  59.6 14.9 %collective-permute-start.13 = (bf16[256,256]{1,0:T(8,128)(2,1)}, bf16[256,256]{1,0:T(8,128)(2,1)S(1)}, u32[]{:S(2)}, u32[]{:S(2)}) collective-permute-start(bf16[256,256]{1,0:T(8,128)(2,1)} %get-tuple-element.64), channel_id=1, source_target_pairs={{0,16},{8,24},{16,0},{24,8},{32,48},{40,56},{48,32},{56,40},{64,80... | collective-permute-start | bytes 393224 | tf_op jit(solution)/shard_map/ppermute | solution.py:33
  61.1 13.7 %collective-permute-start.14 = (bf16[256,256]{1,0:T(8,128)(2,1)}, bf16[256,256]{1,0:T(8,128)(2,1)S(1)}, u32[]{:S(2)}, u32[]{:S(2)}) collective-permute-start(bf16[256,256]{1,0:T(8,128)(2,1)} %get-tuple-element.65), channel_id=1, source_target_pairs={{0,32},{8,40},{16,48},{24,56},{32,0},{40,8},{48,16},{56,24},{64,96... | collective-permute-start | bytes 393224 | tf_op jit(solution)/shard_map/ppermute | solution.py:33
  64.0 10.8 %collective-permute-start.15 = (bf16[256,256]{1,0:T(8,128)(2,1)}, bf16[256,256]{1,0:T(8,128)(2,1)S(1)}, u32[]{:S(2)}, u32[]{:S(2)}) collective-permute-start(bf16[256,256]{1,0:T(8,128)(2,1)} %get-tuple-element.66), channel_id=1, source_target_pairs={{0,64},{8,72},{16,80},{24,88},{32,96},{40,104},{48,112},{56,120},{... | collective-permute-start | bytes 393224 | tf_op jit(solution)/shard_map/ppermute | solution.py:33
  65.5 9.3 %collective-permute-start.16 = (bf16[256,256]{1,0:T(8,128)(2,1)}, bf16[256,256]{1,0:T(8,128)(2,1)S(1)}, u32[]{:S(2)}, u32[]{:S(2)}) collective-permute-start(bf16[256,256]{1,0:T(8,128)(2,1)} %get-tuple-element.67), channel_id=1, source_target_pairs={{0,128},{8,136},{16,144},{24,152},{32,160},{40,168},{48,176},{56,1... | collective-permute-start | bytes 393224 | tf_op jit(solution)/shard_map/ppermute | solution.py:33

commit v7 on v6

--- a/solution.py
+++ b/solution.py
@@ -18,6 +18,7 @@
 FILL = -1e30
 CHUNKS = 8
 LANES = 128
+FAR_FIRST = (2, 1, 4, 0, 3)
 HEAD_DEVICES = 8
 OFFSETS = ((1, 0), (3, 0), (1, 1), (3, 1), (2, 0), (2, 1), (0, 1), (0, 0))
 F32 = jnp.float32
@@ -362,10 +363,10 @@
     key_ref[...] = acc_ref[:, :WIDE].astype(BF16)
     value_ref[...] = acc_ref[:, WIDE:].astype(BF16)
     index.wait()
-    for b in range(LEVELS):
+    for n, b in enumerate(FAR_FIRST):
         for s in range(SEND):
             at = rows_of(sends_ref[b, s])
-            both = acc_ref[at, :] + arrived_refs[b][s * BLK : (s + 1) * BLK, :].astype(F32)
+            both = acc_ref[at, :] + arrived_refs[n][s * BLK : (s + 1) * BLK, :].astype(F32)
             key_ref[at, :] = both[:, :WIDE].astype(BF16)
             value_ref[at, :] = both[:, WIDE:].astype(BF16)
 
@@ -396,9 +397,8 @@
     q = lax.all_to_all(q, "head", 0, 0, tiled=True).reshape(OWN, WIDE)
     recv = [swapped(outgoing[b], b) for b in range(LEVELS)]
     *done, own, grad = inner(rows, counts, q, out_grad, own)
-    levels = tuple(range(LEVELS))
-    attended, query_grad, acc, *back = outer(levels, sends, rows, counts, q, grad, own, recv, done)
-    arrived = [swapped(back[b], b) for b in range(LEVELS)]
+    attended, query_grad, acc, *back = outer(FAR_FIRST, sends, rows, counts, q, grad, own, recv, done)
+    arrived = [swapped(x, b) for x, b in zip(back, FAR_FIRST)]
     attended = lax.all_to_all(attended.reshape(heads, mine, WIDE), "head", 0, 0, tiled=True)
     attended = attended.transpose(1, 0, 2).reshape(mine, heads * WIDE)
     attended, arrived[0] = lax.optimization_barrier((attended, arrived[0]))

time: 77.7 us -> 79.2 us (1.019)
  waiting for transfers between devices: 11.4 us -> 13.3 us
  starting transfers between devices: 40.1 us -> 39.1 us
    ppermute x10, waiting for transfers between devices: 4.67 us -> 6.53 us  [swapped(): return lax.ppermute(block, 'pix', route)]
    ppermute x10, starting transfers between devices: 22.1 us -> 21.1 us  [swapped(): return lax.ppermute(block, 'pix', route)]
  transfers between devices with their start and end apart: 19 -> 19, of which waited for: 4 -> 6; matrix products, arithmetic and copies ran while one was open for 4% -> 4% of each run, Pallas kernels for 9% -> 9%
where the time goes in v7:
time: 79.2 us; the launch traced here: 77.7 us
  starting transfers between devices  39.1 us (49%)
  Pallas kernels  21.7 us (27%)
  waiting for transfers between devices  13.3 us (17%)
  local copies, waits for them, and re-layouts  2.82 us (4%)
  between operations  0.87 us (1%)
    ppermute x10, starting transfers between devices, swapped(): return lax.ppermute(block, 'pix', route)  21.1 us
    pallas_call x1, Pallas kernels, outer(): pl.pallas_call(functools.partial(outer_kernel, levels), out_shape=[pltpu....  9.68 us
    ppermute x7, starting transfers between devices, shifted(): return lax.ppermute(block, 'head', route)  8.47 us
    ppermute x7, waiting for transfers between devices, shifted(): return lax.ppermute(block, 'head', route)  6.74 us
    pallas_call x1, Pallas kernels, inner(): pl.pallas_call(functools.partial(inner_kernel, 12), out_shape=[pltpu.HBM(...  6.73 us
    ppermute x10, waiting for transfers between devices, swapped(): return lax.ppermute(block, 'pix', route)  6.53 us
    all_to_all x1, starting transfers between devices, body(): lax.all_to_all(attended.reshape(heads, mine, WIDE), 'head', 0, 0, tiled=T...  4.81 us
    all_to_all x1, starting transfers between devices, body(): q = lax.all_to_all(q, 'head', 0, 0, tiled=True).reshape(OWN, WIDE)  4.69 us
  transfers between devices with their start and end apart: 19, of which 6 were waited for; matrix products, arithmetic and copies ran while one was open for 4% of the time, Pallas kernels for 9%

profile of v7, /device:TPU:8, one launch (start us, length us, event | category | flops | bytes accessed | tf_op | source)
XLA Modules:
  0.0 77.7 jit_solution(5785571100431554743)
XLA Ops:
  0.6 0.0 copy-start
  0.6 1.5 %split_keys_values.1 = (bf16[256,256]{1,0:T(8,128)(2,1)S(1)}, bf16[256,256]{1,0:T(8,128)(2,1)S(1)}, bf16[256,256]{1,0:T(8,128)(2,1)S(1)}, bf16[256,256]{1,0:T(8,...) custom-call(bf16[256,1024]{1,0:T(8,128)(2,1)} %key_ref.1, ...), custom_call_target="tpu_custom_call" | custom-call | bytes 2097152 | tf_op jit(solution)/shard_map/split_keys_values/pallas_call | solution.py:75
  2.1 1.7 %collective-permute-start = (bf16[256,256]{1,0:T(8,128)(2,1)S(1)}, bf16[256,256]{1,0:T(8,128)(2,1)S(1)}, u32[]{:S(2)}, u32[]{:S(2)}) collective-permute-start(bf16[256,256]{1,0:T(8,128)(2,1)S(1)} %get-tuple-element.37), channel_id=1, source_target_pairs={{0,2},{1,3},{2,4},{3,5},{4,6},{5,7},{6,0},{7,1},{8,10},{9,11},{10,... | collective-permute-start | bytes 393224 | tf_op jit(solution)/shard_map/ppermute | solution.py:48
  3.8 0.7 collective-permute-start.1
  4.5 0.2 collective-permute-start.2
  4.7 1.5 %collective-permute-start.3 = (bf16[256,256]{1,0:T(8,128)(2,1)S(1)}, bf16[256,256]{1,0:T(8,128)(2,1)S(1)}, u32[]{:S(2)}, u32[]{:S(2)}) collective-permute-start(bf16[256,256]{1,0:T(8,128)(2,1)S(1)} %get-tuple-element.40), channel_id=1, source_target_pairs={{0,7},{1,6},{2,1},{3,0},{4,3},{5,2},{6,5},{7,4},{8,15},{9,14},{10,... | collective-permute-start | bytes 393224 | tf_op jit(solution)/shard_map/ppermute | solution.py:48
  6.2 2.0 %collective-permute-start.4 = (bf16[256,256]{1,0:T(8,128)(2,1)S(1)}, bf16[256,256]{1,0:T(8,128)(2,1)S(1)}, u32[]{:S(2)}, u32[]{:S(2)}) collective-permute-start(bf16[256,256]{1,0:T(8,128)(2,1)S(1)} %get-tuple-element.41), channel_id=1, source_target_pairs={{0,4},{1,5},{2,6},{3,7},{4,0},{5,1},{6,2},{7,3},{8,12},{9,13},{10,... | collective-permute-start | bytes 393224 | tf_op jit(solution)/shard_map/ppermute | solution.py:48
  8.3 0.0 collective-permute-done.refs_0_
  8.3 2.3 %collective-permute-start.5 = (bf16[256,256]{1,0:T(8,128)(2,1)S(1)}, bf16[256,256]{1,0:T(8,128)(2,1)S(1)}, u32[]{:S(2)}, u32[]{:S(2)}) collective-permute-start(bf16[256,256]{1,0:T(8,128)(2,1)S(1)} %get-tuple-element.42), channel_id=1, source_target_pairs={{0,5},{1,4},{2,7},{3,6},{4,1},{5,0},{6,3},{7,2},{8,13},{9,12},{10,... | collective-permute-start | bytes 393224 | tf_op jit(solution)/shard_map/ppermute | solution.py:48
  10.6 0.0 collective-permute-done.1.refs_1_
  10.6 0.0 collective-permute-start.6
  10.6 0.0 copy-done
  10.6 0.9 %bitcast_bitcast_fusion = bf16[8,256,128]{2,1,0:T(8,128)(2,1)} fusion(bf16[256,1024]{1,0:T(8,128)(2,1)S(1)} %copy-done), kind=kLoop, calls=%fused_computation.1 | loop fusion | bytes 1048576 | tf_op jit(solution)/shard_map/transpose | solution.py:394
  11.5 0.0 collective-permute-done.2.refs_2_
  11.5 0.0 collective-permute-done.3.refs_3_
  11.5 3.1 %collective-permute-done.4.refs_4_ = bf16[256,256]{1,0:T(8,128)(2,1)S(1)} collective-permute-done((bf16[256,256]{1,0:T(8,128)(2,1)S(1)}, bf16[256,256]{1,0:T(8,128)(2,1)S(1)}, u32[]{:S(2)}, u32[]{:S(2)}) %collective-permute-start.4) | collective-permute-done | bytes 131104 | tf_op jit(solution)/shard_map/ppermute | solution.py:48
  14.6 3.6 %collective-permute-done.5.refs_5_ = bf16[256,256]{1,0:T(8,128)(2,1)S(1)} collective-permute-done((bf16[256,256]{1,0:T(8,128)(2,1)S(1)}, bf16[256,256]{1,0:T(8,128)(2,1)S(1)}, u32[]{:S(2)}, u32[]{:S(2)}) %collective-permute-start.5) | collective-permute-done | bytes 131104 | tf_op jit(solution)/shard_map/ppermute | solution.py:48
  18.2 0.0 collective-permute-done.6.refs_6_
  18.2 1.8 %pick_boundary.1 = (bf16[2048,256]{1,0:T(8,128)(2,1)}, bf16[256,256]{1,0:T(8,128)(2,1)S(1)}, bf16[256,256]{1,0:T(8,128)(2,1)}, bf16[256,256]{1,0:T(8,128)(2,1)},...) custom-call(s32[5,4,32]{2,1,0:T(4,128)} %bitcast.20, bf16[256,256]{1,0:T(8,128)(2,1)S(1)} %collective-permute-done.refs_0_, ...), custom_call_target="tpu_custom_call" | custom-call | bytes 4194304 | tf_op jit(solution)/shard_map/pick_boundary/pallas_call | solution.py:156
  20.1 4.7 %all-to-all-start = ((bf16[8,256,128]{2,1,0:T(8,128)(2,1)}), bf16[8,256,128]{2,1,0:T(8,128)(2,1)S(1)}, u32[]{:S(2)}, u32[]{:S(2)}) async-start(bf16[8,256,128]{2,1,0:T(8,128)(2,1)} %bitcast_bitcast_fusion), calls=%async_computation | async-start | bytes 1048576 | tf_op jit(solution)/shard_map/all_to_all | solution.py:397
  24.8 5.8 %collective-permute-start.7 = (bf16[256,256]{1,0:T(8,128)(2,1)}, bf16[256,256]{1,0:T(8,128)(2,1)S(1)}, u32[]{:S(2)}, u32[]{:S(2)}) collective-permute-start(bf16[256,256]{1,0:T(8,128)(2,1)} %get-tuple-element.50), channel_id=1, source_target_pairs={{0,32},{8,40},{16,48},{24,56},{32,0},{40,8},{48,16},{56,24},{64,96... | collective-permute-start | bytes 393224 | tf_op jit(solution)/shard_map/ppermute | solution.py:34
  30.6 1.5 %collective-permute-start.8 = (bf16[256,256]{1,0:T(8,128)(2,1)}, bf16[256,256]{1,0:T(8,128)(2,1)}, u32[]{:S(2)}, u32[]{:S(2)}) collective-permute-start(bf16[256,256]{1,0:T(8,128)(2,1)} %get-tuple-element.51), channel_id=1, source_target_pairs={{0,16},{8,24},{16,0},{24,8},{32,48},{40,56},{48,32},{56,40},{64,80... | collective-permute-start | bytes 393224 | tf_op jit(solution)/shard_map/ppermute | solution.py:34
  32.0 3.0 %collective-permute-start.9 = (bf16[256,256]{1,0:T(8,128)(2,1)}, bf16[256,256]{1,0:T(8,128)(2,1)}, u32[]{:S(2)}, u32[]{:S(2)}) collective-permute-start(bf16[256,256]{1,0:T(8,128)(2,1)} %get-tuple-element.52), channel_id=1, source_target_pairs={{0,128},{8,136},{16,144},{24,152},{32,160},{40,168},{48,176},{56,1... | collective-permute-start | bytes 393224 | tf_op jit(solution)/shard_map/ppermute | solution.py:34
  35.1 1.0 %collective-permute-start.10 = (bf16[256,256]{1,0:T(8,128)(2,1)S(1)}, bf16[256,256]{1,0:T(8,128)(2,1)}, u32[]{:S(2)}, u32[]{:S(2)}) collective-permute-start(bf16[256,256]{1,0:T(8,128)(2,1)S(1)} %get-tuple-element.53), channel_id=1, source_target_pairs={{0,8},{8,0},{16,24},{24,16},{32,40},{40,32},{48,56},{56,48},{64,72... | collective-permute-start | bytes 393224 | tf_op jit(solution)/shard_map/ppermute | solution.py:34
  36.1 0.6 collective-permute-start.11
  36.7 0.0 all-to-all-done
  36.7 6.7 %attend_inner.1 = (bf16[2048,128]{1,0:T(8,128)(2,1)}, bf16[2048,128]{1,0:T(8,128)(2,1)}, f32[2048,256]{1,0:T(8,128)S(1)}, bf16[2048,256]{1,0:T(8,128)(2,1)S(1)}, bf16[2048,128]{1,0:T(8,128)(2,1)S(1)}) custom-call(s32[9,1024]{1,0:T(8,128)} %bitcast.23, s32[1024]{0:T(1024)} %far_counts_ref.3, bf16[2048,128]{1,0:T(8,128)(2,1)S(1)} %bitcast.17, ...), custom_call_target="tpu_custom_call" | custom-call | flops 4000000000 | bytes 8388608 | tf_op jit(solution)/shard_map/attend_inner/pallas_call | solution.py:280
  43.4 0.0 collective-permute-done.7.refs_0_
  43.4 0.3 collective-permute-done.8.refs_1_
  43.7 0.0 collective-permute-done.9.refs_2_
  43.7 0.1 collective-permute-done.10.refs_3_
  43.9 0.0 collective-permute-done.11.refs_4_
  43.9 9.7 %attend_outer.1 = (bf16[2048,128]{1,0:T(8,128)(2,1)}, bf16[2048,128]{1,0:T(8,128)(2,1)}, f32[2048,256]{1,0:T(8,128)S(1)}, bf16[256,256]{1,0:T(8,128)(2,1)}, bf16...) custom-call(s32[5,4,32]{2,1,0:T(4,128)} %bitcast.21, ...), custom_call_target="tpu_custom_call", output_to_operand_aliasing={{0}: (11, {}), {1}: (12, {}), {2}: (13, {})} | custom-call | flops 4000000000 | bytes 4194304 | tf_op jit(solution)/shard_map/attend_outer/pallas_call | solution.py:337
  53.5 4.8 %all-to-all-start.1 = ((bf16[8,256,128]{2,1,0:T(8,128)(2,1)}), bf16[8,256,128]{2,1,0:T(8,128)(2,1)}, u32[]{:S(2)}, u32[]{:S(2)}) async-start(bf16[8,256,128]{2,1,0:T(8,128)(2,1)} %bitcast.19), calls=%async_computation.1 | async-start | bytes 1048576 | tf_op jit(solution)/shard_map/all_to_all | solution.py:402
  58.4 3.1 %collective-permute-start.12 = (bf16[256,256]{1,0:T(8,128)(2,1)}, bf16[256,256]{1,0:T(8,128)(2,1)S(1)}, u32[]{:S(2)}, u32[]{:S(2)}) collective-permute-start(bf16[256,256]{1,0:T(8,128)(2,1)} %get-tuple-element.59), channel_id=1, source_target_pairs={{0,32},{8,40},{16,48},{24,56},{32,0},{40,8},{48,16},{56,24},{64,96... | collective-permute-start | bytes 393224 | tf_op jit(solution)/shard_map/ppermute | solution.py:34
  61.5 1.5 %collective-permute-start.13 = (bf16[256,256]{1,0:T(8,128)(2,1)}, bf16[256,256]{1,0:T(8,128)(2,1)S(1)}, u32[]{:S(2)}, u32[]{:S(2)}) collective-permute-start(bf16[256,256]{1,0:T(8,128)(2,1)} %get-tuple-element.64), channel_id=1, source_target_pairs={{0,16},{8,24},{16,0},{24,8},{32,48},{40,56},{48,32},{56,40},{64,80... | collective-permute-start | bytes 393224 | tf_op jit(solution)/shard_map/ppermute | solution.py:34
  62.9 3.0 %collective-permute-start.14 = (bf16[256,256]{1,0:T(8,128)(2,1)}, bf16[256,256]{1,0:T(8,128)(2,1)S(1)}, u32[]{:S(2)}, u32[]{:S(2)}) collective-permute-start(bf16[256,256]{1,0:T(8,128)(2,1)} %get-tuple-element.65), channel_id=1, source_target_pairs={{0,128},{8,136},{16,144},{24,152},{32,160},{40,168},{48,176},{56,1... | collective-permute-start | bytes 393224 | tf_op jit(solution)/shard_map/ppermute | solution.py:34
  66.0 1.0 %collective-permute-start.15 = (bf16[256,256]{1,0:T(8,128)(2,1)}, bf16[256,256]{1,0:T(8,128)(2,1)S(1)}, u32[]{:S(2)}, u32[]{:S(2)}) collective-permute-start(bf16[256,256]{1,0:T(8,128)(2,1)} %get-tuple-element.66), channel_id=1, source_target_pairs={{0,8},{8,0},{16,24},{24,16},{32,40},{40,32},{48,56},{56,48},{64,72... | collective-permute-start | bytes 393224 | tf_op jit(solution)/shard_map/ppermute | solution.py:34
  67.0 0.6 collective-permute-start.16
  67.6 0.0 all-to-all-done.1
  67.6 1.9 %copy_bitcast_fusion = bf16[256,1024]{1,0:T(8,128)(2,1)} fusion(bf16[8,256,128]{2,1,0:T(8,128)(2,1)} %all-to-all-done.1), kind=kLoop, calls=%fused_computation | loop fusion | bytes 1048576 | tf_op jit(solution)/shard_map/reshape | solution.py:403
  69.5 1.9 %collective-permute-done.12.refs_0_ = bf16[256,256]{1,0:T(8,128)(2,1)S(1)} collective-permute-done((bf16[256,256]{1,0:T(8,128)(2,1)}, bf16[256,256]{1,0:T(8,128)(2,1)S(1)}, u32[]{:S(2)}, u32[]{:S(2)}) %collective-permute-start.12) | collective-permute-done | bytes 131104 | tf_op jit(solution)/shard_map/ppermute | solution.py:34
  71.4 4.2 %collective-permute-done.13.refs_1_ = bf16[256,256]{1,0:T(8,128)(2,1)S(1)} collective-permute-done((bf16[256,256]{1,0:T(8,128)(2,1)}, bf16[256,256]{1,0:T(8,128)(2,1)S(1)}, u32[]{:S(2)}, u32[]{:S(2)}) %collective-permute-start.13) | collective-permute-done | bytes 131104 | tf_op jit(solution)/shard_map/ppermute | solution.py:34
  75.6 0.0 collective-permute-done.14.refs_2_
  75.6 0.0 collective-permute-done.15.refs_3_
  75.6 0.0 collective-permute-done.16.refs_4_
  75.6 2.0 %join_gradients.1 = (bf16[2048,128]{1,0:T(8,128)(2,1)}, bf16[2048,128]{1,0:T(8,128)(2,1)}) custom-call(s32[5,4,32]{2,1,0:T(4,128)} %bitcast.22, f32[2048,256]{1,0:T(8,128)S(1)} %get-tuple-element.62.acc_ref, bf16[256,256]{1,0:T(8,128)(2,1)S(1)} %collective-permute-done.12.refs_0_, bf16[256,256]{1,0:T(8,128)(2,1)S(1)} %collective-permute-done.13.refs_1_, ...), custom_call_target="tpu_custom_call" | custom-call | flops 1000000 | bytes 4194304 | tf_op jit(solution)/shard_map/join_gradients/pallas_call | solution.py:375
Async XLA Ops:
  0.6 10.0 %copy-start = (bf16[256,1024]{1,0:T(8,128)(2,1)S(1)}, bf16[256,1024]{1,0:T(8,128)(2,1)}, u32[]{:S(2)}) copy-start(bf16[256,1024]{1,0:T(8,128)(2,1)} %param.7) | copy-start | bytes 1572868
  2.1 6.1 %collective-permute-start = (bf16[256,256]{1,0:T(8,128)(2,1)S(1)}, bf16[256,256]{1,0:T(8,128)(2,1)S(1)}, u32[]{:S(2)}, u32[]{:S(2)}) collective-permute-start(bf16[256,256]{1,0:T(8,128)(2,1)S(1)} %get-tuple-element.37), channel_id=1, source_target_pairs={{0,2},{1,3},{2,4},{3,5},{4,6},{5,7},{6,0},{7,1},{8,10},{9,11},{10,... | collective-permute-start | bytes 393224 | tf_op jit(solution)/shard_map/ppermute | solution.py:48
  3.8 6.8 %collective-permute-start.1 = (bf16[256,256]{1,0:T(8,128)(2,1)S(1)}, bf16[256,256]{1,0:T(8,128)(2,1)S(1)}, u32[]{:S(2)}, u32[]{:S(2)}) collective-permute-start(bf16[256,256]{1,0:T(8,128)(2,1)S(1)} %get-tuple-element.38), channel_id=1, source_target_pairs={{0,6},{1,7},{2,0},{3,1},{4,2},{5,3},{6,4},{7,5},{8,14},{9,15},{10,... | collective-permute-start | bytes 393224 | tf_op jit(solution)/shard_map/ppermute | solution.py:48
  4.5 7.0 %collective-permute-start.2 = (bf16[256,256]{1,0:T(8,128)(2,1)S(1)}, bf16[256,256]{1,0:T(8,128)(2,1)S(1)}, u32[]{:S(2)}, u32[]{:S(2)}) collective-permute-start(bf16[256,256]{1,0:T(8,128)(2,1)S(1)} %get-tuple-element.39), channel_id=1, source_target_pairs={{0,3},{1,2},{2,5},{3,4},{4,7},{5,6},{6,1},{7,0},{8,11},{9,10},{10,... | collective-permute-start | bytes 393224 | tf_op jit(solution)/shard_map/ppermute | solution.py:48
  4.7 6.8 %collective-permute-start.3 = (bf16[256,256]{1,0:T(8,128)(2,1)S(1)}, bf16[256,256]{1,0:T(8,128)(2,1)S(1)}, u32[]{:S(2)}, u32[]{:S(2)}) collective-permute-start(bf16[256,256]{1,0:T(8,128)(2,1)S(1)} %get-tuple-element.40), channel_id=1, source_target_pairs={{0,7},{1,6},{2,1},{3,0},{4,3},{5,2},{6,5},{7,4},{8,15},{9,14},{10,... | collective-permute-start | bytes 393224 | tf_op jit(solution)/shard_map/ppermute | solution.py:48
  6.2 8.4 %collective-permute-start.4 = (bf16[256,256]{1,0:T(8,128)(2,1)S(1)}, bf16[256,256]{1,0:T(8,128)(2,1)S(1)}, u32[]{:S(2)}, u32[]{:S(2)}) collective-permute-start(bf16[256,256]{1,0:T(8,128)(2,1)S(1)} %get-tuple-element.41), channel_id=1, source_target_pairs={{0,4},{1,5},{2,6},{3,7},{4,0},{5,1},{6,2},{7,3},{8,12},{9,13},{10,... | collective-permute-start | bytes 393224 | tf_op jit(solution)/shard_map/ppermute | solution.py:48
  8.3 10.0 %collective-permute-start.5 = (bf16[256,256]{1,0:T(8,128)(2,1)S(1)}, bf16[256,256]{1,0:T(8,128)(2,1)S(1)}, u32[]{:S(2)}, u32[]{:S(2)}) collective-permute-start(bf16[256,256]{1,0:T(8,128)(2,1)S(1)} %get-tuple-element.42), channel_id=1, source_target_pairs={{0,5},{1,4},{2,7},{3,6},{4,1},{5,0},{6,3},{7,2},{8,13},{9,12},{10,... | collective-permute-start | bytes 393224 | tf_op jit(solution)/shard_map/ppermute | solution.py:48
  10.6 7.6 %collective-permute-start.6 = (bf16[256,256]{1,0:T(8,128)(2,1)S(1)}, bf16[256,256]{1,0:T(8,128)(2,1)S(1)}, u32[]{:S(2)}, u32[]{:S(2)}) collective-permute-start(bf16[256,256]{1,0:T(8,128)(2,1)S(1)} %get-tuple-element.43), channel_id=1, source_target_pairs={{0,1},{1,0},{2,3},{3,2},{4,5},{5,4},{6,7},{7,6},{8,9},{9,8},{10,11... | collective-permute-start | bytes 393224 | tf_op jit(solution)/shard_map/ppermute | solution.py:48
  20.1 16.6 %all-to-all-start = ((bf16[8,256,128]{2,1,0:T(8,128)(2,1)}), bf16[8,256,128]{2,1,0:T(8,128)(2,1)S(1)}, u32[]{:S(2)}, u32[]{:S(2)}) async-start(bf16[8,256,128]{2,1,0:T(8,128)(2,1)} %bitcast_bitcast_fusion), calls=%async_computation | async-start | bytes 1048576 | tf_op jit(solution)/shard_map/all_to_all | solution.py:397
  24.8 18.6 %collective-permute-start.7 = (bf16[256,256]{1,0:T(8,128)(2,1)}, bf16[256,256]{1,0:T(8,128)(2,1)S(1)}, u32[]{:S(2)}, u32[]{:S(2)}) collective-permute-start(bf16[256,256]{1,0:T(8,128)(2,1)} %get-tuple-element.50), channel_id=1, source_target_pairs={{0,32},{8,40},{16,48},{24,56},{32,0},{40,8},{48,16},{56,24},{64,96... | collective-permute-start | bytes 393224 | tf_op jit(solution)/shard_map/ppermute | solution.py:34
  30.6 13.2 %collective-permute-start.8 = (bf16[256,256]{1,0:T(8,128)(2,1)}, bf16[256,256]{1,0:T(8,128)(2,1)}, u32[]{:S(2)}, u32[]{:S(2)}) collective-permute-start(bf16[256,256]{1,0:T(8,128)(2,1)} %get-tuple-element.51), channel_id=1, source_target_pairs={{0,16},{8,24},{16,0},{24,8},{32,48},{40,56},{48,32},{56,40},{64,80... | collective-permute-start | bytes 393224 | tf_op jit(solution)/shard_map/ppermute | solution.py:34
  32.0 11.7 %collective-permute-start.9 = (bf16[256,256]{1,0:T(8,128)(2,1)}, bf16[256,256]{1,0:T(8,128)(2,1)}, u32[]{:S(2)}, u32[]{:S(2)}) collective-permute-start(bf16[256,256]{1,0:T(8,128)(2,1)} %get-tuple-element.52), channel_id=1, source_target_pairs={{0,128},{8,136},{16,144},{24,152},{32,160},{40,168},{48,176},{56,1... | collective-permute-start | bytes 393224 | tf_op jit(solution)/shard_map/ppermute | solution.py:34
  35.1 8.8 %collective-permute-start.10 = (bf16[256,256]{1,0:T(8,128)(2,1)S(1)}, bf16[256,256]{1,0:T(8,128)(2,1)}, u32[]{:S(2)}, u32[]{:S(2)}) collective-permute-start(bf16[256,256]{1,0:T(8,128)(2,1)S(1)} %get-tuple-element.53), channel_id=1, source_target_pairs={{0,8},{8,0},{16,24},{24,16},{32,40},{40,32},{48,56},{56,48},{64,72... | collective-permute-start | bytes 393224 | tf_op jit(solution)/shard_map/ppermute | solution.py:34
  36.1 7.8 %collective-permute-start.11 = (bf16[256,256]{1,0:T(8,128)(2,1)S(1)}, bf16[256,256]{1,0:T(8,128)(2,1)}, u32[]{:S(2)}, u32[]{:S(2)}) collective-permute-start(bf16[256,256]{1,0:T(8,128)(2,1)S(1)} %get-tuple-element.54), channel_id=1, source_target_pairs={{0,64},{8,72},{16,80},{24,88},{32,96},{40,104},{48,112},{56,120},{... | collective-permute-start | bytes 393224 | tf_op jit(solution)/shard_map/ppermute | solution.py:34
  53.5 14.0 %all-to-all-start.1 = ((bf16[8,256,128]{2,1,0:T(8,128)(2,1)}), bf16[8,256,128]{2,1,0:T(8,128)(2,1)}, u32[]{:S(2)}, u32[]{:S(2)}) async-start(bf16[8,256,128]{2,1,0:T(8,128)(2,1)} %bitcast.19), calls=%async_computation.1 | async-start | bytes 1048576 | tf_op jit(solution)/shard_map/all_to_all | solution.py:402
  58.4 13.0 %collective-permute-start.12 = (bf16[256,256]{1,0:T(8,128)(2,1)}, bf16[256,256]{1,0:T(8,128)(2,1)S(1)}, u32[]{:S(2)}, u32[]{:S(2)}) collective-permute-start(bf16[256,256]{1,0:T(8,128)(2,1)} %get-tuple-element.59), channel_id=1, source_target_pairs={{0,32},{8,40},{16,48},{24,56},{32,0},{40,8},{48,16},{56,24},{64,96... | collective-permute-start | bytes 393224 | tf_op jit(solution)/shard_map/ppermute | solution.py:34
  61.5 14.1 %collective-permute-start.13 = (bf16[256,256]{1,0:T(8,128)(2,1)}, bf16[256,256]{1,0:T(8,128)(2,1)S(1)}, u32[]{:S(2)}, u32[]{:S(2)}) collective-permute-start(bf16[256,256]{1,0:T(8,128)(2,1)} %get-tuple-element.64), channel_id=1, source_target_pairs={{0,16},{8,24},{16,0},{24,8},{32,48},{40,56},{48,32},{56,40},{64,80... | collective-permute-start | bytes 393224 | tf_op jit(solution)/shard_map/ppermute | solution.py:34
  62.9 12.7 %collective-permute-start.14 = (bf16[256,256]{1,0:T(8,128)(2,1)}, bf16[256,256]{1,0:T(8,128)(2,1)S(1)}, u32[]{:S(2)}, u32[]{:S(2)}) collective-permute-start(bf16[256,256]{1,0:T(8,128)(2,1)} %get-tuple-element.65), channel_id=1, source_target_pairs={{0,128},{8,136},{16,144},{24,152},{32,160},{40,168},{48,176},{56,1... | collective-permute-start | bytes 393224 | tf_op jit(solution)/shard_map/ppermute | solution.py:34
  66.0 9.6 %collective-permute-start.15 = (bf16[256,256]{1,0:T(8,128)(2,1)}, bf16[256,256]{1,0:T(8,128)(2,1)S(1)}, u32[]{:S(2)}, u32[]{:S(2)}) collective-permute-start(bf16[256,256]{1,0:T(8,128)(2,1)} %get-tuple-element.66), channel_id=1, source_target_pairs={{0,8},{8,0},{16,24},{24,16},{32,40},{40,32},{48,56},{56,48},{64,72... | collective-permute-start | bytes 393224 | tf_op jit(solution)/shard_map/ppermute | solution.py:34
  67.0 8.6 %collective-permute-start.16 = (bf16[256,256]{1,0:T(8,128)(2,1)}, bf16[256,256]{1,0:T(8,128)(2,1)S(1)}, u32[]{:S(2)}, u32[]{:S(2)}) collective-permute-start(bf16[256,256]{1,0:T(8,128)(2,1)} %get-tuple-element.67), channel_id=1, source_target_pairs={{0,64},{8,72},{16,80},{24,88},{32,96},{40,104},{48,112},{56,120},{... | collective-permute-start | bytes 393224 | tf_op jit(solution)/shard_map/ppermute | solution.py:34
